TPU v7x, 32 devices: a whole 2x2x4 slice. The times are simulated.
32 devices in a mesh: term: 4 (over z), row: 4 (over y, x), col: 2 (over core).
Axes of the slice: x: 2, y: 2, z: 4, core: 2. Of those that a mesh axis runs over, the one named last changes fastest.
Arguments:
- panel_column: float32 [4, 49152, 128], P('term', 'row'), may hold values from -3 to 8, as said below
- trailing: float32 [4, 49152, 256], P('term', 'row', 'col'), may hold values from -6 to 6
- right_side: float32 [49152, 512], P('row', 'col'), may hold values from -6 to 6
- term_weights: float32 [4], P('term'), may hold values from 0.5 to 1.5
Outputs:
- factor_column: float32 [4, 49152, 128], P('term', 'row')
- updated: float32 [4, 49152, 256], P('term', 'row', 'col')
- combined: float32 [49152, 512], P('row', 'col')
Inputs may be any that keep to these rules, and one draw needn't show every extreme that they name: For each term, rows 0 to 127 of panel_column form a symmetric positive definite block.
All inputs are finite; a program needn't handle non-finite values.
Results may differ from a plain program's by a relative error of at most 0.0001.
Values sent between devices are 32-bit elements; how exact they have to be, the bound alone decides.
No kernel may reach another device: no remote copies, remote signals or barrier semaphores. Data moves between devices by JAX's collectives and lax.ppermute only.
A program may use at most 128 MiB of HBM per device.

v0:
```python
import jax
import jax.numpy as jnp
from jax import lax
from jax.sharding import PartitionSpec as P

B = 128


HIGH = lax.Precision.HIGHEST


def from_root(x, axis, root):
    mine = lax.axis_index(axis) == root
    return lax.psum(jnp.where(mine, x, jnp.zeros_like(x)), axis)


def contract_rows(left, right):
    return lax.dot_general(
        left, right, (((1,), (1,)), ((), ())), precision=HIGH, preferred_element_type=jnp.float32
    )


def body(panel_column, trailing, right_side, term_weights):
    column = panel_column[0]
    window_dev = trailing.shape[2]
    per_row = window_dev * lax.axis_size("col") // lax.axis_size("row")
    leading = lax.axis_index("row") == 0
    corner, right_top = (from_root(column[:B], "row", 0), from_root(right_side[:B], "row", 0))
    lower_block = jnp.linalg.cholesky(corner)
    solved_rows = lax.linalg.triangular_solve(
        lower_block, column, left_side=False, lower=True, transpose_a=True
    )
    factor = jnp.concatenate(
        [jnp.where(leading, lower_block, solved_rows[:B]), solved_rows[B:]], axis=0
    )
    gathered = lax.all_gather(factor[B : B + per_row], "row", axis=0, tiled=True)
    picked = lax.dynamic_slice_in_dim(gathered, lax.axis_index("col") * window_dev, window_dev, 0)
    updated = trailing[0] - contract_rows(factor, picked)
    top_solved = lax.linalg.triangular_solve(lower_block, right_top, left_side=True, lower=True)
    reduced = right_side - jnp.dot(
        factor, top_solved, precision=HIGH, preferred_element_type=jnp.float32
    )
    solved = jnp.concatenate([jnp.where(leading, top_solved, reduced[:B]), reduced[B:]], axis=0)
    combined = lax.psum(term_weights[0] * solved, "term")
    return (factor[None], updated[None], combined)


def solution(mesh):
    placed = (P("term", "row", None), P("term", "row", "col"), P("row", "col"), P("term"))
    return jax.shard_map(
        body,
        mesh=mesh,
        in_specs=placed,
        out_specs=(P("term", "row", None), P("term", "row", "col"), P("row", "col")),
        check_vma=False,
    )
```

profile of v0, /device:TPU:0, one launch (start us, length us, event | category | flops | bytes accessed | tf_op | source)
XLA Modules:
  0.0 556.4 jit_solution(12605251428152548124)
XLA Ops:
  7.2 0.0 all-reduce.6.cloned.1.call-start
  7.2 0.8 slice.37
  8.1 0.1 copy.11
  8.2 0.6 select_bitcast_fusion.1
  8.8 1.6 slice_select_fusion.1
  10.4 0.0 all-reduce.6.cloned.1.call-update
  10.4 0.0 all-reduce.4.cloned.1.call-start
  11.1 45.7 %all-reduce.6.cloned.1.call-done = (f32[128,128]{0,1:T(8,128)}, f32[128,256]{1,0:T(8,128)}) async-done(((f32[128,128]{0,1:T(8,128)}, f32[128,256]{1,0:T(8,128)}), (f32[128,128]{0,1:T(8,128)}, f32[128,256]{1,0:T(8,128)})) %all-reduce.6.cloned.1.call-update) | async-done | bytes 196624 | tf_op jit(solution)/shard_map/psum | solution.py:14
  56.8 0.9 copy.8
  57.7 0.9 fusion.6
  58.6 11.7 %cholesky.17 = f32[128,128]{1,0:T(8,128)S(1)} custom-call(f32[128,128]{1,0:T(8,128)S(1)} %fusion.6), custom_call_target="Cholesky" | custom-call | tf_op jit(solution)/shard_map/jit(cholesky)/cholesky | solution.py:29
  70.3 0.6 compare_reduce_fusion
  71.0 0.7 select_bitcast_fusion
  71.7 9.8 %custom-call.8 = f32[1,128,128]{1,2,0:T(8,128)S(1)} custom-call(f32[1,128,128]{2,1,0:T(8,128)S(1)} %select_bitcast_fusion), custom_call_target="InvertDiagBlocksLowerTriangular" | custom-call | tf_op jit(solution)/shard_map/triangular_solve | solution.py:30
  81.5 7.8 %convolution_bitcast_fusion = f32[12288,128]{1,0:T(8,128)S(1)} fusion(f32[1,12288,128]{2,1,0:T(8,128)} %param.4, f32[1,128,128]{1,2,0:T(8,128)S(1)} %custom-call.8), kind=kOutput, calls=%fused_computation.3 | convolution fusion | flops 2415919104 | bytes 12648448 | tf_op jit(solution)/shard_map/triangular_solve | solution.py:30
  89.3 0.0 copy-start.1
  89.3 0.0 copy-start.2
  89.3 0.8 slice_select_fusion.2
  90.1 0.5 slice.45
  90.6 1.4 copy-done.1
  92.0 0.0 copy-start
  92.0 0.0 copy-done.2
  92.0 0.3 fusion.3
  92.3 15.0 %convolution_subtract_fusion = f32[12288,256]{1,0:T(8,128)S(1)} fusion(f32[12288,256]{1,0:T(8,128)} %param.6, f32[128,256]{1,0:T(8,128)S(1)} %fusion.3, f32[12160,128]{1,0:T(8,128)S(1)} %slice.45, f32[128,128]{1,0:T(8,128)S(1)} %slice_select_fusion.2), kind=kOutput, calls=%fused_computation | convolution fusion | flops 4836556800 | bytes 31588352 | tf_op jit(solution)/shard_map/dot_general | solution.py:40
  107.3 0.0 copy-done
  107.4 0.9 slice.48
  108.2 5.0 maximum_multiply_fusion
  113.2 0.0 slice-start.2
  113.2 0.0 slice-start
  113.2 0.0 all-reduce.4.cloned.1.call-update
  113.3 0.7 slice-done.2
  114.0 8.6 %all_gather.3 = f32[256,128]{1,0:T(8,128)S(1)} all-gather(f32[64,128]{1,0:T(8,128)S(1)} %slice-done.2), channel_id=1, replica_groups=mesh['term'=4,'row'=4,'col'=2] {'row'}, dimensions={0}, use_global_device_ids=true | all-gather | bytes 163840 | tf_op jit(solution)/shard_map/all_gather | solution.py:36
  122.6 0.0 slice-start.1
  122.6 9.9 %fusion = f32[1,12288,128]{2,1,0:T(8,128)} fusion(f32[1,12288,128]{2,1,0:T(8,128)} %param.5, f32[12160,128]{1,0:T(8,128)} %copy-done, f32[128,128]{1,0:T(8,128)S(1)} %slice_select_fusion.2, f32[256,128]{1,0:T(8,128)S(1)} %all_gather.3, s32[]{:T(128)S(6)} %select_n.42), kind=kOutput, calls=%fused_computation.2 | convolution fusion | flops 2419064832 | bytes 18939908 | tf_op jit(solution)/shard_map/dot_general | solution.py:18
  132.5 0.0 slice-done
  132.5 0.0 slice-done.1
  132.5 2.9 fusion.2
  135.4 404.1 %all-reduce.4.cloned.1.call-done = f32[12288,256]{1,0:T(8,128)} async-done(((f32[12288,256]{1,0:T(8,128)}), f32[12288,256]{1,0:T(8,128)}) %all-reduce.4.cloned.1.call-update) | async-done | bytes 12582928 | tf_op jit(solution)/shard_map/psum | solution.py:44
  539.5 10.1 %copy.16 = f32[12288,256]{1,0:T(8,128)} copy(f32[12288,256]{1,0:T(8,128)} %all-reduce.4.cloned.1.call-done) | data formatting | bytes 25165824
  (3 shorter events, 0.1 us)
Async XLA Ops:
  7.2 49.6 %all-reduce.6.cloned.1.call-start = ((), (), s32[]{:S(2)}) async-start(), calls=%async_computation.1 | async-start | bytes 393216 | tf_op jit(solution)/shard_map/psum | solution.py:14
  10.4 529.1 %all-reduce.4.cloned.1.call-start = ((), (), s32[]{:S(2)}) async-start(), calls=%async_computation | async-start | bytes 25165824 | tf_op jit(solution)/shard_map/psum | solution.py:44
  89.3 2.7 copy-start.1
  89.3 2.7 copy-start.2
  92.0 15.3 %copy-start = (f32[12160,128]{1,0:T(8,128)}, f32[12160,128]{1,0:T(8,128)S(1)}, u32[]{:S(2)}) copy-start(f32[12160,128]{1,0:T(8,128)S(1)} %slice.45) | copy-start | bytes 18677764
  113.2 0.8 slice-start.2
  113.2 19.2 %slice-start = ((s8[6225920]{0:T(1024)(128)(4,1)}), s8[2031616]{0:T(1024)(128)(4,1)S(1)}, s32[]{:S(2)}) async-start(s8[6225920]{0:T(1024)(128)(4,1)} %bitcast.28), calls=%async_computation.2 | async-start | bytes 4063232
  122.6 9.9 %slice-start.1 = ((s8[6225920]{0:T(1024)(128)(4,1)}), s8[4194304]{0:T(1024)(128)(4,1)S(1)}, s32[]{:S(2)}) async-start(s8[6225920]{0:T(1024)(128)(4,1)} %bitcast.28), calls=%async_computation.3 | async-start | bytes 8388608
Sparse Core Ops, SparseCore 0:
  11.5 45.2 all-reduce.5
  113.4 426.0 all-reduce.3
where the time goes:
time: 557 us; the launch traced here: 556 us
  waiting for transfers between devices  450 us (81%)
  other arithmetic  34.6 us (6%)
  matrix products  33 us (6%)
  local copies, waits for them, and re-layouts  15.4 us (3%)
  between operations  14.8 us (3%)
  blocking collectives  8.56 us (2%)
    psum x1, waiting for transfers between devices, body(): combined = lax.psum(term_weights[0] * solved, 'term')  404 us
    psum x1, waiting for transfers between devices, from_root(): return lax.psum(jnp.where(mine, x, jnp.zeros_like(x)), axis)  45.7 us
    dot_general x1, matrix products, body(): jnp.dot(factor, top_solved, precision=HIGH, preferred_element_type=jnp.fl...  15 us
    another operation x3, other arithmetic, body(): lower_block = jnp.linalg.cholesky(corner)  12.4 us
    unnamed x12, local copies, waits for them, and re-layouts  11.6 us
  transfers between devices with their start and end apart: 2, of which 2 were waited for; matrix products, arithmetic and copies ran while one was open for 2% of the time, Pallas kernels for 0%

commit v1 on v0

v1 whole, which is shorter than its diff:
```python
import functools
import math

import jax
import jax.numpy as jnp
from jax import lax
from jax.experimental import pallas as pl
from jax.experimental.pallas import tpu as pltpu
from jax.sharding import PartitionSpec as P

HIGH = lax.Precision.HIGHEST
F32 = jnp.float32
LANES = 128
PAD = 8
VMEM_LIMIT = 40 * 1024 * 1024


def dot(left, right):
    return jnp.dot(left, right, precision=HIGH, preferred_element_type=F32)


def chunk_sizes(part, width):
    unit = part // 12
    if part % 12 == 0 and unit >= width:
        return [unit, 4 * unit, 4 * unit, 2 * unit, unit]
    return [width] * (part // width)


def block_rows(*extents):
    return math.gcd(512, *extents)


def hops(mine, t, n):
    slots = []
    right = left = mine
    merged = False
    for h in range(1, n):
        to_right = [(j, j + 1) for j in range(h - 1, n - 1)]
        to_left = [(j, j - 1) for j in range(1, n - h + 1)]
        source = jnp.where(t >= h, n - h, h)
        valid = (t >= h) | (t < n - h)
        if merged:
            right = left = lax.ppermute(right, "term", to_right + to_left)
            slots.append((right, source, valid))
            continue
        right = lax.ppermute(right, "term", to_right)
        left = lax.ppermute(left, "term", to_left)
        if 2 * h > n - 1:
            right = left = jnp.where(t >= h, right, left)
            merged = True
            slots.append((right, source, valid))
        else:
            slots.append((right, jnp.int32(n - h), t >= h))
            slots.append((left, jnp.int32(h), t < n - h))
    return slots


def factor_kernel(width, flag, panel, trailing, inverse_t, picked_t, lower, factor, updated):
    solved = dot(panel[...], inverse_t[...])
    factor[...] = solved

    @pl.when((pl.program_id(0) == 0) & (flag[0] == 1))
    def _():
        factor[:width] = lower[...]

    updated[...] = trailing[...] - dot(factor[...], picked_t[...])


def factor_call(leading, panel, trailing, inverse_t, picked_t, lower):
    rows, width = panel.shape
    window = trailing.shape[1]
    block = block_rows(rows) * (2 if rows % 1024 == 0 else 1)
    whole = lambda a: pl.BlockSpec(a.shape, lambda i, f: (0, 0))
    tile = lambda n: pl.BlockSpec((block, n), lambda i, f: (i, 0))
    return pl.pallas_call(
        functools.partial(factor_kernel, width),
        grid_spec=pltpu.PrefetchScalarGridSpec(
            num_scalar_prefetch=1,
            grid=(rows // block,),
            in_specs=[tile(width), tile(window), whole(inverse_t), whole(picked_t), whole(lower)],
            out_specs=[tile(width), tile(window)],
        ),
        out_shape=[
            jax.ShapeDtypeStruct((rows, width), F32),
            jax.ShapeDtypeStruct((rows, window), F32),
        ],
        compiler_params=pltpu.CompilerParams(vmem_limit_bytes=VMEM_LIMIT),
        cost_estimate=pl.CostEstimate(
            flops=2 * rows * width * (width + window) * 6,
            bytes_accessed=8 * rows * (width + window),
            transcendentals=0,
        ),
        name="factor_update",
    )(leading, panel, trailing, inverse_t, picked_t, lower)


def early_kernel(n_bufs, sides, *refs):
    bufs, weights, outs = refs[:n_bufs], refs[n_bufs], refs[n_bufs + 1 :]
    stacked = jnp.concatenate([b[...] for b in bufs], axis=1)
    total = dot(stacked, weights[...])
    for k, out in enumerate(outs):
        out[...] = total[:, k * sides : (k + 1) * sides]


def early_call(size, bufs, weights, n_col):
    width = bufs[0].shape[1]
    sides = weights.shape[1] // n_col
    block = block_rows(size)
    return pl.pallas_call(
        functools.partial(early_kernel, len(bufs), sides),
        grid=(size // block,),
        in_specs=[pl.BlockSpec((block, width), lambda i: (i, 0))] * len(bufs)
        + [pl.BlockSpec(weights.shape, lambda i: (0, 0))],
        out_specs=[pl.BlockSpec((block, sides), lambda i: (i, 0))] * n_col,
        out_shape=[jax.ShapeDtypeStruct((size, sides), F32)] * n_col,
        compiler_params=pltpu.CompilerParams(vmem_limit_bytes=VMEM_LIMIT),
        cost_estimate=pl.CostEstimate(
            flops=2 * size * weights.shape[0] * weights.shape[1] * 6,
            bytes_accessed=4 * size * (width * len(bufs) + weights.shape[1]),
            transcendentals=0,
        ),
        name="early_terms",
    )(*bufs, weights)


def late_kernel(n_col, n_late, first, width, scalars, total_weight, rhs, top, weights, *refs):
    early, late = refs[:n_col], refs[n_col : n_col * (1 + n_late)]
    out = refs[-1]
    phase = pl.program_id(0)
    for k in range(n_col):

        @pl.when(phase == k)
        def _(k=k):
            out[...] = total_weight[0] * rhs[...] - early[k][...]
            for i in range(n_late):
                out[...] -= dot(
                    late[i * n_col + k][...], weights[i * width : (i + 1) * width]
                )

    if first:
        part = lax.rem(scalars[0] - phase + n_col, n_col)

        @pl.when((part == 0) & (scalars[1] == 1) & (pl.program_id(1) == 0))
        def _():
            out[:width] = top[...]


def late_call(scalars, total_weight, rhs, top, weights, early, late, start, size, part, combined):
    n_col, n_late = len(early), len(late)
    sides = rhs.shape[1]
    width = weights.shape[0] // n_late
    block = block_rows(size, start, part)
    steps = size // block
    at = lambda k, j, s: (
        (lax.rem(s[0] - k + n_col, n_col) * (part // block) + start // block + j),
        0,
    )

    def held(phase):
        return lambda k, j, s: (
            jnp.where(k == phase, j, jnp.where(k < phase, 0, steps - 1)),
            0,
        )

    rhs_spec = pl.BlockSpec((block, sides), at)
    in_specs = [
        pl.BlockSpec(memory_space=pltpu.SMEM),
        rhs_spec,
        pl.BlockSpec(top.shape, lambda k, j, s: (0, 0)),
        pl.BlockSpec(weights.shape, lambda k, j, s: (0, 0)),
    ]
    in_specs += [pl.BlockSpec((block, sides), held(k)) for k in range(n_col)]
    in_specs += [pl.BlockSpec((block, width), held(k)) for _ in late for k in range(n_col)]
    operands = [total_weight, rhs, top, weights, *early, *[b for bufs in late for b in bufs]]
    aliases = {}
    if combined is not None:
        in_specs.append(pl.BlockSpec(memory_space=pl.ANY))
        operands.append(combined)
        aliases = {len(operands): 0}
    return pl.pallas_call(
        functools.partial(late_kernel, n_col, n_late, start == 0, width),
        grid_spec=pltpu.PrefetchScalarGridSpec(
            num_scalar_prefetch=1,
            grid=(n_col, steps),
            in_specs=in_specs,
            out_specs=rhs_spec,
        ),
        out_shape=jax.ShapeDtypeStruct(rhs.shape, F32),
        input_output_aliases=aliases,
        compiler_params=pltpu.CompilerParams(vmem_limit_bytes=VMEM_LIMIT),
        cost_estimate=pl.CostEstimate(
            flops=2 * size * n_col * width * n_late * sides * 6,
            bytes_accessed=4 * size * n_col * (width * n_late + 3 * sides),
            transcendentals=0,
        ),
        name="late_terms",
    )(scalars, *operands)


def to_col(x, k):
    n = lax.axis_size("col")
    return x if k == 0 else lax.ppermute(x, "col", [(i, (i + k) % n) for i in range(n)])


def body(panel_column, trailing, right_side, term_weights):
    column = panel_column[0]
    rows, width = column.shape
    n_term, n_row, n_col = (lax.axis_size(a) for a in ("term", "row", "col"))
    t, r, c = (lax.axis_index(a) for a in ("term", "row", "col"))
    window = trailing.shape[2]
    per_row = window * n_col // n_row
    part = rows // n_col
    sizes = chunk_sizes(part, width)
    starts = [sum(sizes[:i]) for i in range(len(sizes))]
    scalars = jnp.stack([c, (r == 0).astype(jnp.int32)]).astype(jnp.int32)

    mine = [lax.dynamic_slice_in_dim(column, c * part + o, s, 0) for o, s in zip(starts, sizes)]
    mine[0] = jnp.concatenate([mine[0], jnp.full((PAD, width), term_weights[0], F32)], axis=0)
    slots = [hops(m, t, n_term) for m in mine]

    tops = right_side[:width]
    n_side = tops.shape[1] // LANES
    packed = [column[width : width + per_row]] + [
        tops[:, i * LANES : (i + 1) * LANES] for i in range(n_side)
    ]
    packed = lax.all_gather(jnp.concatenate(packed, axis=0), "row", axis=0)
    window_rows = packed[:, :per_row].reshape(n_row * per_row, width)
    window_rows = lax.dynamic_slice_in_dim(window_rows, c * window, window, 0)
    right_top = jnp.concatenate(
        [packed[0, per_row + i * width : per_row + (i + 1) * width] for i in range(n_side)], axis=1
    )
    right_tops = jnp.concatenate([to_col(right_top, n_col - k if k else 0) for k in range(n_col)], axis=1)

    heads = [mine[0]]
    for s in range(1, n_term):
        heads.append(
            sum(
                jnp.where((source == s) & valid, buf, 0.0)
                for buf, source, valid in slots[0]
            )
        )
    weights = jnp.stack([h[sizes[0], 0] for h in heads])
    total_weight = jnp.sum(weights)
    corners = jnp.concatenate([h[:width] for h in heads], axis=0)
    others = lax.ppermute(corners, "col", [(0, 1)]) if n_col == 2 else lax.all_gather(corners, "col")[0]
    corners = jnp.where(c == 0, corners, others)
    corner = corners[:width]
    for s in range(1, n_term):
        got = lax.ppermute(corners[s * width : (s + 1) * width], "row", [(0, s)])
        corner = jnp.where(r == s, got, corner)
    lower = jnp.linalg.cholesky(corner)
    inverse = lax.linalg.triangular_solve(
        lower, jnp.eye(width, dtype=F32), left_side=True, lower=True
    )
    inverses = lax.all_gather(inverse, "row", axis=0)[:n_term]

    inverse_t = inverses[0].T
    picked_t = dot(window_rows, inverse_t).T
    factor, updated = factor_call(scalars[1:], column, trailing[0], inverse_t, picked_t, lower)

    solved = [weights[s] * dot(inverses[s], right_tops) for s in range(n_term)]
    tall = jnp.stack([dot(inverses[s].T, solved[s]) for s in range(n_term)])
    top = sum(solved)[:, : tops.shape[1]]

    def of(source, valid):
        return jnp.where(valid, lax.dynamic_index_in_dim(tall, source, 0, keepdims=False), 0.0)

    n_late = 1 if n_term > 2 else 0
    n_slots = len(slots[0])
    early_ids, late_ids = range(n_slots - n_late), range(n_slots - n_late, n_slots)
    early_weights = jnp.concatenate([tall[0]] + [of(*slots[0][i][1:]) for i in early_ids], axis=0)
    late_weights = jnp.concatenate([of(*slots[0][i][1:]) for i in late_ids], axis=0)
    late_weights = late_weights[:, : tops.shape[1]]

    combined = None
    for i, (start, size) in enumerate(zip(starts, sizes)):
        products = early_call(
            size, [mine[i]] + [slots[i][j][0] for j in early_ids], early_weights, n_col
        )
        early = [to_col(products[k], k) for k in range(n_col)]
        late = [[to_col(slots[i][j][0], k) for k in range(n_col)] for j in late_ids]
        combined = late_call(
            scalars, total_weight[None], right_side, top, late_weights, early, late,
            start, size, part, combined,
        )
    return (factor[None], updated[None], combined)


def solution(mesh):
    placed = (P("term", "row", None), P("term", "row", "col"), P("row", "col"), P("term"))
    return jax.shard_map(
        body,
        mesh=mesh,
        in_specs=placed,
        out_specs=(P("term", "row", None), P("term", "row", "col"), P("row", "col")),
        check_vma=False,
    )
```

time: 557 us -> 369 us (0.66)
  waiting for transfers between devices: 450 us -> 120 us
  Pallas kernels: 0 us -> 83.9 us
  starting transfers between devices: 0.08 us -> 60.7 us
  matrix products: 33 us -> 11.4 us
  local copies, waits for them, and re-layouts: 15.4 us -> 34.2 us
  blocking collectives: 8.56 us -> 19.7 us
  between operations: 14.8 us -> 4.03 us
    psum x2 -> x0, waiting for transfers between devices: 450 us -> none  [the longest x1 404 us: body(): combined = lax.psum(term_weights[0] * solved, 'term')]
    ppermute x0 -> x40, waiting for transfers between devices: none -> 120 us  [the longest x10 78.8 us: hops(): left = lax.ppermute(left, 'term', to_left)]
    pallas_call x0 -> x11, Pallas kernels: none -> 83.9 us  [the longest x5 30.5 us: late_call(): pl.pallas_call(functools.partial(late_kernel, n_col, n_late, start == 0,...]
    ppermute x0 -> x40, starting transfers between devices: none -> 60.7 us  [the longest x10 28.7 us: hops(): right = lax.ppermute(right, 'term', to_right)]
    dot_general x2 -> x9, matrix products: 24.9 us -> 11.1 us  [dot(): return jnp.dot(left, right, precision=HIGH, preferred_element_type=F32)]
    all_gather x1 -> x2, blocking collectives: 8.56 us -> 19.7 us  [the longest x1 11 us: body(): packed = lax.all_gather(jnp.concatenate(packed, axis=0), 'row', axis=0)]
    unnamed x12 -> x106, local copies, waits for them, and re-layouts: 11.6 us -> 20.6 us
    another operation x2 -> x1, matrix products: 8.16 us -> 0.25 us  [body(): lax.linalg.triangular_solve(lower, jnp.eye(width, dtype=F32), left_side=T...]
  transfers between devices with their start and end apart: 2 -> 40, of which waited for: 2 -> 7; matrix products, arithmetic and copies ran while one was open for 2% -> 16% of each run, Pallas kernels for 0% -> 22%
where the time goes in v1:
time: 369 us; the launch traced here: 367 us
  waiting for transfers between devices  120 us (33%)
  Pallas kernels  83.9 us (23%)
  starting transfers between devices  60.7 us (16%)
  local copies, waits for them, and re-layouts  34.2 us (9%)
  other arithmetic  33.4 us (9%)
  blocking collectives  19.7 us (5%)
  matrix products  11.4 us (3%)
  between operations  4.03 us (1%)
    ppermute x10, waiting for transfers between devices, hops(): left = lax.ppermute(left, 'term', to_left)  78.8 us
    ppermute x5, waiting for transfers between devices, hops(): right = left = lax.ppermute(right, 'term', to_right + to_left)  39.5 us
    pallas_call x5, Pallas kernels, late_call(): pl.pallas_call(functools.partial(late_kernel, n_col, n_late, start == 0,...  30.5 us
    pallas_call x5, Pallas kernels, early_call(): pl.pallas_call(functools.partial(early_kernel, len(bufs), sides), grid=(s...  29.8 us
    ppermute x10, starting transfers between devices, hops(): right = lax.ppermute(right, 'term', to_right)  28.7 us
    pallas_call x1, Pallas kernels, factor_call(): pl.pallas_call(functools.partial(factor_kernel, width), grid_spec=pltpu.P...  23.6 us
    unnamed x106, local copies, waits for them, and re-layouts  20.6 us
    ppermute x10, starting transfers between devices, hops(): left = lax.ppermute(left, 'term', to_left)  13.1 us
  transfers between devices with their start and end apart: 40, of which 7 were waited for; matrix products, arithmetic and copies ran while one was open for 16% of the time, Pallas kernels for 22%

profile of v1, /device:TPU:0, one launch (start us, length us, event | category | flops | bytes accessed | tf_op | source)
XLA Modules:
  0.0 367.0 jit_solution(5020428716287440533)
XLA Ops:
  2.4 4.9 %collective-permute-start.1 = (f32[520,128]{1,0:T(8,128)S(1)}, f32[520,128]{1,0:T(8,128)S(1)}, u32[]{:S(2)}, u32[]{:S(2)}) collective-permute-start(f32[520,128]{1,0:T(8,128)S(1)} %concatenate.19.refs_0_), channel_id=1, source_target_pairs={{0,8},{8,16},{16,24},{1,9},{9,17},{17,25},{2,10},{10,18},{18,26},{... | collective-permute-start | bytes 798728 | tf_op jit(solution)/shard_map/ppermute | solution.py:46
  7.4 1.3 collective-permute-start
  8.7 1.7 dynamic-slice_bitcast_fusion
  10.4 5.5 %collective-permute-start.31 = (f32[2048,128]{1,0:T(8,128)S(1)}, f32[2048,128]{1,0:T(8,128)}, u32[]{:S(2)}, u32[]{:S(2)}) collective-permute-start(f32[2048,128]{1,0:T(8,128)S(1)} %get-tuple-element.31.refs_0_), channel_id=1, source_target_pairs={{0,8},{8,16},{16,24},{1,9},{9,17},{17,25},{2,10},{10,18},{18,26},{... | collective-permute-start | bytes 3145736 | tf_op jit(solution)/shard_map/ppermute | solution.py:46
  15.9 1.3 collective-permute-start.32
  17.2 5.3 %collective-permute-start.10 = (f32[512,128]{1,0:T(8,128)S(1)}, f32[512,128]{1,0:T(8,128)}, u32[]{:S(2)}, u32[]{:S(2)}) collective-permute-start(f32[512,128]{1,0:T(8,128)S(1)} %get-tuple-element.33.refs_0_), channel_id=1, source_target_pairs={{0,8},{8,16},{16,24},{1,9},{9,17},{17,25},{2,10},{10,18},{18,26},{... | collective-permute-start | bytes 786440 | tf_op jit(solution)/shard_map/ppermute | solution.py:46
  23.2 1.3 collective-permute-start.3
  24.5 1.4 slice_bitcast_fusion.3
  25.8 1.5 fusion.39
  27.3 1.3 collective-permute-start.11
  28.6 19.0 %collective-permute-done.3 = f32[520,128]{1,0:T(8,128)} collective-permute-done((f32[520,128]{1,0:T(8,128)S(1)}, f32[520,128]{1,0:T(8,128)}, u32[]{:S(2)}, u32[]{:S(2)}) %collective-permute-start.3) | collective-permute-done | bytes 266272 | tf_op jit(solution)/shard_map/ppermute | solution.py:47
  48.6 1.3 collective-permute-start.4
  51.7 11.0 %all-gather.1 = f32[1280,128]{1,0:T(8,128)S(1)} all-gather(f32[320,128]{1,0:T(8,128)S(1)} %pad_maximum_fusion.3), channel_id=3, replica_groups=mesh['term'=4,'row'=4,'col'=2] {'row'}, dimensions={0}, use_global_device_ids=true | all-gather | bytes 819200 | tf_op jit(solution)/shard_map/all_gather | solution.py:226
  63.8 2.0 collective-permute-start.5
  66.5 1.6 slice.134
  68.1 1.5 pad_maximum_fusion.4
  71.4 1.3 collective-permute-start.13
  73.7 3.7 collective-permute-start.6
  77.4 1.3 collective-permute-start.7
  78.7 10.6 %collective-permute-done.13 = f32[512,128]{1,0:T(8,128)S(1)} collective-permute-done((f32[512,128]{1,0:T(8,128)}, f32[512,128]{1,0:T(8,128)S(1)}, u32[]{:S(2)}, u32[]{:S(2)}) %collective-permute-start.13) | collective-permute-done | bytes 262176 | tf_op jit(solution)/shard_map/ppermute | solution.py:47
  89.3 3.2 collective-permute-start.8
  93.2 1.2 slice.136
  94.4 1.2 slice.135
  95.6 1.2 slice.137
  96.8 4.9 %collective-permute-start.24 = (f32[2048,128]{1,0:T(8,128)S(1)}, f32[2048,128]{1,0:T(8,128)}, u32[]{:S(2)}, u32[]{:S(2)}) collective-permute-start(f32[2048,128]{1,0:T(8,128)S(1)} %get-tuple-element.32.refs_0_), channel_id=1, source_target_pairs={{0,8},{8,16},{16,24},{1,9},{9,17},{17,25},{2,10},{10,18},{18,26},{... | collective-permute-start | bytes 3145736 | tf_op jit(solution)/shard_map/ppermute | solution.py:46
  101.7 1.3 collective-permute-start.25
  103.3 11.7 %cholesky.17 = f32[128,128]{1,0:T(8,128)S(1)} custom-call(f32[128,128]{1,0:T(8,128)S(1)} %fusion.9), custom_call_target="Cholesky" | custom-call | tf_op jit(solution)/shard_map/jit(cholesky)/cholesky | solution.py:251
  116.4 9.8 %custom-call.6 = f32[1,128,128]{1,2,0:T(8,128)S(1)} custom-call(f32[1,128,128]{2,1,0:T(8,128)S(1)} %get-tuple-element.27), custom_call_target="InvertDiagBlocksLowerTriangular" | custom-call | tf_op jit(solution)/shard_map/triangular_solve | solution.py:252
  126.5 8.7 %all-gather = f32[512,128]{0,1:T(8,128)S(1)} all-gather(f32[128,128]{0,1:T(8,128)S(1)} %fusion.7), channel_id=2, replica_groups=mesh['term'=4,'row'=4,'col'=2] {'row'}, dimensions={0}, use_global_device_ids=true | all-gather | bytes 327680 | tf_op jit(solution)/shard_map/all_gather | solution.py:255
  135.2 4.6 %collective-permute-start.17 = (f32[1024,128]{1,0:T(8,128)S(1)}, f32[1024,128]{1,0:T(8,128)S(1)}, u32[]{:S(2)}, u32[]{:S(2)}) collective-permute-start(f32[1024,128]{1,0:T(8,128)S(1)} %dynamic-slice_bitcast_fusion.2.refs_0_), channel_id=1, source_target_pairs={{0,8},{8,16},{16,24},{1,9},{9,17},{17,25},{2,10},{10,18},{18,26},{... | collective-permute-start | bytes 1572872 | tf_op jit(solution)/shard_map/ppermute | solution.py:46
  140.6 1.3 collective-permute-start.34
  141.9 2.0 broadcast_multiply_fusion.1
  143.8 1.1 broadcast_select_fusion.4
  144.9 1.3 convolution_multiply_fusion
  146.7 2.0 broadcast_multiply_fusion.2
  150.3 1.5 collective-permute-start.18
  151.7 2.0 broadcast_multiply_fusion
  153.7 1.1 broadcast_select_fusion.6
  154.9 23.0 %collective-permute-done.18.refs_2_ = f32[1024,128]{1,0:T(8,128)S(1)} collective-permute-done((f32[1024,128]{1,0:T(8,128)S(1)}, f32[1024,128]{1,0:T(8,128)S(1)}, u32[]{:S(2)}, u32[]{:S(2)}) %collective-permute-start.18) | collective-permute-done | bytes 524320 | tf_op jit(solution)/shard_map/ppermute | solution.py:47
  177.8 1.3 collective-permute-start.15
  179.8 1.3 collective-permute-start.20
  181.9 1.3 collective-permute-start.27
  184.3 9.4 %early_terms.8 = (f32[2048,256]{1,0:T(8,128)S(1)}, f32[2048,256]{1,0:T(8,128)}) custom-call(f32[2048,128]{1,0:T(8,128)S(1)} %copy-done.7, f32[2048,128]{1,0:T(8,128)} %collective-permute-done.31.refs_1_, f32[2048,128]{1,0:T(8,128)} %collective-permute-done.32.refs_2_, f32[2048,128]{1,0:T(8,128)} %broadcast_select_fusion.refs_3_, ...), custom_call_target="tpu_custom_call" | custom-call | flops 6442450944 | bytes 8388608 | tf_op jit(solution)/shard_map/early_terms/pallas_call | solution.py:109
  193.8 26.2 %collective-permute-done.27 = f32[2048,128]{1,0:T(8,128)S(1)} collective-permute-done((f32[2048,128]{1,0:T(8,128)}, f32[2048,128]{1,0:T(8,128)S(1)}, u32[]{:S(2)}, u32[]{:S(2)}) %collective-permute-start.27) | collective-permute-done | bytes 1048608 | tf_op jit(solution)/shard_map/ppermute | solution.py:47
  220.0 1.1 broadcast_select_fusion.1.refs_3_
  221.1 9.3 %early_terms.7 = (f32[2048,256]{1,0:T(8,128)S(1)}, f32[2048,256]{1,0:T(8,128)}) custom-call(f32[2048,128]{1,0:T(8,128)S(1)} %copy-done.5, f32[2048,128]{1,0:T(8,128)} %collective-permute-done.24.refs_1_, f32[2048,128]{1,0:T(8,128)} %collective-permute-done.25.refs_2_, f32[2048,128]{1,0:T(8,128)} %broadcast_select_fusion.1.refs_3_, ...), custom_call_target="tpu_custom_call" | custom-call | flops 6442450944 | bytes 8388608 | tf_op jit(solution)/shard_map/early_terms/pallas_call | solution.py:109
  230.4 1.3 copy-done.2
  231.7 1.3 collective-permute-start.36
  233.0 1.3 collective-permute-start.29
  235.8 1.3 collective-permute-start.22
  239.0 1.2 copy-done.9
  243.0 1.8 early_terms.9
  248.1 5.6 %early_terms.6 = (f32[1024,256]{1,0:T(8,128)S(1)}, f32[1024,256]{1,0:T(8,128)}) custom-call(f32[1024,128]{1,0:T(8,128)S(1)} %copy-done.12, f32[1024,128]{1,0:T(8,128)S(1)} %copy-done.25, f32[1024,128]{1,0:T(8,128)S(1)} %copy-done.27, f32[1024,128]{1,0:T(8,128)} %broadcast_select_fusion.2.refs_3_, f32[512,512]{1,0:T(8,128)S(1)} %copy-done.9), custom_call_target="tpu_custom_call" | custom-call | flops 3221225472 | bytes 4194304 | tf_op jit(solution)/shard_map/early_terms/pallas_call | solution.py:109
  253.6 39.5 %collective-permute-done.22.refs_2_ = f32[1024,128]{1,0:T(8,128)S(1)} collective-permute-done((f32[1024,128]{1,0:T(8,128)}, f32[1024,128]{1,0:T(8,128)S(1)}, u32[]{:S(2)}, u32[]{:S(2)}) %collective-permute-start.22) | collective-permute-done | bytes 524320 | tf_op jit(solution)/shard_map/ppermute | solution.py:43
  295.2 2.8 copy-done.23
  298.0 23.6 %factor_update.1 = (f32[12288,128]{1,0:T(8,128)}, f32[12288,128]{1,0:T(8,128)}) custom-call(s32[1]{0:T(128)} %bitcast.flag, f32[12288,128]{1,0:T(8,128)S(1)} %bitcast.57, f32[12288,128]{1,0:T(8,128)S(1)} %bitcast.58, f32[128,128]{1,0:T(8,128)S(1)} %slice_bitcast_fusion.2.inverse_t, f32[128,128]{1,0:T(8,128)S(1)} %fusion.10.picked_t, ...), custom_call_target="tpu_custom_call" | custom-call | flops 4831838208 | bytes 25165824 | tf_op jit(solution)/shard_map/factor_update/pallas_call | solution.py:75
  321.9 3.8 %early_terms.5 = (f32[512,256]{1,0:T(8,128)S(1)}, f32[512,256]{1,0:T(8,128)}) custom-call(f32[512,128]{1,0:T(8,128)S(1)} %copy-done.22, f32[512,128]{1,0:T(8,128)} %collective-permute-done.10.refs_1_, f32[512,128]{1,0:T(8,128)} %collective-permute-done.11.refs_2_, f32[512,128]{1,0:T(8,128)} %broadcast_select_fusion.7.refs_3_, f32[512,512]{1,0:T(8,128)S(1)} %copy-done.10), custom_call_target="tpu_custom_call" | custom-call | flops 1610612736 | bytes 2097152 | tf_op jit(solution)/shard_map/early_terms/pallas_call | solution.py:109
  326.9 4.6 %copy-done = f32[12288,256]{1,0:T(8,128)S(1)} copy-done((f32[12288,256]{1,0:T(8,128)S(1)}, f32[12288,256]{1,0:T(8,128)}, u32[]{:S(2)}) %copy-start) | copy-done | bytes 12582936
  331.4 2.6 late_terms.5.refs_4_
  334.4 10.0 %late_terms.6.refs_4_ = f32[12288,256]{1,0:T(8,128)} custom-call(s32[2]{0:T(128)S(1)} %pad_add_fusion.scalars, f32[1]{0:T(128)} %bitcast.19.total_weight, f32[12288,256]{1,0:T(8,128)} %rhs.11, f32[128,256]{1,0:T(8,128)S(1)} %slice_add_fusion.top, f32[128,256]{1,0:T(8,128)S(1)} %slice.147.weights, ...), custom_call_target="tpu_custom_call", output_to_operand_aliasing={{}: (9, {})} | custom-call | flops 1610612736 | bytes 14680064 | tf_op jit(solution)/shard_map/late_terms/pallas_call | solution.py:180
  344.4 9.9 %late_terms.7.refs_4_ = f32[12288,256]{1,0:T(8,128)} custom-call(s32[2]{0:T(128)S(1)} %pad_add_fusion.scalars, f32[1]{0:T(128)} %bitcast.19.total_weight, f32[12288,256]{1,0:T(8,128)} %rhs.11, f32[128,256]{1,0:T(8,128)S(1)} %slice_add_fusion.top, f32[128,256]{1,0:T(8,128)S(1)} %slice.147.weights, ...), custom_call_target="tpu_custom_call", output_to_operand_aliasing={{}: (9, {})} | custom-call | flops 1610612736 | bytes 14680064 | tf_op jit(solution)/shard_map/late_terms/pallas_call | solution.py:180
  354.3 5.5 %late_terms.8.refs_4_ = f32[12288,256]{1,0:T(8,128)} custom-call(s32[2]{0:T(128)S(1)} %pad_add_fusion.scalars, f32[1]{0:T(128)} %bitcast.19.total_weight, f32[12288,256]{1,0:T(8,128)} %rhs.11, f32[128,256]{1,0:T(8,128)S(1)} %slice_add_fusion.top, f32[128,256]{1,0:T(8,128)S(1)} %slice.147.weights, ...), custom_call_target="tpu_custom_call", output_to_operand_aliasing={{}: (9, {})} | custom-call | flops 805306368 | bytes 7340032 | tf_op jit(solution)/shard_map/late_terms/pallas_call | solution.py:180
  359.8 4.6 %copy-done.1 = f32[12288,256]{1,0:T(8,128)S(1)} copy-done((f32[12288,256]{1,0:T(8,128)S(1)}, f32[12288,256]{1,0:T(8,128)}, u32[]{:S(2)}) %copy-start.1) | copy-done | bytes 12582936
  364.4 2.6 late_terms.9
  (186 shorter events, 28.4 us)
Async XLA Ops:
  2.4 71.3 %copy-start.21 = (f32[512,128]{1,0:T(8,128)}, f32[512,128]{1,0:T(8,128)S(1)}, u32[]{:S(2)}) copy-start(f32[512,128]{1,0:T(8,128)S(1)} %get-tuple-element.33.refs_0_) | copy-start | bytes 786436
  2.4 45.3 %copy-start.13 = (f32[520,128]{1,0:T(8,128)}, f32[520,128]{1,0:T(8,128)S(1)}, u32[]{:S(2)}) copy-start(f32[520,128]{1,0:T(8,128)S(1)} %concatenate.19.refs_0_) | copy-start | bytes 798724
  2.4 20.1 %collective-permute-start.1 = (f32[520,128]{1,0:T(8,128)S(1)}, f32[520,128]{1,0:T(8,128)S(1)}, u32[]{:S(2)}, u32[]{:S(2)}) collective-permute-start(f32[520,128]{1,0:T(8,128)S(1)} %concatenate.19.refs_0_), channel_id=1, source_target_pairs={{0,8},{8,16},{16,24},{1,9},{9,17},{17,25},{2,10},{10,18},{18,26},{... | collective-permute-start | bytes 798728 | tf_op jit(solution)/shard_map/ppermute | solution.py:46
  7.4 15.8 %collective-permute-start = (f32[520,128]{1,0:T(8,128)S(1)}, f32[520,128]{1,0:T(8,128)S(1)}, u32[]{:S(2)}, u32[]{:S(2)}) collective-permute-start(f32[520,128]{1,0:T(8,128)S(1)} %concatenate.19.refs_0_), channel_id=1, source_target_pairs={{8,0},{16,8},{24,16},{9,1},{17,9},{25,17},{10,2},{18,10},{26,18},{... | collective-permute-start | bytes 798728 | tf_op jit(solution)/shard_map/ppermute | solution.py:47
  10.3 136.3 %copy-start.4 = (f32[2048,128]{1,0:T(8,128)}, f32[2048,128]{1,0:T(8,128)S(1)}, u32[]{:S(2)}) copy-start(f32[2048,128]{1,0:T(8,128)S(1)} %get-tuple-element.32.refs_0_) | copy-start | bytes 3145732
  10.4 136.3 %copy-start.6 = (f32[2048,128]{1,0:T(8,128)}, f32[2048,128]{1,0:T(8,128)S(1)}, u32[]{:S(2)}) copy-start(f32[2048,128]{1,0:T(8,128)S(1)} %get-tuple-element.31.refs_0_) | copy-start | bytes 3145732
  10.4 129.4 %collective-permute-start.31 = (f32[2048,128]{1,0:T(8,128)S(1)}, f32[2048,128]{1,0:T(8,128)}, u32[]{:S(2)}, u32[]{:S(2)}) collective-permute-start(f32[2048,128]{1,0:T(8,128)S(1)} %get-tuple-element.31.refs_0_), channel_id=1, source_target_pairs={{0,8},{8,16},{16,24},{1,9},{9,17},{17,25},{2,10},{10,18},{18,26},{... | collective-permute-start | bytes 3145736 | tf_op jit(solution)/shard_map/ppermute | solution.py:46
  15.9 124.7 %collective-permute-start.32 = (f32[2048,128]{1,0:T(8,128)S(1)}, f32[2048,128]{1,0:T(8,128)}, u32[]{:S(2)}, u32[]{:S(2)}) collective-permute-start(f32[2048,128]{1,0:T(8,128)S(1)} %get-tuple-element.31.refs_0_), channel_id=1, source_target_pairs={{8,0},{16,8},{24,16},{9,1},{17,9},{25,17},{10,2},{18,10},{26,18},{... | collective-permute-start | bytes 3145736 | tf_op jit(solution)/shard_map/ppermute | solution.py:47
  17.2 53.5 %collective-permute-start.10 = (f32[512,128]{1,0:T(8,128)S(1)}, f32[512,128]{1,0:T(8,128)}, u32[]{:S(2)}, u32[]{:S(2)}) collective-permute-start(f32[512,128]{1,0:T(8,128)S(1)} %get-tuple-element.33.refs_0_), channel_id=1, source_target_pairs={{0,8},{8,16},{16,24},{1,9},{9,17},{17,25},{2,10},{10,18},{18,26},{... | collective-permute-start | bytes 786440 | tf_op jit(solution)/shard_map/ppermute | solution.py:46
  22.5 45.6 %copy-start.15 = (f32[520,128]{1,0:T(8,128)}, f32[520,128]{1,0:T(8,128)S(1)}, u32[]{:S(2)}) copy-start(f32[520,128]{1,0:T(8,128)S(1)} %collective-permute-done.1.refs_1_) | copy-start | bytes 798724
  22.5 4.9 %collective-permute-start.2 = (f32[520,128]{1,0:T(8,128)S(1)}, f32[520,128]{1,0:T(8,128)S(1)}, u32[]{:S(2)}, u32[]{:S(2)}) collective-permute-start(f32[520,128]{1,0:T(8,128)S(1)} %collective-permute-done.1.refs_1_), channel_id=1, source_target_pairs={{8,16},{16,24},{9,17},{17,25},{10,18},{18,26},{11,19},{19,27},{12,... | collective-permute-start | bytes 798728 | tf_op jit(solution)/shard_map/ppermute | solution.py:46
  23.1 44.9 %copy-start.17 = (f32[520,128]{1,0:T(8,128)}, f32[520,128]{1,0:T(8,128)S(1)}, u32[]{:S(2)}) copy-start(f32[520,128]{1,0:T(8,128)S(1)} %collective-permute-done.refs_2_) | copy-start | bytes 798724
  23.2 24.5 %collective-permute-start.3 = (f32[520,128]{1,0:T(8,128)S(1)}, f32[520,128]{1,0:T(8,128)}, u32[]{:S(2)}, u32[]{:S(2)}) collective-permute-start(f32[520,128]{1,0:T(8,128)S(1)} %collective-permute-done.refs_2_), channel_id=1, source_target_pairs={{8,0},{16,8},{9,1},{17,9},{10,2},{18,10},{11,3},{19,11},{12,4},{20... | collective-permute-start | bytes 798728 | tf_op jit(solution)/shard_map/ppermute | solution.py:47
  27.3 44.0 %collective-permute-start.11 = (f32[512,128]{1,0:T(8,128)S(1)}, f32[512,128]{1,0:T(8,128)}, u32[]{:S(2)}, u32[]{:S(2)}) collective-permute-start(f32[512,128]{1,0:T(8,128)S(1)} %get-tuple-element.33.refs_0_), channel_id=1, source_target_pairs={{8,0},{16,8},{24,16},{9,1},{17,9},{25,17},{10,2},{18,10},{26,18},{... | collective-permute-start | bytes 786440 | tf_op jit(solution)/shard_map/ppermute | solution.py:47
  48.6 14.0 %collective-permute-start.4 = (f32[520,128]{1,0:T(8,128)S(1)}, f32[520,128]{1,0:T(8,128)S(1)}, u32[]{:S(2)}, u32[]{:S(2)}) collective-permute-start(f32[520,128]{1,0:T(8,128)S(1)} %broadcast_select_fusion.3.refs_3_), channel_id=1, source_target_pairs={{16,24},{8,0},{17,25},{9,1},{18,26},{10,2},{19,27},{11,3},{20,28},... | collective-permute-start | bytes 798728 | tf_op jit(solution)/shard_map/ppermute | solution.py:43
  63.8 8.9 %collective-permute-start.5 = (f32[512,128]{1,0:T(8,128)}, f32[512,128]{1,0:T(8,128)}, u32[]{:S(2)}, u32[]{:S(2)}) collective-permute-start(f32[512,128]{1,0:T(8,128)} %pad_maximum_fusion.1), channel_id=1, source_target_pairs={{0,1},{2,3},{4,5},{6,7},{8,9},{10,11},{12,13},{14,15},{16,17},{18,... | collective-permute-start | bytes 786440 | tf_op jit(solution)/shard_map/ppermute | solution.py:245
  70.6 113.7 %copy-start.11 = (f32[1024,128]{1,0:T(8,128)}, f32[1024,128]{1,0:T(8,128)S(1)}, u32[]{:S(2)}) copy-start(f32[1024,128]{1,0:T(8,128)S(1)} %dynamic-slice_bitcast_fusion.2.refs_0_) | copy-start | bytes 1572868
  70.7 6.7 %collective-permute-start.12 = (f32[512,128]{1,0:T(8,128)}, f32[512,128]{1,0:T(8,128)S(1)}, u32[]{:S(2)}, u32[]{:S(2)}) collective-permute-start(f32[512,128]{1,0:T(8,128)} %collective-permute-done.10.refs_1_), channel_id=1, source_target_pairs={{8,16},{16,24},{9,17},{17,25},{10,18},{18,26},{11,19},{19,27},{12,... | collective-permute-start | bytes 786440 | tf_op jit(solution)/shard_map/ppermute | solution.py:46
  71.4 17.9 %collective-permute-start.13 = (f32[512,128]{1,0:T(8,128)}, f32[512,128]{1,0:T(8,128)S(1)}, u32[]{:S(2)}, u32[]{:S(2)}) collective-permute-start(f32[512,128]{1,0:T(8,128)} %collective-permute-done.11.refs_2_), channel_id=1, source_target_pairs={{8,0},{16,8},{9,1},{17,9},{10,2},{18,10},{11,3},{19,11},{12,4},{20... | collective-permute-start | bytes 786440 | tf_op jit(solution)/shard_map/ppermute | solution.py:47
  73.7 23.1 %collective-permute-start.6 = (f32[128,128]{1,0:T(8,128)S(1)}, f32[128,128]{1,0:T(8,128)S(1)}, u32[]{:S(2)}, u32[]{:S(2)}) collective-permute-start(f32[128,128]{1,0:T(8,128)S(1)} %get-tuple-element.42), channel_id=1, source_target_pairs={{0,6},{1,7},{8,14},{9,15},{16,22},{17,23},{24,30},{25,31}} | collective-permute-start | bytes 196616 | tf_op jit(solution)/shard_map/ppermute | solution.py:249
  77.4 24.4 %collective-permute-start.7 = (f32[128,128]{1,0:T(8,128)S(1)}, f32[128,128]{1,0:T(8,128)S(1)}, u32[]{:S(2)}, u32[]{:S(2)}) collective-permute-start(f32[128,128]{1,0:T(8,128)S(1)} %get-tuple-element.41), channel_id=1, source_target_pairs={{0,4},{1,5},{8,12},{9,13},{16,20},{17,21},{24,28},{25,29}} | collective-permute-start | bytes 196616 | tf_op jit(solution)/shard_map/ppermute | solution.py:249
  89.3 13.7 %collective-permute-start.8 = (f32[128,128]{1,0:T(8,128)S(1)}, f32[128,128]{1,0:T(8,128)S(1)}, u32[]{:S(2)}, u32[]{:S(2)}) collective-permute-start(f32[128,128]{1,0:T(8,128)S(1)} %get-tuple-element.40), channel_id=1, source_target_pairs={{0,2},{1,3},{8,10},{9,11},{16,18},{17,19},{24,26},{25,27}} | collective-permute-start | bytes 196616 | tf_op jit(solution)/shard_map/ppermute | solution.py:249
  96.8 82.3 %collective-permute-start.24 = (f32[2048,128]{1,0:T(8,128)S(1)}, f32[2048,128]{1,0:T(8,128)}, u32[]{:S(2)}, u32[]{:S(2)}) collective-permute-start(f32[2048,128]{1,0:T(8,128)S(1)} %get-tuple-element.32.refs_0_), channel_id=1, source_target_pairs={{0,8},{8,16},{16,24},{1,9},{9,17},{17,25},{2,10},{10,18},{18,26},{... | collective-permute-start | bytes 3145736 | tf_op jit(solution)/shard_map/ppermute | solution.py:46
  101.7 78.1 %collective-permute-start.25 = (f32[2048,128]{1,0:T(8,128)S(1)}, f32[2048,128]{1,0:T(8,128)}, u32[]{:S(2)}, u32[]{:S(2)}) collective-permute-start(f32[2048,128]{1,0:T(8,128)S(1)} %get-tuple-element.32.refs_0_), channel_id=1, source_target_pairs={{8,0},{16,8},{24,16},{9,1},{17,9},{25,17},{10,2},{18,10},{26,18},{... | collective-permute-start | bytes 3145736 | tf_op jit(solution)/shard_map/ppermute | solution.py:47
  103.0 32.2 %collective-permute-start.9 = (f32[128,256]{1,0:T(8,128)}, f32[128,256]{1,0:T(8,128)}, u32[]{:S(2)}, u32[]{:S(2)}) collective-permute-start(f32[128,256]{1,0:T(8,128)} %pad_maximum_fusion.4), channel_id=1, source_target_pairs={{0,1},{1,0},{2,3},{3,2},{4,5},{5,4},{6,7},{7,6},{8,9},{9,8},{10,11... | collective-permute-start | bytes 393224 | tf_op jit(solution)/shard_map/ppermute | solution.py:202
  135.2 58.5 %copy-start.28 = (f32[512,128]{0,1:T(8,128)}, f32[512,128]{0,1:T(8,128)S(1)}, u32[]{:S(2)}) copy-start(f32[512,128]{0,1:T(8,128)S(1)} %all-gather) | copy-start | bytes 786436
  135.2 15.0 %collective-permute-start.17 = (f32[1024,128]{1,0:T(8,128)S(1)}, f32[1024,128]{1,0:T(8,128)S(1)}, u32[]{:S(2)}, u32[]{:S(2)}) collective-permute-start(f32[1024,128]{1,0:T(8,128)S(1)} %dynamic-slice_bitcast_fusion.2.refs_0_), channel_id=1, source_target_pairs={{0,8},{8,16},{16,24},{1,9},{9,17},{17,25},{2,10},{10,18},{18,26},{... | collective-permute-start | bytes 1572872 | tf_op jit(solution)/shard_map/ppermute | solution.py:46
  139.8 41.3 %collective-permute-start.33 = (f32[2048,128]{1,0:T(8,128)}, f32[2048,128]{1,0:T(8,128)S(1)}, u32[]{:S(2)}, u32[]{:S(2)}) collective-permute-start(f32[2048,128]{1,0:T(8,128)} %collective-permute-done.31.refs_1_), channel_id=1, source_target_pairs={{8,16},{16,24},{9,17},{17,25},{10,18},{18,26},{11,19},{19,27},{12,... | collective-permute-start | bytes 3145736 | tf_op jit(solution)/shard_map/ppermute | solution.py:46
  140.6 41.3 %collective-permute-start.34 = (f32[2048,128]{1,0:T(8,128)}, f32[2048,128]{1,0:T(8,128)S(1)}, u32[]{:S(2)}, u32[]{:S(2)}) collective-permute-start(f32[2048,128]{1,0:T(8,128)} %collective-permute-done.32.refs_2_), channel_id=1, source_target_pairs={{8,0},{16,8},{9,1},{17,9},{10,2},{18,10},{11,3},{19,11},{12,4},{20... | collective-permute-start | bytes 3145736 | tf_op jit(solution)/shard_map/ppermute | solution.py:47
  146.7 37.6 %copy-start.7 = (f32[2048,128]{1,0:T(8,128)S(1)}, f32[2048,128]{1,0:T(8,128)}, u32[]{:S(2)}) copy-start(f32[2048,128]{1,0:T(8,128)} %copy-done.6) | copy-start | bytes 3145732
  148.7 34.5 %copy-start.36 = (f32[128,512]{1,0:T(8,128)}, f32[128,512]{1,0:T(8,128)S(1)}, u32[]{:S(2)}) copy-start(f32[128,512]{1,0:T(8,128)S(1)} %broadcast_multiply_fusion.2) | copy-start | bytes 786436
  150.3 43.4 %copy-start.24 = (f32[1024,128]{1,0:T(8,128)}, f32[1024,128]{1,0:T(8,128)S(1)}, u32[]{:S(2)}) copy-start(f32[1024,128]{1,0:T(8,128)S(1)} %collective-permute-done.17.refs_1_) | copy-start | bytes 1572868
  150.3 27.6 %collective-permute-start.18 = (f32[1024,128]{1,0:T(8,128)S(1)}, f32[1024,128]{1,0:T(8,128)S(1)}, u32[]{:S(2)}, u32[]{:S(2)}) collective-permute-start(f32[1024,128]{1,0:T(8,128)S(1)} %dynamic-slice_bitcast_fusion.2.refs_0_), channel_id=1, source_target_pairs={{8,0},{16,8},{24,16},{9,1},{17,9},{25,17},{10,2},{18,10},{26,18},{... | collective-permute-start | bytes 1572872 | tf_op jit(solution)/shard_map/ppermute | solution.py:47
  153.7 29.5 %copy-start.38 = (f32[128,512]{1,0:T(8,128)}, f32[128,512]{1,0:T(8,128)S(1)}, u32[]{:S(2)}) copy-start(f32[128,512]{1,0:T(8,128)S(1)} %broadcast_multiply_fusion) | copy-start | bytes 786436
  154.9 66.2 %copy-start.8 = (f32[512,512]{1,0:T(8,128)}, f32[512,512]{1,0:T(8,128)S(1)}, u32[]{:S(2)}) copy-start(f32[512,512]{1,0:T(8,128)S(1)} %pad_maximum_fusion.refs_4_) | copy-start | bytes 3145732
  177.8 53.9 %collective-permute-start.15 = (f32[512,128]{1,0:T(8,128)}, f32[512,128]{1,0:T(8,128)S(1)}, u32[]{:S(2)}, u32[]{:S(2)}) collective-permute-start(f32[512,128]{1,0:T(8,128)} %broadcast_select_fusion.7.refs_3_), channel_id=1, source_target_pairs={{16,24},{8,0},{17,25},{9,1},{18,26},{10,2},{19,27},{11,3},{20,28},... | collective-permute-start | bytes 786440 | tf_op jit(solution)/shard_map/ppermute | solution.py:43
  179.1 53.9 %collective-permute-start.19 = (f32[1024,128]{1,0:T(8,128)S(1)}, f32[1024,128]{1,0:T(8,128)S(1)}, u32[]{:S(2)}, u32[]{:S(2)}) collective-permute-start(f32[1024,128]{1,0:T(8,128)S(1)} %collective-permute-done.17.refs_1_), channel_id=1, source_target_pairs={{8,16},{16,24},{9,17},{17,25},{10,18},{18,26},{11,19},{19,27},{12,... | collective-permute-start | bytes 1572872 | tf_op jit(solution)/shard_map/ppermute | solution.py:46
  179.8 54.5 %collective-permute-start.20 = (f32[1024,128]{1,0:T(8,128)S(1)}, f32[1024,128]{1,0:T(8,128)S(1)}, u32[]{:S(2)}, u32[]{:S(2)}) collective-permute-start(f32[1024,128]{1,0:T(8,128)S(1)} %collective-permute-done.18.refs_2_), channel_id=1, source_target_pairs={{8,0},{16,8},{9,1},{17,9},{10,2},{18,10},{11,3},{19,11},{12,4},{20... | collective-permute-start | bytes 1572872 | tf_op jit(solution)/shard_map/ppermute | solution.py:47
  181.2 12.5 %collective-permute-start.26 = (f32[2048,128]{1,0:T(8,128)}, f32[2048,128]{1,0:T(8,128)S(1)}, u32[]{:S(2)}, u32[]{:S(2)}) collective-permute-start(f32[2048,128]{1,0:T(8,128)} %collective-permute-done.24.refs_1_), channel_id=1, source_target_pairs={{8,16},{16,24},{9,17},{17,25},{10,18},{18,26},{11,19},{19,27},{12,... | collective-permute-start | bytes 3145736 | tf_op jit(solution)/shard_map/ppermute | solution.py:46
  181.9 38.1 %collective-permute-start.27 = (f32[2048,128]{1,0:T(8,128)}, f32[2048,128]{1,0:T(8,128)S(1)}, u32[]{:S(2)}, u32[]{:S(2)}) collective-permute-start(f32[2048,128]{1,0:T(8,128)} %collective-permute-done.25.refs_2_), channel_id=1, source_target_pairs={{8,0},{16,8},{9,1},{17,9},{10,2},{18,10},{11,3},{19,11},{12,4},{20... | collective-permute-start | bytes 3145736 | tf_op jit(solution)/shard_map/ppermute | solution.py:47
  184.3 36.8 %copy-start.5 = (f32[2048,128]{1,0:T(8,128)S(1)}, f32[2048,128]{1,0:T(8,128)}, u32[]{:S(2)}) copy-start(f32[2048,128]{1,0:T(8,128)} %copy-done.4) | copy-start | bytes 3145732
  193.7 42.0 %collective-permute-start.39 = (f32[520,128]{1,0:T(8,128)S(1)}, f32[520,128]{1,0:T(8,128)S(1)}, u32[]{:S(2)}, u32[]{:S(2)}) collective-permute-start(f32[520,128]{1,0:T(8,128)S(1)} %collective-permute-done.4.refs_2_), channel_id=1, source_target_pairs={{0,1},{1,0},{2,3},{3,2},{4,5},{5,4},{6,7},{7,6},{8,9},{9,8},{10,11... | collective-permute-start | bytes 798728 | tf_op jit(solution)/shard_map/ppermute | solution.py:202
  220.0 101.5 %collective-permute-start.35 = (f32[2048,256]{1,0:T(8,128)}, f32[2048,256]{1,0:T(8,128)}, u32[]{:S(2)}, u32[]{:S(2)}) collective-permute-start(f32[2048,256]{1,0:T(8,128)} %get-tuple-element.24), channel_id=1, source_target_pairs={{0,1},{1,0},{2,3},{3,2},{4,5},{5,4},{6,7},{7,6},{8,9},{9,8},{10,11... | collective-permute-start | bytes 6291464 | tf_op jit(solution)/shard_map/ppermute | solution.py:202
  231.7 61.5 %collective-permute-start.36 = (f32[2048,128]{1,0:T(8,128)}, f32[2048,128]{1,0:T(8,128)}, u32[]{:S(2)}, u32[]{:S(2)}) collective-permute-start(f32[2048,128]{1,0:T(8,128)} %broadcast_select_fusion.refs_3_), channel_id=1, source_target_pairs={{16,24},{8,0},{17,25},{9,1},{18,26},{10,2},{19,27},{11,3},{20,28},... | collective-permute-start | bytes 3145736 | tf_op jit(solution)/shard_map/ppermute | solution.py:43
  233.0 60.7 %collective-permute-start.29 = (f32[2048,128]{1,0:T(8,128)}, f32[2048,128]{1,0:T(8,128)}, u32[]{:S(2)}, u32[]{:S(2)}) collective-permute-start(f32[2048,128]{1,0:T(8,128)} %broadcast_select_fusion.1.refs_3_), channel_id=1, source_target_pairs={{16,24},{8,0},{17,25},{9,1},{18,26},{10,2},{19,27},{11,3},{20,28},... | collective-permute-start | bytes 3145736 | tf_op jit(solution)/shard_map/ppermute | solution.py:43
  234.4 99.7 %collective-permute-start.28 = (f32[2048,256]{1,0:T(8,128)}, f32[2048,256]{1,0:T(8,128)}, u32[]{:S(2)}, u32[]{:S(2)}) collective-permute-start(f32[2048,256]{1,0:T(8,128)} %get-tuple-element.22), channel_id=1, source_target_pairs={{0,1},{1,0},{2,3},{3,2},{4,5},{5,4},{6,7},{7,6},{8,9},{9,8},{10,11... | collective-permute-start | bytes 6291464 | tf_op jit(solution)/shard_map/ppermute | solution.py:202
  235.8 57.3 %collective-permute-start.22 = (f32[1024,128]{1,0:T(8,128)}, f32[1024,128]{1,0:T(8,128)S(1)}, u32[]{:S(2)}, u32[]{:S(2)}) collective-permute-start(f32[1024,128]{1,0:T(8,128)} %broadcast_select_fusion.2.refs_3_), channel_id=1, source_target_pairs={{16,24},{8,0},{17,25},{9,1},{18,26},{10,2},{19,27},{11,3},{20,28},... | collective-permute-start | bytes 1572872 | tf_op jit(solution)/shard_map/ppermute | solution.py:43
  243.0 52.1 %slice-start = ((s8[6291456]{0:T(1024)(128)(4,1)}), s8[4194304]{0:T(1024)(128)(4,1)S(1)}, s32[]{:S(2)}) async-start(s8[6291456]{0:T(1024)(128)(4,1)} %bitcast.55), calls=%async_computation | async-start | bytes 8388608
  248.0 45.1 %copy-start.33 = (f32[128,512]{1,0:T(8,128)S(1)}, f32[128,512]{1,0:T(8,128)}, u32[]{:S(2)}) copy-start(f32[128,512]{1,0:T(8,128)} %copy-done.32) | copy-start | bytes 786436
  248.0 45.1 %copy-start.35 = (f32[128,512]{1,0:T(8,128)S(1)}, f32[128,512]{1,0:T(8,128)}, u32[]{:S(2)}) copy-start(f32[128,512]{1,0:T(8,128)} %copy-done.34) | copy-start | bytes 786436
  248.0 45.1 %copy-start.37 = (f32[128,512]{1,0:T(8,128)S(1)}, f32[128,512]{1,0:T(8,128)}, u32[]{:S(2)}) copy-start(f32[128,512]{1,0:T(8,128)} %copy-done.36) | copy-start | bytes 786436
  248.0 45.1 %copy-start.39 = (f32[128,512]{1,0:T(8,128)S(1)}, f32[128,512]{1,0:T(8,128)}, u32[]{:S(2)}) copy-start(f32[128,512]{1,0:T(8,128)} %copy-done.38) | copy-start | bytes 786436
  248.0 45.7 %copy-start.29 = (f32[512,128]{0,1:T(8,128)S(1)}, f32[512,128]{0,1:T(8,128)}, u32[]{:S(2)}) copy-start(f32[512,128]{0,1:T(8,128)} %copy-done.28) | copy-start | bytes 786436
  248.0 45.9 %copy-start.49 = (f32[4,64,128]{2,1,0:T(8,128)S(1)}, f32[4,64,128]{2,1,0:T(8,128)}, u32[]{:S(2)}) copy-start(f32[4,64,128]{2,1,0:T(8,128)} %slice.134) | copy-start | bytes 393220
  248.0 47.1 %slice-start.1 = ((s8[6291456]{0:T(1024)(128)(4,1)}), s8[2097152]{0:T(1024)(128)(4,1)S(1)}, s32[]{:S(2)}) async-start(s8[6291456]{0:T(1024)(128)(4,1)} %bitcast.55), calls=%async_computation.1 | async-start | bytes 4194304
  293.1 1.9 collective-permute-start.38
  293.2 32.4 %collective-permute-start.37 = (f32[2048,128]{1,0:T(8,128)}, f32[2048,128]{1,0:T(8,128)S(1)}, u32[]{:S(2)}, u32[]{:S(2)}) collective-permute-start(f32[2048,128]{1,0:T(8,128)} %collective-permute-done.36.refs_2_), channel_id=1, source_target_pairs={{0,1},{1,0},{2,3},{3,2},{4,5},{5,4},{6,7},{7,6},{8,9},{9,8},{10,11... | collective-permute-start | bytes 3145736 | tf_op jit(solution)/shard_map/ppermute | solution.py:202
  293.8 50.6 %collective-permute-start.30 = (f32[2048,128]{1,0:T(8,128)}, f32[2048,128]{1,0:T(8,128)S(1)}, u32[]{:S(2)}, u32[]{:S(2)}) collective-permute-start(f32[2048,128]{1,0:T(8,128)} %collective-permute-done.29.refs_2_), channel_id=1, source_target_pairs={{0,1},{1,0},{2,3},{3,2},{4,5},{5,4},{6,7},{7,6},{8,9},{9,8},{10,11... | collective-permute-start | bytes 3145736 | tf_op jit(solution)/shard_map/ppermute | solution.py:202
  295.0 59.3 %collective-permute-start.21 = (f32[1024,256]{1,0:T(8,128)}, f32[1024,256]{1,0:T(8,128)S(1)}, u32[]{:S(2)}, u32[]{:S(2)}) collective-permute-start(f32[1024,256]{1,0:T(8,128)} %get-tuple-element.20), channel_id=1, source_target_pairs={{0,1},{1,0},{2,3},{3,2},{4,5},{5,4},{6,7},{7,6},{8,9},{9,8},{10,11... | collective-permute-start | bytes 3145736 | tf_op jit(solution)/shard_map/ppermute | solution.py:202
  297.9 27.8 %copy-start.31 = (f32[128,512]{1,0:T(8,128)S(1)}, f32[128,512]{1,0:T(8,128)}, u32[]{:S(2)}) copy-start(f32[128,512]{1,0:T(8,128)} %copy-done.30) | copy-start | bytes 786436
  297.9 27.8 %copy-start.41 = (f32[128,512]{1,0:T(8,128)S(1)}, f32[128,512]{1,0:T(8,128)}, u32[]{:S(2)}) copy-start(f32[128,512]{1,0:T(8,128)} %get-tuple-element.44) | copy-start | bytes 786436
  321.5 32.8 %collective-permute-start.23 = (f32[1024,128]{1,0:T(8,128)S(1)}, f32[1024,128]{1,0:T(8,128)S(1)}, u32[]{:S(2)}, u32[]{:S(2)}) collective-permute-start(f32[1024,128]{1,0:T(8,128)S(1)} %collective-permute-done.22.refs_2_), channel_id=1, source_target_pairs={{0,1},{1,0},{2,3},{3,2},{4,5},{5,4},{6,7},{7,6},{8,9},{9,8},{10,11... | collective-permute-start | bytes 1572872 | tf_op jit(solution)/shard_map/ppermute | solution.py:202
  325.6 34.2 %collective-permute-start.14 = (f32[512,256]{1,0:T(8,128)}, f32[512,256]{1,0:T(8,128)S(1)}, u32[]{:S(2)}, u32[]{:S(2)}) collective-permute-start(f32[512,256]{1,0:T(8,128)} %get-tuple-element.18), channel_id=1, source_target_pairs={{0,1},{1,0},{2,3},{3,2},{4,5},{5,4},{6,7},{7,6},{8,9},{9,8},{10,11... | collective-permute-start | bytes 1572872 | tf_op jit(solution)/shard_map/ppermute | solution.py:202
  334.0 25.8 %collective-permute-start.16 = (f32[512,128]{1,0:T(8,128)S(1)}, f32[512,128]{1,0:T(8,128)S(1)}, u32[]{:S(2)}, u32[]{:S(2)}) collective-permute-start(f32[512,128]{1,0:T(8,128)S(1)} %copy-done.20), channel_id=1, source_target_pairs={{0,1},{1,0},{2,3},{3,2},{4,5},{5,4},{6,7},{7,6},{8,9},{9,8},{10,11... | collective-permute-start | bytes 786440 | tf_op jit(solution)/shard_map/ppermute | solution.py:202
  (29 other events, 155.9 us)

commit v2 on v1

v2 whole, which is shorter than its diff:
```python
import functools
import math

import jax
import jax.numpy as jnp
from jax import lax
from jax.experimental import pallas as pl
from jax.experimental.pallas import tpu as pltpu
from jax.sharding import PartitionSpec as P

HIGH = lax.Precision.HIGHEST
F32 = jnp.float32
BF16 = jnp.bfloat16
LANES = 128
PAD = 8
VMEM_LIMIT = 60 * 1024 * 1024
ANY = pl.BlockSpec(memory_space=pl.ANY)
COST = pl.CostEstimate(flops=1, bytes_accessed=1, transcendentals=0)


def dot(left, right):
    return jnp.dot(left, right, precision=HIGH, preferred_element_type=F32)


def chunk_sizes(part, width):
    unit = part // 12
    if part % 12 == 0 and unit % 8 == 0 and unit >= width:
        return [unit, 9 * unit, 2 * unit], [1, 3, 1]
    parts = part // width
    return [width, (parts - 2) * width, width], [1, 1, 1]


def block_rows(*extents):
    return math.gcd(512, *extents)


def send_hop(h, mine, t, n):
    to_right = [(j, j + 1) for j in range(h - 1, n - 1)]
    to_left = [(j, j - 1) for j in range(1, n - h + 1)]
    if 2 * (h - 1) > n - 1:
        return (lax.ppermute(mine[0], "term", to_right + to_left),)
    return (lax.ppermute(mine[0], "term", to_right), lax.ppermute(mine[-1], "term", to_left))


def merge_hop(h, got, t, n):
    if len(got) == 2 and 2 * h > n - 1:
        return (jnp.where(t >= h, got[0], got[1]),)
    return got


def slot_terms(t, n):
    slots = []
    for h in range(1, n):
        if 2 * h > n - 1:
            slots.append((h, 0, jnp.where(t >= h, n - h, h), (t >= h) | (t < n - h)))
        else:
            slots.append((h, 0, jnp.int32(n - h), t >= h))
            slots.append((h, 1, jnp.int32(h), t < n - h))
    return slots


def gate(token, after, passed):
    def kernel(*refs):
        pass

    first = 1 + len(after)
    outs = [token, *passed]
    got = pl.pallas_call(
        kernel,
        in_specs=[ANY] * (first + len(passed)),
        out_specs=[ANY] * len(outs),
        out_shape=[jax.ShapeDtypeStruct(a.shape, a.dtype) for a in outs],
        input_output_aliases={0: 0} | {first + i: 1 + i for i in range(len(passed))},
        compiler_params=pltpu.CompilerParams(vmem_limit_bytes=VMEM_LIMIT),
        cost_estimate=COST,
        name="gate",
    )(token, *after, *passed)
    return got[0], got[1:]


def factor_kernel(width, flag, panel, trailing, inverse_t, picked_t, lower, factor, updated):
    solved = dot(panel[...], inverse_t[...])
    factor[...] = solved

    @pl.when((pl.program_id(0) == 0) & (flag[0] == 1))
    def _():
        factor[:width] = lower[...]

    updated[...] = trailing[...] - dot(factor[...], picked_t[...])


def factor_call(leading, panel, trailing, inverse_t, picked_t, lower):
    rows, width = panel.shape
    window = trailing.shape[1]
    block = block_rows(rows) * (2 if rows % 1024 == 0 else 1)
    whole = lambda a: pl.BlockSpec(a.shape, lambda i, f: (0, 0))
    tile = lambda n: pl.BlockSpec((block, n), lambda i, f: (i, 0))
    return pl.pallas_call(
        functools.partial(factor_kernel, width),
        grid_spec=pltpu.PrefetchScalarGridSpec(
            num_scalar_prefetch=1,
            grid=(rows // block,),
            in_specs=[tile(width), tile(window), whole(inverse_t), whole(picked_t), whole(lower)],
            out_specs=[tile(width), tile(window)],
        ),
        out_shape=[
            jax.ShapeDtypeStruct((rows, width), F32),
            jax.ShapeDtypeStruct((rows, window), F32),
        ],
        compiler_params=pltpu.CompilerParams(vmem_limit_bytes=VMEM_LIMIT),
        cost_estimate=COST,
        name="factor_update",
    )(leading, panel, trailing, inverse_t, picked_t, lower)


def split(x):
    high = x.astype(BF16)
    return high, (x - high.astype(F32)).astype(BF16)


def subtract(scalars, total_weight, rhs, product, top, out, first, part, step):
    out[...] = total_weight[0] * rhs[...] - product
    if first:

        @pl.when((part == 0) & (scalars[1] == 1) & (step == 0))
        def _():
            out[: top.shape[0]] = top[...]


def product_kernel(n_terms, n_col, first, scalars, total_weight, rhs, top, weights, *refs):
    bufs, outs = refs[:n_terms], refs[-n_col:]
    sides = rhs.shape[1]
    high, low = split(jnp.concatenate([b[...] for b in bufs], axis=1))
    stacked = jnp.concatenate([high, low, high], axis=1)

    def product(k):
        return jnp.dot(
            stacked, weights[:, k * sides : (k + 1) * sides], preferred_element_type=F32
        )

    for k in range(1, n_col):
        outs[k][...] = product(k)
    step = pl.program_id(0)
    subtract(scalars, total_weight, rhs, product(0), top, outs[0], first, scalars[0], step)


def product_call(common, bufs, firsts, weights, start, size, part, n_col, combined, after):
    scalars, total_weight, rhs, top = common
    width = bufs[0].shape[1]
    sides = rhs.shape[1]
    block = block_rows(size, start, part, *firsts)
    at = lambda i, s: (s[0] * (part // block) + start // block + i, 0)
    in_specs = [
        pl.BlockSpec(memory_space=pltpu.SMEM),
        pl.BlockSpec((block, sides), at),
        pl.BlockSpec(top.shape, lambda i, s: (0, 0)),
        pl.BlockSpec(weights.shape, lambda i, s: (0, 0)),
    ]
    in_specs += [
        pl.BlockSpec((block, width), lambda i, s, f=f: (f // block + i, 0)) for f in firsts
    ]
    operands = [total_weight, rhs, top, weights, *bufs, *after]
    in_specs += [ANY] * len(after)
    aliases = {}
    if combined is not None:
        in_specs.append(ANY)
        operands.append(combined)
        aliases = {len(operands): 0}
    got = pl.pallas_call(
        functools.partial(product_kernel, len(bufs), n_col, start == 0),
        grid_spec=pltpu.PrefetchScalarGridSpec(
            num_scalar_prefetch=1,
            grid=(size // block,),
            in_specs=in_specs,
            out_specs=[pl.BlockSpec((block, sides), at)]
            + [pl.BlockSpec((block, sides), lambda i, s: (i, 0))] * (n_col - 1),
        ),
        out_shape=[jax.ShapeDtypeStruct(rhs.shape, F32)]
        + [jax.ShapeDtypeStruct((size, sides), F32)] * (n_col - 1),
        input_output_aliases=aliases,
        compiler_params=pltpu.CompilerParams(vmem_limit_bytes=VMEM_LIMIT),
        cost_estimate=COST,
        name="products",
    )(scalars, *operands)
    return got[0], [to_col(q, k + 1) for k, q in enumerate(got[1:])]


def finish_kernel(n_other, first, scalars, total_weight, rhs, top, *refs):
    products, out = refs[:n_other], refs[-1]
    phase = pl.program_id(0)
    n_col = n_other + 1
    part = lax.rem(scalars[0] - phase - 1 + n_col, n_col)
    for k in range(n_other):

        @pl.when(phase == k)
        def _(k=k):
            subtract(
                scalars, total_weight, rhs, products[k][...], top, out, first, part, pl.program_id(1)
            )


def finish_call(common, products, start, size, part, combined):
    scalars, total_weight, rhs, top = common
    n_other = len(products)
    n_col = n_other + 1
    sides = rhs.shape[1]
    block = block_rows(size, start, part)
    steps = size // block
    at = lambda k, j, s: (
        (lax.rem(s[0] - k - 1 + n_col, n_col) * (part // block) + start // block + j),
        0,
    )

    def held(phase):
        return lambda k, j, s: (
            jnp.where(k == phase, j, jnp.where(k < phase, 0, steps - 1)),
            0,
        )

    rhs_spec = pl.BlockSpec((block, sides), at)
    in_specs = [
        pl.BlockSpec(memory_space=pltpu.SMEM),
        rhs_spec,
        pl.BlockSpec(top.shape, lambda k, j, s: (0, 0)),
    ]
    in_specs += [pl.BlockSpec((block, sides), held(k)) for k in range(n_other)] + [ANY]
    operands = [total_weight, rhs, top, *products, combined]
    return pl.pallas_call(
        functools.partial(finish_kernel, n_other, start == 0),
        grid_spec=pltpu.PrefetchScalarGridSpec(
            num_scalar_prefetch=1,
            grid=(n_other, steps),
            in_specs=in_specs,
            out_specs=rhs_spec,
        ),
        out_shape=jax.ShapeDtypeStruct(rhs.shape, F32),
        input_output_aliases={len(operands): 0},
        compiler_params=pltpu.CompilerParams(vmem_limit_bytes=VMEM_LIMIT),
        cost_estimate=COST,
        name="finish",
    )(scalars, *operands)


def to_col(x, k):
    n = lax.axis_size("col")
    return x if k == 0 else lax.ppermute(x, "col", [(i, (i + k) % n) for i in range(n)])


def body(panel_column, trailing, right_side, term_weights):
    column = panel_column[0]
    rows, width = column.shape
    n_term, n_row, n_col = (lax.axis_size(a) for a in ("term", "row", "col"))
    t, r, c = (lax.axis_index(a) for a in ("term", "row", "col"))
    window = trailing.shape[2]
    sides = right_side.shape[1]
    per_row = window * n_col // n_row
    part = rows // n_col
    sizes, pieces = chunk_sizes(part, width)
    starts = [sum(sizes[:i]) for i in range(len(sizes))]
    scalars = jnp.stack([c, (r == 0).astype(jnp.int32)]).astype(jnp.int32)
    slots = slot_terms(t, n_term)

    mine = [lax.dynamic_slice_in_dim(column, c * part + o, s, 0) for o, s in zip(starts, sizes)]
    sent = (jnp.concatenate([mine[0], jnp.full((PAD, width), term_weights[0], F32)], axis=0),)
    arrived = [sent]
    for h in range(1, n_term):
        sent = merge_hop(h, send_hop(h, sent, t, n_term), t, n_term)
        arrived.append(sent)
    _, bulk = gate(jnp.zeros((8, LANES), F32), [], mine[1:])
    gathered = [lax.all_gather(m, "term", axis=0, tiled=True) for m in bulk]

    tops = right_side[:width]
    n_side = sides // LANES
    packed = [column[width : width + per_row]] + [
        tops[:, i * LANES : (i + 1) * LANES] for i in range(n_side)
    ]
    packed = lax.all_gather(jnp.concatenate(packed, axis=0), "row", axis=0)
    window_rows = packed[:, :per_row].reshape(n_row * per_row, width)
    window_rows = lax.dynamic_slice_in_dim(window_rows, c * window, window, 0)
    right_top = jnp.concatenate(
        [packed[0, per_row + i * width : per_row + (i + 1) * width] for i in range(n_side)], axis=1
    )
    right_tops = jnp.concatenate(
        [to_col(right_top, n_col - k if k else 0) for k in range(n_col)], axis=1
    )

    heads = [arrived[0][0]]
    for s in range(1, n_term):
        heads.append(
            sum(
                jnp.where((source == s) & valid, arrived[h][place], 0.0)
                for h, place, source, valid in slots
            )
        )
    weights = jnp.stack([h[sizes[0], 0] for h in heads])
    total_weight = jnp.sum(weights)[None]
    corners = jnp.concatenate([h[:width] for h in heads], axis=0)
    others = lax.ppermute(corners, "col", [(0, 1)]) if n_col == 2 else lax.all_gather(corners, "col")[0]
    corners = jnp.where(c == 0, corners, others)
    corner = corners[:width]
    for s in range(1, n_term):
        got = lax.ppermute(corners[s * width : (s + 1) * width], "row", [(0, s)])
        corner = jnp.where(r == s, got, corner)
    lower = jnp.linalg.cholesky(corner)
    inverse = lax.linalg.triangular_solve(
        lower, jnp.eye(width, dtype=F32), left_side=True, lower=True
    )
    inverses = lax.all_gather(inverse, "row", axis=0)[:n_term]

    inverse_t = inverses[0].T
    picked_t = dot(window_rows, inverse_t).T
    factor, updated = factor_call(scalars[1:], column, trailing[0], inverse_t, picked_t, lower)

    solved = [weights[s] * dot(inverses[s], right_tops) for s in range(n_term)]
    top = sum(solved)[:, :sides]
    tall = jnp.concatenate([dot(inverses[s].T, solved[s]) for s in range(n_term)], axis=0)

    def stack(x):
        high = lax.reduce_precision(x, 8, 7)
        high, low = high.astype(BF16), (x - high).astype(BF16)
        return jnp.concatenate([high, high, low], axis=0)

    near = stack(tall)
    by_term = stack(
        lax.dynamic_slice_in_dim(
            jnp.concatenate([tall, tall], axis=0), (n_term - t) * width, n_term * width, 0
        )
    )

    common = (scalars, total_weight, right_side, top)
    combined = None
    for i, (start, size) in enumerate(zip(starts, sizes)):
        step = size // pieces[i]
        waiting = []
        for o in range(0, size, step):
            if i == 0:
                bufs, firsts, tall = heads, [0] * n_term, near
            else:
                bufs, tall = [gathered[i - 1]] * n_term, by_term
                firsts = [size * s + o for s in range(n_term)]
            after = [factor] if i and o == 0 else []
            combined, products = product_call(
                common, bufs, firsts, tall, start + o, step, part, n_col, combined, after
            )
            waiting.append((products, start + o))
            if len(waiting) == 2:
                combined = finish_call(common, *waiting.pop(0), step, part, combined)
        for products, begin in waiting:
            combined = finish_call(common, products, begin, step, part, combined)
    return (factor[None], updated[None], combined)


def solution(mesh):
    placed = (P("term", "row", None), P("term", "row", "col"), P("row", "col"), P("term"))
    return jax.shard_map(
        body,
        mesh=mesh,
        in_specs=placed,
        out_specs=(P("term", "row", None), P("term", "row", "col"), P("row", "col")),
        check_vma=False,
    )
```

time: 369 us -> 266 us (0.72)
  starting transfers between devices: 60.7 us -> 18.4 us
  waiting for transfers between devices: 120 us -> 81.7 us
  local copies, waits for them, and re-layouts: 34.2 us -> 16.9 us
  between operations: 4.03 us -> 17 us
  Pallas kernels: 83.9 us -> 77.3 us
  other arithmetic: 33.4 us -> 28 us
  matrix products: 11.4 us -> 6.19 us
    ppermute x25 -> x5, waiting for transfers between devices: 119 us -> 45.1 us  [the longest x2 21.6 us: send_hop(): lax.ppermute(mine[-1], 'term', to_left)]
    ppermute x25 -> x5, starting transfers between devices: 48.2 us -> 9.47 us  [the longest x2 5.61 us: send_hop(): lax.ppermute(mine[0], 'term', to_right)]
    all_gather x0 -> x2, waiting for transfers between devices: none -> 32.8 us  [body(): gathered = [lax.all_gather(m, 'term', axis=0, tiled=True) for m in bulk]]
    unnamed x106 -> x21, local copies, waits for them, and re-layouts: 20.6 us -> 5.33 us
    pallas_call x10 -> x11, Pallas kernels: 60.4 us -> 52.3 us  [the longest x5 33 us: product_call(): pl.pallas_call(functools.partial(product_kernel, len(bufs), n_col, start...]
    select_n x6 -> x1, other arithmetic: 5.76 us -> 0.04 us  [merge_hop(): return (jnp.where(t >= h, got[0], got[1]),)]
    dot_general x9, matrix products: 11.1 us -> 5.93 us  [dot(): return jnp.dot(left, right, precision=HIGH, preferred_element_type=F32)]
  transfers between devices with their start and end apart: 40 -> 17, of which waited for: 7 -> 8; matrix products, arithmetic and copies ran while one was open for 16% -> 15% of each run, Pallas kernels for 22% -> 23%
where the time goes in v2:
time: 266 us; the launch traced here: 265 us
  waiting for transfers between devices  81.7 us (31%)
  Pallas kernels  77.3 us (29%)
  other arithmetic  28 us (11%)
  blocking collectives  19.5 us (7%)
  starting transfers between devices  18.4 us (7%)
  between operations  17 us (6%)
  local copies, waits for them, and re-layouts  16.9 us (6%)
  matrix products  6.19 us (2%)
    pallas_call x5, Pallas kernels, product_call(): pl.pallas_call(functools.partial(product_kernel, len(bufs), n_col, start...  33 us
    all_gather x2, waiting for transfers between devices, body(): gathered = [lax.all_gather(m, 'term', axis=0, tiled=True) for m in bulk]  32.8 us
    pallas_call x1, Pallas kernels, factor_call(): pl.pallas_call(functools.partial(factor_kernel, width), grid_spec=pltpu.P...  25 us
    ppermute x2, waiting for transfers between devices, send_hop(): lax.ppermute(mine[-1], 'term', to_left)  21.6 us
    pallas_call x5, Pallas kernels, finish_call(): pl.pallas_call(functools.partial(finish_kernel, n_other, start == 0), gri...  19.3 us
    ppermute x1, waiting for transfers between devices, send_hop(): return (lax.ppermute(mine[0], 'term', to_right + to_left),)  19.2 us
    another operation x3, other arithmetic, body(): lower = jnp.linalg.cholesky(corner)  12.4 us
    another operation x2, other arithmetic, body(): lax.linalg.triangular_solve(lower, jnp.eye(width, dtype=F32), left_side=T...  11.1 us
  transfers between devices with their start and end apart: 17, of which 8 were waited for; matrix products, arithmetic and copies ran while one was open for 15% of the time, Pallas kernels for 23%

profile of v2, /device:TPU:0, one launch (start us, length us, event | category | flops | bytes accessed | tf_op | source)
XLA Modules:
  0.0 265.0 jit_solution(16905606883286565817)
XLA Ops:
  7.2 3.2 %dynamic-slice_bitcast_fusion.refs_1_ = f32[4608,128]{1,0:T(8,128)} fusion(f32[1,12288,128]{2,1,0:T(8,128)} %param.4, s32[]{:T(128)S(6)} %select_n.137), kind=kLoop, calls=%fused_computation | loop fusion | bytes 4718596 | tf_op jit(solution)/shard_map/dynamic_slice | solution.py:263
  10.4 1.9 dynamic-slice_bitcast_fusion.1.refs_2_
  12.3 0.6 broadcast_in_dim.34.refs_0_
  13.6 1.0 dynamic-slice_bitcast_fusion.2
  14.6 4.9 %collective-permute-start.1 = (f32[520,128]{1,0:T(8,128)S(1)}, f32[520,128]{1,0:T(8,128)S(1)}, u32[]{:S(2)}, u32[]{:S(2)}) collective-permute-start(f32[520,128]{1,0:T(8,128)S(1)} %concatenate.29.refs_0_), channel_id=1, source_target_pairs={{0,8},{8,16},{16,24},{1,9},{9,17},{17,25},{2,10},{10,18},{18,26},{... | collective-permute-start | bytes 798728 | tf_op jit(solution)/shard_map/ppermute | solution.py:42
  19.6 1.3 collective-permute-start
  20.9 4.3 %collective-permute-done.1 = f32[520,128]{1,0:T(8,128)S(1)} collective-permute-done((f32[520,128]{1,0:T(8,128)S(1)}, f32[520,128]{1,0:T(8,128)S(1)}, u32[]{:S(2)}, u32[]{:S(2)}) %collective-permute-start.1) | collective-permute-done | bytes 266272 | tf_op jit(solution)/shard_map/ppermute | solution.py:42
  25.2 0.7 collective-permute-start.2
  25.8 5.9 %collective-permute-done = f32[520,128]{1,0:T(8,128)S(1)} collective-permute-done((f32[520,128]{1,0:T(8,128)S(1)}, f32[520,128]{1,0:T(8,128)S(1)}, u32[]{:S(2)}, u32[]{:S(2)}) %collective-permute-start) | collective-permute-done | bytes 266272 | tf_op jit(solution)/shard_map/ppermute | solution.py:42
  31.8 1.3 collective-permute-start.3
  33.1 0.8 slice_bitcast_fusion.3
  33.8 0.9 fusion.36
  34.7 15.7 %collective-permute-done.3 = f32[520,128]{1,0:T(8,128)S(1)} collective-permute-done((f32[520,128]{1,0:T(8,128)S(1)}, f32[520,128]{1,0:T(8,128)S(1)}, u32[]{:S(2)}, u32[]{:S(2)}) %collective-permute-start.3) | collective-permute-done | bytes 266272 | tf_op jit(solution)/shard_map/ppermute | solution.py:42
  50.4 1.3 collective-permute-start.4
  51.7 0.9 dynamic-slice_bitcast_fusion.3
  52.6 10.8 %all-gather.1 = f32[1280,128]{1,0:T(8,128)S(1)} all-gather(f32[320,128]{1,0:T(8,128)S(1)} %pad_maximum_fusion.5), channel_id=3, replica_groups=mesh['term'=4,'row'=4,'col'=2] {'row'}, dimensions={0}, use_global_device_ids=true | all-gather | bytes 819200 | tf_op jit(solution)/shard_map/all_gather | solution.py:277
  63.4 19.2 %collective-permute-done.4 = f32[520,128]{1,0:T(8,128)S(1)} collective-permute-done((f32[520,128]{1,0:T(8,128)S(1)}, f32[520,128]{1,0:T(8,128)S(1)}, u32[]{:S(2)}, u32[]{:S(2)}) %collective-permute-start.4) | collective-permute-done | bytes 266272 | tf_op jit(solution)/shard_map/ppermute | solution.py:41
  82.8 1.3 collective-permute-start.5
  84.2 1.0 collective-permute-done.5
  85.3 4.3 %collective-permute-start.6 = (f32[128,128]{1,0:T(8,128)S(1)}, f32[128,128]{1,0:T(8,128)S(1)}, u32[]{:S(2)}, u32[]{:S(2)}) collective-permute-start(f32[128,128]{1,0:T(8,128)S(1)} %get-tuple-element.46), channel_id=1, source_target_pairs={{0,6},{1,7},{8,14},{9,15},{16,22},{17,23},{24,30},{25,31}} | collective-permute-start | bytes 196616 | tf_op jit(solution)/shard_map/ppermute | solution.py:302
  89.6 1.3 collective-permute-start.7
  90.9 1.3 collective-permute-start.8
  92.2 0.6 pad_add_fusion.scalars
  92.8 0.6 slice.128
  93.4 0.6 slice.129
  94.0 0.5 slice.130
  96.6 11.7 %cholesky.17 = f32[128,128]{1,0:T(8,128)S(1)} custom-call(f32[128,128]{1,0:T(8,128)S(1)} %fusion.6), custom_call_target="Cholesky" | custom-call | tf_op jit(solution)/shard_map/jit(cholesky)/cholesky | solution.py:304
  108.3 0.6 compare_reduce_fusion
  108.9 1.3 select_bitcast_fusion
  110.2 9.8 %custom-call.6 = f32[1,128,128]{1,2,0:T(8,128)S(1)} custom-call(f32[1,128,128]{2,1,0:T(8,128)S(1)} %get-tuple-element.31), custom_call_target="InvertDiagBlocksLowerTriangular" | custom-call | tf_op jit(solution)/shard_map/triangular_solve | solution.py:305
  120.3 8.7 %all-gather = f32[512,128]{0,1:T(8,128)S(1)} all-gather(f32[128,128]{0,1:T(8,128)S(1)} %fusion.4), channel_id=2, replica_groups=mesh['term'=4,'row'=4,'col'=2] {'row'}, dimensions={0}, use_global_device_ids=true | all-gather | bytes 327680 | tf_op jit(solution)/shard_map/all_gather | solution.py:308
  129.0 1.0 broadcast_multiply_fusion.2
  130.0 1.1 broadcast_multiply_fusion.1
  131.1 1.1 broadcast_multiply_fusion
  132.1 0.4 convolution_multiply_fusion
  132.6 0.4 constant_dynamic-update-slice_fusion.7
  132.9 0.4 constant_dynamic-update-slice_fusion.6
  133.3 0.4 constant_dynamic-update-slice_fusion.5
  133.7 0.4 constant_dynamic-update-slice_fusion.4
  134.2 0.7 slice_add_fusion.top
  134.9 1.3 pad_maximum_fusion.1.weights
  136.2 4.7 %products.5 = (f32[12288,256]{1,0:T(8,128)}, f32[512,256]{1,0:T(8,128)}) custom-call(s32[2]{0:T(128)} %pad_add_fusion.scalars, f32[1]{0:T(128)} %bitcast.19.total_weight, f32[12288,256]{1,0:T(8,128)} %rhs.21, f32[128,256]{1,0:T(8,128)} %slice_add_fusion.top, bf16[1536,512]{1,0:T(8,128)(2,1)} %pad_maximum_fusion.1.weights, f32[520,128]{1,0:T(8,128)} %copy-done.6, ...), custom_call_target="tpu_custom_call" | custom-call | flops 1 | bytes 1 | tf_op jit(solution)/shard_map/products/pallas_call | solution.py:169
  140.9 0.6 slice_bitcast_fusion.2.inverse_t
  141.5 0.9 fusion.7.picked_t
  142.4 25.0 %factor_update.1 = (f32[12288,128]{1,0:T(8,128)}, f32[12288,128]{1,0:T(8,128)}) custom-call(s32[1]{0:T(128)} %bitcast.flag, f32[12288,128]{1,0:T(8,128)} %bitcast.46, f32[12288,128]{1,0:T(8,128)} %bitcast.47, f32[128,128]{1,0:T(8,128)} %slice_bitcast_fusion.2.inverse_t, f32[128,128]{1,0:T(8,128)} %fusion.7.picked_t, f32[128,128]{1,0:T(8,128)} %get-tuple-element.32.lower), custom_call_target="tpu_custom_call" | custom-call | flops 1 | bytes 1 | tf_op jit(solution)/shard_map/factor_update/pallas_call | solution.py:98
  167.7 1.4 pad_maximum_fusion.weights
  169.0 0.8 copy-done.8
  169.8 2.8 %finish.5.refs_5_ = f32[12288,256]{1,0:T(8,128)} custom-call(s32[2]{0:T(128)} %pad_add_fusion.scalars, f32[1]{0:T(128)} %bitcast.19.total_weight, f32[12288,256]{1,0:T(8,128)} %rhs.21, f32[128,256]{1,0:T(8,128)} %slice_add_fusion.top, f32[512,256]{1,0:T(8,128)} %copy-done.8, f32[12288,256]{1,0:T(8,128)} %get-tuple-element.22.refs_1_), custom_call_target="tpu_custom_call", output_to_operand_aliasing={{}: (5, {})} | custom-call | flops 1 | bytes 1 | tf_op jit(solution)/shard_map/finish/pallas_call | solution.py:228
  172.6 20.1 %all-gather.7.cloned.1.call-done.refs_0_.refs_1_.refs_2_.refs_3_ = f32[18432,128]{1,0:T(8,128)} async-done(((f32[4608,128]{1,0:T(8,128)}), f32[18432,128]{1,0:T(8,128)}) %all-gather.7.cloned.1.call-update) | async-done | bytes 9437200 | tf_op jit(solution)/shard_map/all_gather | solution.py:270
  192.8 7.5 %products.6 = (f32[12288,256]{1,0:T(8,128)}, f32[1536,256]{1,0:T(8,128)}) custom-call(s32[2]{0:T(128)} %pad_add_fusion.scalars, f32[1]{0:T(128)} %bitcast.19.total_weight, f32[12288,256]{1,0:T(8,128)} %rhs.21, f32[128,256]{1,0:T(8,128)} %slice_add_fusion.top, bf16[1536,512]{1,0:T(8,128)(2,1)} %pad_maximum_fusion.weights, ...), custom_call_target="tpu_custom_call", output_to_operand_aliasing={{0}: (10, {})} | custom-call | flops 1 | bytes 1 | tf_op jit(solution)/shard_map/products/pallas_call | solution.py:169
  200.3 7.5 %products.7 = (f32[12288,256]{1,0:T(8,128)}, f32[1536,256]{1,0:T(8,128)}) custom-call(s32[2]{0:T(128)} %pad_add_fusion.scalars, f32[1]{0:T(128)} %bitcast.19.total_weight, f32[12288,256]{1,0:T(8,128)} %rhs.21, f32[128,256]{1,0:T(8,128)} %slice_add_fusion.top, bf16[1536,512]{1,0:T(8,128)(2,1)} %pad_maximum_fusion.weights, ...), custom_call_target="tpu_custom_call", output_to_operand_aliasing={{0}: (9, {})} | custom-call | flops 1 | bytes 1 | tf_op jit(solution)/shard_map/products/pallas_call | solution.py:169
  207.8 0.5 collective-permute-start.13
  208.3 1.1 copy-done
  209.5 4.5 %finish.6.refs_4_ = f32[12288,256]{1,0:T(8,128)} custom-call(s32[2]{0:T(128)} %pad_add_fusion.scalars, f32[1]{0:T(128)} %bitcast.19.total_weight, f32[12288,256]{1,0:T(8,128)} %rhs.21, f32[128,256]{1,0:T(8,128)} %slice_add_fusion.top, f32[1536,256]{1,0:T(8,128)} %copy-done, f32[12288,256]{1,0:T(8,128)} %get-tuple-element.25.refs_1_), custom_call_target="tpu_custom_call", output_to_operand_aliasing={{}: (5, {})} | custom-call | flops 1 | bytes 1 | tf_op jit(solution)/shard_map/finish/pallas_call | solution.py:228
  213.9 7.5 %products.8 = (f32[12288,256]{1,0:T(8,128)}, f32[1536,256]{1,0:T(8,128)}) custom-call(s32[2]{0:T(128)} %pad_add_fusion.scalars, f32[1]{0:T(128)} %bitcast.19.total_weight, f32[12288,256]{1,0:T(8,128)} %rhs.21, f32[128,256]{1,0:T(8,128)} %slice_add_fusion.top, bf16[1536,512]{1,0:T(8,128)(2,1)} %pad_maximum_fusion.weights, ...), custom_call_target="tpu_custom_call", output_to_operand_aliasing={{0}: (9, {})} | custom-call | flops 1 | bytes 1 | tf_op jit(solution)/shard_map/products/pallas_call | solution.py:169
  221.5 1.1 copy-done.1
  222.6 4.5 %finish.7.refs_1_ = f32[12288,256]{1,0:T(8,128)} custom-call(s32[2]{0:T(128)} %pad_add_fusion.scalars, f32[1]{0:T(128)} %bitcast.19.total_weight, f32[12288,256]{1,0:T(8,128)} %rhs.21, f32[128,256]{1,0:T(8,128)} %slice_add_fusion.top, f32[1536,256]{1,0:T(8,128)} %copy-done.1, f32[12288,256]{1,0:T(8,128)} %get-tuple-element.28.refs_1_), custom_call_target="tpu_custom_call", output_to_operand_aliasing={{}: (5, {})} | custom-call | flops 1 | bytes 1 | tf_op jit(solution)/shard_map/finish/pallas_call | solution.py:228
  227.1 1.2 copy-done.2
  228.3 4.5 %finish.8.refs_5_ = f32[12288,256]{1,0:T(8,128)} custom-call(s32[2]{0:T(128)} %pad_add_fusion.scalars, f32[1]{0:T(128)} %bitcast.19.total_weight, f32[12288,256]{1,0:T(8,128)} %rhs.21, f32[128,256]{1,0:T(8,128)} %slice_add_fusion.top, f32[1536,256]{1,0:T(8,128)} %copy-done.2, f32[12288,256]{1,0:T(8,128)} %finish.7.refs_1_), custom_call_target="tpu_custom_call", output_to_operand_aliasing={{}: (5, {})} | custom-call | flops 1 | bytes 1 | tf_op jit(solution)/shard_map/finish/pallas_call | solution.py:228
  232.8 12.6 %all-gather.5.cloned.1.call-done.refs_0_.refs_1_.refs_2_.refs_3_ = f32[4096,128]{1,0:T(8,128)} async-done(((f32[1024,128]{1,0:T(8,128)}), f32[4096,128]{1,0:T(8,128)}) %all-gather.5.cloned.1.call-update) | async-done | bytes 2097168 | tf_op jit(solution)/shard_map/all_gather | solution.py:270
  245.4 5.8 %products.9 = (f32[12288,256]{1,0:T(8,128)}, f32[1024,256]{1,0:T(8,128)}) custom-call(s32[2]{0:T(128)} %pad_add_fusion.scalars, f32[1]{0:T(128)} %bitcast.19.total_weight, f32[12288,256]{1,0:T(8,128)} %rhs.21, f32[128,256]{1,0:T(8,128)} %slice_add_fusion.top, bf16[1536,512]{1,0:T(8,128)(2,1)} %pad_maximum_fusion.weights, ...), custom_call_target="tpu_custom_call", output_to_operand_aliasing={{0}: (10, {})} | custom-call | flops 1 | bytes 1 | tf_op jit(solution)/shard_map/products/pallas_call | solution.py:169
  251.2 2.9 %collective-permute-done.14.refs_0_ = f32[1024,256]{1,0:T(8,128)S(1)} collective-permute-done((f32[1024,256]{1,0:T(8,128)}, f32[1024,256]{1,0:T(8,128)S(1)}, u32[]{:S(2)}, u32[]{:S(2)}) %collective-permute-start.14) | collective-permute-done | bytes 1048608 | tf_op jit(solution)/shard_map/ppermute | solution.py:246
  254.1 1.0 copy-done.7
  255.1 3.1 %finish.9 = f32[12288,256]{1,0:T(8,128)} custom-call(s32[2]{0:T(128)} %pad_add_fusion.scalars, f32[1]{0:T(128)} %bitcast.19.total_weight, f32[12288,256]{1,0:T(8,128)} %rhs.21, f32[128,256]{1,0:T(8,128)} %slice_add_fusion.top, f32[1024,256]{1,0:T(8,128)} %copy-done.7, f32[12288,256]{1,0:T(8,128)} %get-tuple-element.30.refs_1_), custom_call_target="tpu_custom_call", output_to_operand_aliasing={{}: (5, {})} | custom-call | flops 1 | bytes 1 | tf_op jit(solution)/shard_map/finish/pallas_call | solution.py:228
  (56 shorter events, 1.4 us)
Async XLA Ops:
  7.2 185.6 %all-gather.7.cloned.1.call-start = ((), (), s32[]{:S(2)}) async-start(), calls=%async_computation.1 | async-start | bytes 11796480 | tf_op jit(solution)/shard_map/all_gather | solution.py:270
  12.9 232.5 %all-gather.5.cloned.1.call-start = ((), (), s32[]{:S(2)}) async-start(), calls=%async_computation | async-start | bytes 2621440 | tf_op jit(solution)/shard_map/all_gather | solution.py:270
  14.6 68.1 %copy-start.6 = (f32[520,128]{1,0:T(8,128)}, f32[520,128]{1,0:T(8,128)S(1)}, u32[]{:S(2)}) copy-start(f32[520,128]{1,0:T(8,128)S(1)} %concatenate.29.refs_0_) | copy-start | bytes 798724
  14.6 10.6 %collective-permute-start.1 = (f32[520,128]{1,0:T(8,128)S(1)}, f32[520,128]{1,0:T(8,128)S(1)}, u32[]{:S(2)}, u32[]{:S(2)}) collective-permute-start(f32[520,128]{1,0:T(8,128)S(1)} %concatenate.29.refs_0_), channel_id=1, source_target_pairs={{0,8},{8,16},{16,24},{1,9},{9,17},{17,25},{2,10},{10,18},{18,26},{... | collective-permute-start | bytes 798728 | tf_op jit(solution)/shard_map/ppermute | solution.py:42
  19.6 12.2 %collective-permute-start = (f32[520,128]{1,0:T(8,128)S(1)}, f32[520,128]{1,0:T(8,128)S(1)}, u32[]{:S(2)}, u32[]{:S(2)}) collective-permute-start(f32[520,128]{1,0:T(8,128)S(1)} %concatenate.29.refs_0_), channel_id=1, source_target_pairs={{8,0},{16,8},{24,16},{9,1},{17,9},{25,17},{10,2},{18,10},{26,18},{... | collective-permute-start | bytes 798728 | tf_op jit(solution)/shard_map/ppermute | solution.py:42
  25.2 9.5 %collective-permute-start.2 = (f32[520,128]{1,0:T(8,128)S(1)}, f32[520,128]{1,0:T(8,128)S(1)}, u32[]{:S(2)}, u32[]{:S(2)}) collective-permute-start(f32[520,128]{1,0:T(8,128)S(1)} %collective-permute-done.1), channel_id=1, source_target_pairs={{8,16},{16,24},{9,17},{17,25},{10,18},{18,26},{11,19},{19,27},{12,... | collective-permute-start | bytes 798728 | tf_op jit(solution)/shard_map/ppermute | solution.py:42
  31.8 18.6 %collective-permute-start.3 = (f32[520,128]{1,0:T(8,128)S(1)}, f32[520,128]{1,0:T(8,128)S(1)}, u32[]{:S(2)}, u32[]{:S(2)}) collective-permute-start(f32[520,128]{1,0:T(8,128)S(1)} %collective-permute-done), channel_id=1, source_target_pairs={{8,0},{16,8},{9,1},{17,9},{10,2},{18,10},{11,3},{19,11},{12,4},{20... | collective-permute-start | bytes 798728 | tf_op jit(solution)/shard_map/ppermute | solution.py:42
  50.4 32.2 %collective-permute-start.4 = (f32[520,128]{1,0:T(8,128)S(1)}, f32[520,128]{1,0:T(8,128)S(1)}, u32[]{:S(2)}, u32[]{:S(2)}) collective-permute-start(f32[520,128]{1,0:T(8,128)S(1)} %broadcast_select_fusion), channel_id=1, source_target_pairs={{16,24},{8,0},{17,25},{9,1},{18,26},{10,2},{19,27},{11,3},{20,28},... | collective-permute-start | bytes 798728 | tf_op jit(solution)/shard_map/ppermute | solution.py:41
  82.7 46.3 %copy-start.3 = (f32[520,128]{1,0:T(8,128)}, f32[520,128]{1,0:T(8,128)S(1)}, u32[]{:S(2)}) copy-start(f32[520,128]{1,0:T(8,128)S(1)} %get-tuple-element.41.refs_1_) | copy-start | bytes 798724
  82.7 46.3 %copy-start.4 = (f32[520,128]{1,0:T(8,128)}, f32[520,128]{1,0:T(8,128)S(1)}, u32[]{:S(2)}) copy-start(f32[520,128]{1,0:T(8,128)S(1)} %get-tuple-element.42.refs_3_) | copy-start | bytes 798724
  82.7 46.3 %copy-start.5 = (f32[520,128]{1,0:T(8,128)}, f32[520,128]{1,0:T(8,128)S(1)}, u32[]{:S(2)}) copy-start(f32[520,128]{1,0:T(8,128)S(1)} %get-tuple-element.43.refs_2_) | copy-start | bytes 798724
  82.8 2.4 collective-permute-start.5
  84.1 44.8 %collective-permute-start.9 = (f32[128,256]{1,0:T(8,128)S(1)}, f32[128,256]{1,0:T(8,128)S(1)}, u32[]{:S(2)}, u32[]{:S(2)}) collective-permute-start(f32[128,256]{1,0:T(8,128)S(1)} %pad_maximum_fusion.6), channel_id=1, source_target_pairs={{0,1},{1,0},{2,3},{3,2},{4,5},{5,4},{6,7},{7,6},{8,9},{9,8},{10,11... | collective-permute-start | bytes 393224 | tf_op jit(solution)/shard_map/ppermute | solution.py:246
  85.3 11.1 %collective-permute-start.6 = (f32[128,128]{1,0:T(8,128)S(1)}, f32[128,128]{1,0:T(8,128)S(1)}, u32[]{:S(2)}, u32[]{:S(2)}) collective-permute-start(f32[128,128]{1,0:T(8,128)S(1)} %get-tuple-element.46), channel_id=1, source_target_pairs={{0,6},{1,7},{8,14},{9,15},{16,22},{17,23},{24,30},{25,31}} | collective-permute-start | bytes 196616 | tf_op jit(solution)/shard_map/ppermute | solution.py:302
  89.6 6.8 %collective-permute-start.7 = (f32[128,128]{1,0:T(8,128)S(1)}, f32[128,128]{1,0:T(8,128)S(1)}, u32[]{:S(2)}, u32[]{:S(2)}) collective-permute-start(f32[128,128]{1,0:T(8,128)S(1)} %get-tuple-element.45), channel_id=1, source_target_pairs={{0,4},{1,5},{8,12},{9,13},{16,20},{17,21},{24,28},{25,29}} | collective-permute-start | bytes 196616 | tf_op jit(solution)/shard_map/ppermute | solution.py:302
  90.9 5.5 %collective-permute-start.8 = (f32[128,128]{1,0:T(8,128)S(1)}, f32[128,128]{1,0:T(8,128)S(1)}, u32[]{:S(2)}, u32[]{:S(2)}) collective-permute-start(f32[128,128]{1,0:T(8,128)S(1)} %get-tuple-element.44), channel_id=1, source_target_pairs={{0,2},{1,3},{8,10},{9,11},{16,18},{17,19},{24,26},{25,27}} | collective-permute-start | bytes 196616 | tf_op jit(solution)/shard_map/ppermute | solution.py:302
  140.9 28.1 %collective-permute-start.10 = (f32[512,256]{1,0:T(8,128)}, f32[512,256]{1,0:T(8,128)S(1)}, u32[]{:S(2)}, u32[]{:S(2)}) collective-permute-start(f32[512,256]{1,0:T(8,128)} %get-tuple-element.21), channel_id=1, source_target_pairs={{0,1},{1,0},{2,3},{3,2},{4,5},{5,4},{6,7},{7,6},{8,9},{9,8},{10,11... | collective-permute-start | bytes 1572872 | tf_op jit(solution)/shard_map/ppermute | solution.py:246
  169.0 0.8 copy-start.8
  200.2 8.1 %collective-permute-start.11 = (f32[1536,256]{1,0:T(8,128)}, f32[1536,256]{1,0:T(8,128)S(1)}, u32[]{:S(2)}, u32[]{:S(2)}) collective-permute-start(f32[1536,256]{1,0:T(8,128)} %get-tuple-element.23), channel_id=1, source_target_pairs={{0,1},{1,0},{2,3},{3,2},{4,5},{5,4},{6,7},{7,6},{8,9},{9,8},{10,11... | collective-permute-start | bytes 4718600 | tf_op jit(solution)/shard_map/ppermute | solution.py:246
  207.8 13.6 %collective-permute-start.13 = (f32[1536,256]{1,0:T(8,128)}, f32[1536,256]{1,0:T(8,128)S(1)}, u32[]{:S(2)}, u32[]{:S(2)}) collective-permute-start(f32[1536,256]{1,0:T(8,128)} %get-tuple-element.27), channel_id=1, source_target_pairs={{0,1},{1,0},{2,3},{3,2},{4,5},{5,4},{6,7},{7,6},{8,9},{9,8},{10,11... | collective-permute-start | bytes 4718600 | tf_op jit(solution)/shard_map/ppermute | solution.py:246
  208.3 1.1 copy-start
  221.5 5.6 %collective-permute-start.12 = (f32[1536,256]{1,0:T(8,128)}, f32[1536,256]{1,0:T(8,128)S(1)}, u32[]{:S(2)}, u32[]{:S(2)}) collective-permute-start(f32[1536,256]{1,0:T(8,128)} %get-tuple-element.26), channel_id=1, source_target_pairs={{0,1},{1,0},{2,3},{3,2},{4,5},{5,4},{6,7},{7,6},{8,9},{9,8},{10,11... | collective-permute-start | bytes 4718600 | tf_op jit(solution)/shard_map/ppermute | solution.py:246
  221.5 1.1 copy-start.1
  227.1 1.2 copy-start.2
  251.2 2.9 %collective-permute-start.14 = (f32[1024,256]{1,0:T(8,128)}, f32[1024,256]{1,0:T(8,128)S(1)}, u32[]{:S(2)}, u32[]{:S(2)}) collective-permute-start(f32[1024,256]{1,0:T(8,128)} %get-tuple-element.29), channel_id=1, source_target_pairs={{0,1},{1,0},{2,3},{3,2},{4,5},{5,4},{6,7},{7,6},{8,9},{9,8},{10,11... | collective-permute-start | bytes 3145736 | tf_op jit(solution)/shard_map/ppermute | solution.py:246
  254.1 1.0 copy-start.7
Sparse Core Ops, SparseCore 0:
  13.0 179.6 all-gather.6
  200.4 44.9 all-gather.4

commit v3 on v2

v3 whole, which is shorter than its diff:
```python
import functools
import math

import jax
import jax.numpy as jnp
from jax import lax
from jax.experimental import pallas as pl
from jax.experimental.pallas import tpu as pltpu
from jax.sharding import PartitionSpec as P

HIGH = lax.Precision.HIGHEST
F32 = jnp.float32
BF16 = jnp.bfloat16
LANES = 128
PAD = 8
VMEM_LIMIT = 60 * 1024 * 1024
ANY = pl.BlockSpec(memory_space=pl.ANY)
COST = pl.CostEstimate(flops=1, bytes_accessed=1, transcendentals=0)


def dot(left, right):
    return jnp.dot(left, right, precision=HIGH, preferred_element_type=F32)


def chunk_sizes(part, width):
    unit = part // 12
    if part % 12 == 0 and unit % width == 0:
        return [11 * unit, unit]
    return [part - width, width]


def block_rows(*extents):
    return math.gcd(512, *extents)


def send_hop(h, mine, t, n):
    to_right = [(j, j + 1) for j in range(h - 1, n - 1)]
    to_left = [(j, j - 1) for j in range(1, n - h + 1)]
    if 2 * (h - 1) > n - 1:
        return (lax.ppermute(mine[0], "term", to_right + to_left),)
    return (lax.ppermute(mine[0], "term", to_right), lax.ppermute(mine[-1], "term", to_left))


def merge_hop(h, got, t, n):
    if len(got) == 2 and 2 * h > n - 1:
        return (jnp.where(t >= h, got[0], got[1]),)
    return got


def slot_terms(t, n):
    slots = []
    for h in range(1, n):
        if 2 * h > n - 1:
            slots.append((h, 0, jnp.where(t >= h, n - h, h), (t >= h) | (t < n - h)))
        else:
            slots.append((h, 0, jnp.int32(n - h), t >= h))
            slots.append((h, 1, jnp.int32(h), t < n - h))
    return slots


def gate(token, after, passed):
    def kernel(*refs):
        pass

    first = 1 + len(after)
    outs = [token, *passed]
    got = pl.pallas_call(
        kernel,
        in_specs=[ANY] * (first + len(passed)),
        out_specs=[ANY] * len(outs),
        out_shape=[jax.ShapeDtypeStruct(a.shape, a.dtype) for a in outs],
        input_output_aliases={0: 0} | {first + i: 1 + i for i in range(len(passed))},
        compiler_params=pltpu.CompilerParams(vmem_limit_bytes=VMEM_LIMIT),
        cost_estimate=COST,
        name="gate",
    )(token, *after, *passed)
    return got[0], got[1:]


def factor_kernel(width, flag, panel, trailing, inverse_t, picked_t, lower, factor, updated):
    solved = dot(panel[...], inverse_t[...])
    factor[...] = solved

    @pl.when((pl.program_id(0) == 0) & (flag[0] == 1))
    def _():
        factor[:width] = lower[...]

    updated[...] = trailing[...] - dot(factor[...], picked_t[...])


def factor_call(leading, panel, trailing, inverse_t, picked_t, lower):
    rows, width = panel.shape
    window = trailing.shape[1]
    block = block_rows(rows) * (2 if rows % 1024 == 0 else 1)
    whole = lambda a: pl.BlockSpec(a.shape, lambda i, f: (0, 0))
    tile = lambda n: pl.BlockSpec((block, n), lambda i, f: (i, 0))
    return pl.pallas_call(
        functools.partial(factor_kernel, width),
        grid_spec=pltpu.PrefetchScalarGridSpec(
            num_scalar_prefetch=1,
            grid=(rows // block,),
            in_specs=[tile(width), tile(window), whole(inverse_t), whole(picked_t), whole(lower)],
            out_specs=[tile(width), tile(window)],
        ),
        out_shape=[
            jax.ShapeDtypeStruct((rows, width), F32),
            jax.ShapeDtypeStruct((rows, window), F32),
        ],
        compiler_params=pltpu.CompilerParams(vmem_limit_bytes=VMEM_LIMIT),
        cost_estimate=COST,
        name="factor_update",
    )(leading, panel, trailing, inverse_t, picked_t, lower)


def split(x):
    high = x.astype(BF16)
    return high, (x - high.astype(F32)).astype(BF16)


def terms_kernel(n_terms, first, leading, total_weight, rhs, top, weights, *refs):
    bufs, out = refs[:n_terms], refs[-1]
    high, low = split(jnp.concatenate([b[...] for b in bufs], axis=1))
    stacked = jnp.concatenate([high, low, high], axis=1)
    product = jnp.dot(stacked, weights[...], preferred_element_type=F32)
    out[...] = total_weight[0] * rhs[...] - product
    if first:

        @pl.when((leading[0] == 1) & (pl.program_id(0) == 0) & (pl.program_id(1) == 0))
        def _():
            out[: top.shape[0]] = top[...]


def terms_call(common, gathered, weights, start, size, n_col, part, combined, after):
    leading, total_weight, rhs, top = common
    width, sides = gathered.shape[1], rhs.shape[1]
    n_terms = gathered.shape[0] // (n_col * size)
    block = block_rows(size, start, part)
    steps = size // block
    at = lambda k, j, s: (k * (part // block) + start // block + j, 0)
    in_specs = [
        pl.BlockSpec(memory_space=pltpu.SMEM),
        pl.BlockSpec((block, sides), at),
        pl.BlockSpec(top.shape, lambda k, j, s: (0, 0)),
        pl.BlockSpec(weights.shape, lambda k, j, s: (0, 0)),
    ]
    in_specs += [
        pl.BlockSpec((block, width), lambda k, j, s, i=i: ((i * n_col + k) * steps + j, 0))
        for i in range(n_terms)
    ]
    operands = [total_weight, rhs, top, weights, *[gathered] * n_terms, *after]
    in_specs += [ANY] * len(after)
    aliases = {}
    if combined is not None:
        in_specs.append(ANY)
        operands.append(combined)
        aliases = {len(operands): 0}
    return pl.pallas_call(
        functools.partial(terms_kernel, n_terms, start == 0),
        grid_spec=pltpu.PrefetchScalarGridSpec(
            num_scalar_prefetch=1,
            grid=(n_col, steps),
            in_specs=in_specs,
            out_specs=pl.BlockSpec((block, sides), at),
        ),
        out_shape=jax.ShapeDtypeStruct(rhs.shape, F32),
        input_output_aliases=aliases,
        compiler_params=pltpu.CompilerParams(vmem_limit_bytes=VMEM_LIMIT),
        cost_estimate=COST,
        name="terms",
    )(leading, *operands)


def body(panel_column, trailing, right_side, term_weights):
    column = panel_column[0]
    rows, width = column.shape
    n_term, n_row, n_col = (lax.axis_size(a) for a in ("term", "row", "col"))
    t, r, c = (lax.axis_index(a) for a in ("term", "row", "col"))
    window = trailing.shape[2]
    sides = right_side.shape[1]
    per_row = window * n_col // n_row
    part = rows // n_col
    sizes = chunk_sizes(part, width)
    starts = [sum(sizes[:i]) for i in range(len(sizes))]
    leading = (r == 0).astype(jnp.int32)[None]
    slots = slot_terms(t, n_term)

    mine = [lax.dynamic_slice_in_dim(column, c * part + o, s, 0) for o, s in zip(starts, sizes)]
    _, mine = gate(jnp.zeros((8, LANES), F32), [], mine)
    gathered = [lax.all_gather(m, ("term", "col"), axis=0, tiled=True) for m in mine]

    sent = jnp.concatenate([column[:width], jnp.full((PAD, width), term_weights[0], F32)], axis=0)
    arrived = [(sent,)]
    for h in range(1, n_term):
        arrived.append(merge_hop(h, send_hop(h, arrived[-1], t, n_term), t, n_term))

    tops = right_side[:width]
    n_side = sides // LANES
    packed = [column[width : width + per_row]] + [
        tops[:, i * LANES : (i + 1) * LANES] for i in range(n_side)
    ]
    packed = lax.all_gather(jnp.concatenate(packed, axis=0), "row", axis=0)
    window_rows = packed[:, :per_row].reshape(n_row * per_row, width)
    window_rows = lax.dynamic_slice_in_dim(window_rows, c * window, window, 0)
    right_top = jnp.concatenate(
        [packed[0, per_row + i * width : per_row + (i + 1) * width] for i in range(n_side)], axis=1
    )

    heads = [sent]
    for s in range(1, n_term):
        heads.append(
            sum(
                jnp.where((source == s) & valid, arrived[h][place], 0.0)
                for h, place, source, valid in slots
            )
        )
    weights = jnp.stack([h[width, 0] for h in heads])
    total_weight = jnp.sum(weights)[None]
    corner = heads[0][:width]
    for s in range(1, n_term):
        got = lax.ppermute(heads[s][:width], "row", [(0, s)])
        corner = jnp.where(r == s, got, corner)
    lower = jnp.linalg.cholesky(corner)
    inverse = lax.linalg.triangular_solve(
        lower, jnp.eye(width, dtype=F32), left_side=True, lower=True
    )
    inverses = lax.all_gather(inverse, "row", axis=0)[:n_term]

    inverse_t = inverses[0].T
    picked_t = dot(window_rows, inverse_t).T
    factor, updated = factor_call(leading, column, trailing[0], inverse_t, picked_t, lower)

    solved = [weights[s] * dot(inverses[s], right_top) for s in range(n_term)]
    top = sum(solved)
    tall = jnp.concatenate([dot(inverses[s].T, solved[s]) for s in range(n_term)], axis=0)
    tall = lax.dynamic_slice_in_dim(
        jnp.concatenate([tall, tall], axis=0), (n_term - t) * width, n_term * width, 0
    )
    high = lax.reduce_precision(tall, 8, 7)
    high, low = high.astype(BF16), (tall - high).astype(BF16)
    stacked = jnp.concatenate([high, high, low], axis=0)

    common = (leading, total_weight, right_side, top)
    combined = None
    for i, (start, size) in enumerate(zip(starts, sizes)):
        combined = terms_call(
            common, gathered[i], stacked, start, size, n_col, part, combined, [] if i else [factor]
        )
    return (factor[None], updated[None], combined)


def solution(mesh):
    placed = (P("term", "row", None), P("term", "row", "col"), P("row", "col"), P("term"))
    return jax.shard_map(
        body,
        mesh=mesh,
        in_specs=placed,
        out_specs=(P("term", "row", None), P("term", "row", "col"), P("row", "col")),
        check_vma=False,
    )
```

time: 266 us -> 264 us (level)
  waiting for transfers between devices: 81.7 us -> 111 us
  Pallas kernels: 77.3 us -> 55.4 us
  local copies, waits for them, and re-layouts: 16.9 us -> 9.93 us
  other arithmetic: 28 us -> 24.7 us
    all_gather x2, waiting for transfers between devices: 32.8 us -> 94.5 us  [body(): lax.all_gather(m, ('term', 'col'), axis=0, tiled=True)]
    pallas_call x10 -> x2, Pallas kernels: 52.3 us -> 30.4 us  [terms_call(): pl.pallas_call(functools.partial(terms_kernel, n_terms, start == 0), grid...]
    ppermute x1, waiting for transfers between devices: 19.2 us -> 4.39 us  [send_hop(): return (lax.ppermute(mine[0], 'term', to_right + to_left),)]
    ppermute x2, waiting for transfers between devices: 21.6 us -> 12.5 us  [send_hop(): lax.ppermute(mine[-1], 'term', to_left)]
    unnamed x21 -> x4, local copies, waits for them, and re-layouts: 5.33 us -> 0.12 us
    ppermute x2, waiting for transfers between devices: 4.32 us -> 0.01 us  [send_hop(): lax.ppermute(mine[0], 'term', to_right)]
    ppermute x10 -> x3, waiting for transfers between devices: 3.85 us -> 0.01 us  [body(): got = lax.ppermute(heads[s][:width], 'row', [(0, s)])]
    ppermute x10 -> x3, starting transfers between devices: 8.84 us -> 6.88 us  [body(): got = lax.ppermute(heads[s][:width], 'row', [(0, s)])]
  transfers between devices with their start and end apart: 17 -> 10, of which waited for: 8 -> 5; matrix products, arithmetic and copies ran while one was open for 15% -> 14% of each run, Pallas kernels for 23% -> 20%
where the time goes in v3:
time: 264 us; the launch traced here: 263 us
  waiting for transfers between devices  111 us (42%)
  Pallas kernels  55.4 us (21%)
  other arithmetic  24.7 us (9%)
  blocking collectives  20.3 us (8%)
  between operations  16.9 us (6%)
  starting transfers between devices  16.4 us (6%)
  local copies, waits for them, and re-layouts  9.93 us (4%)
  matrix products  7.75 us (3%)
    all_gather x2, waiting for transfers between devices, body(): lax.all_gather(m, ('term', 'col'), axis=0, tiled=True)  94.5 us
    pallas_call x2, Pallas kernels, terms_call(): pl.pallas_call(functools.partial(terms_kernel, n_terms, start == 0), grid...  30.4 us
    pallas_call x1, Pallas kernels, factor_call(): pl.pallas_call(functools.partial(factor_kernel, width), grid_spec=pltpu.P...  25 us
    ppermute x2, waiting for transfers between devices, send_hop(): lax.ppermute(mine[-1], 'term', to_left)  12.5 us
    another operation x3, other arithmetic, body(): lower = jnp.linalg.cholesky(corner)  12.4 us
    another operation x2, other arithmetic, body(): lax.linalg.triangular_solve(lower, jnp.eye(width, dtype=F32), left_side=T...  11.1 us
    all_gather x1, blocking collectives, body(): packed = lax.all_gather(jnp.concatenate(packed, axis=0), 'row', axis=0)  10.9 us
    all_gather x1, blocking collectives, body(): inverses = lax.all_gather(inverse, 'row', axis=0)[:n_term]  9.48 us
  transfers between devices with their start and end apart: 10, of which 5 were waited for; matrix products, arithmetic and copies ran while one was open for 14% of the time, Pallas kernels for 20%

profile of v3, /device:TPU:0, one launch (start us, length us, event | category | flops | bytes accessed | tf_op | source)
XLA Modules:
  0.0 262.8 jit_solution(3068166905311385074)
XLA Ops:
  7.2 0.0 slice-start
  7.2 0.0 all-gather.7.cloned.1.call-start
  7.2 1.7 dynamic-slice_bitcast_fusion.1.refs_2_
  8.9 3.6 %dynamic-slice_bitcast_fusion.refs_1_ = f32[5632,128]{1,0:T(8,128)} fusion(f32[1,12288,128]{2,1,0:T(8,128)} %param.4, s32[]{:T(128)S(6)} %select_n.123), kind=kLoop, calls=%fused_computation | loop fusion | bytes 5767172 | tf_op jit(solution)/shard_map/dynamic_slice | solution.py:187
  12.5 0.6 broadcast_in_dim.41.refs_0_
  13.1 0.0 all-gather.7.cloned.1.call-update
  13.1 0.0 all-gather.5.cloned.1.call-start
  13.8 0.0 slice-done
  13.8 0.1 copy.15
  13.9 4.9 %collective-permute-start = (f32[136,128]{0,1:T(8,128)S(1)}, f32[136,128]{0,1:T(8,128)S(1)}, u32[]{:S(2)}, u32[]{:S(2)}) collective-permute-start(f32[136,128]{0,1:T(8,128)S(1)} %concatenate.17), channel_id=1, source_target_pairs={{0,8},{8,16},{16,24},{1,9},{9,17},{17,25},{2,10},{10,18},{18,26},{... | collective-permute-start | bytes 208904 | tf_op jit(solution)/shard_map/ppermute | solution.py:41
  18.8 1.3 collective-permute-start.2
  20.1 0.0 all-gather.5.cloned.1.call-update
  20.2 0.9 fusion.33
  21.1 0.8 slice_bitcast_fusion.3
  21.8 0.0 collective-permute-done
  21.8 0.7 collective-permute-start.1
  22.5 3.2 %collective-permute-done.2 = f32[136,128]{0,1:T(8,128)S(1)} collective-permute-done((f32[136,128]{0,1:T(8,128)S(1)}, f32[136,128]{0,1:T(8,128)S(1)}, u32[]{:S(2)}, u32[]{:S(2)}) %collective-permute-start.2) | collective-permute-done | bytes 69664 | tf_op jit(solution)/shard_map/ppermute | solution.py:41
  25.7 1.3 collective-permute-start.3
  27.0 0.0 collective-permute-done.1
  27.0 9.3 %collective-permute-done.3 = f32[136,128]{0,1:T(8,128)S(1)} collective-permute-done((f32[136,128]{0,1:T(8,128)S(1)}, f32[136,128]{0,1:T(8,128)S(1)}, u32[]{:S(2)}, u32[]{:S(2)}) %collective-permute-start.3) | collective-permute-done | bytes 69664 | tf_op jit(solution)/shard_map/ppermute | solution.py:41
  36.3 1.3 collective-permute-start.4
  37.6 10.9 %all-gather.1 = f32[1280,128]{1,0:T(8,128)S(1)} all-gather(f32[320,128]{1,0:T(8,128)S(1)} %pad_maximum_fusion.1), channel_id=3, replica_groups=mesh['term'=4,'row'=4,'col'=2] {'row'}, dimensions={0}, use_global_device_ids=true | all-gather | bytes 819200 | tf_op jit(solution)/shard_map/all_gather | solution.py:201
  48.5 4.4 %collective-permute-done.4 = f32[136,128]{0,1:T(8,128)S(1)} collective-permute-done((f32[136,128]{0,1:T(8,128)S(1)}, f32[136,128]{0,1:T(8,128)S(1)}, u32[]{:S(2)}, u32[]{:S(2)}) %collective-permute-start.4) | collective-permute-done | bytes 69664 | tf_op jit(solution)/shard_map/ppermute | solution.py:40
  53.0 4.3 %collective-permute-start.5 = (f32[128,128]{0,1:T(8,128)S(1)}, f32[128,128]{0,1:T(8,128)S(1)}, u32[]{:S(2)}, u32[]{:S(2)}) collective-permute-start(f32[128,128]{0,1:T(8,128)S(1)} %slice.99), channel_id=1, source_target_pairs={{0,6},{1,7},{8,14},{9,15},{16,22},{17,23},{24,30},{25,31}} | collective-permute-start | bytes 196616 | tf_op jit(solution)/shard_map/ppermute | solution.py:220
  57.3 1.3 collective-permute-start.6
  58.6 1.3 collective-permute-start.7
  59.9 0.5 slice.104
  60.4 0.5 slice.105
  61.0 0.5 slice.106
  63.3 0.0 collective-permute-done.5
  63.3 0.0 collective-permute-done.6
  63.3 0.0 collective-permute-done.7
  63.4 0.1 copy.12
  63.5 11.7 %cholesky.17 = f32[128,128]{1,0:T(8,128)S(1)} custom-call(f32[128,128]{1,0:T(8,128)S(1)} %fusion.9), custom_call_target="Cholesky" | custom-call | tf_op jit(solution)/shard_map/jit(cholesky)/cholesky | solution.py:222
  75.2 0.6 compare_reduce_fusion
  75.9 1.3 select_bitcast_fusion
  77.2 9.8 %custom-call.6 = f32[1,128,128]{1,2,0:T(8,128)S(1)} custom-call(f32[1,128,128]{2,1,0:T(8,128)S(1)} %get-tuple-element.11), custom_call_target="InvertDiagBlocksLowerTriangular" | custom-call | tf_op jit(solution)/shard_map/triangular_solve | solution.py:223
  87.0 0.3 fusion.7
  87.2 9.5 %all-gather = f32[512,128]{0,1:T(8,128)S(1)} all-gather(f32[128,128]{0,1:T(8,128)S(1)} %fusion.7), channel_id=2, replica_groups=mesh['term'=4,'row'=4,'col'=2] {'row'}, dimensions={0}, use_global_device_ids=true | all-gather | bytes 327680 | tf_op jit(solution)/shard_map/all_gather | solution.py:226
  96.7 0.6 slice_bitcast_fusion.2.inverse_t
  97.3 0.9 fusion.13.picked_t
  98.3 25.0 %factor_update.1 = (f32[12288,128]{1,0:T(8,128)}, f32[12288,128]{1,0:T(8,128)}) custom-call(s32[1]{0:T(128)} %bitcast.flag.leading, f32[12288,128]{1,0:T(8,128)} %bitcast.39, f32[12288,128]{1,0:T(8,128)} %bitcast.41, f32[128,128]{1,0:T(8,128)} %slice_bitcast_fusion.2.inverse_t, f32[128,128]{1,0:T(8,128)} %fusion.13.picked_t, f32[128,128]{1,0:T(8,128)} %get-tuple-element.12.lower), custom_call_target="tpu_custom_call" | custom-call | flops 1 | bytes 1 | tf_op jit(solution)/shard_map/factor_update/pallas_call | solution.py:97
  123.2 0.3 fusion.15
  123.5 0.3 fusion.18
  123.8 0.3 fusion.21
  124.2 2.8 %add_add_fusion = (f32[128,256]{1,0:T(8,128)}, f32[128,256]{1,0:T(8,128)S(1)}) fusion(f32[128,256]{1,0:T(8,128)S(1)} %fusion.15, f32[128,256]{1,0:T(8,128)S(1)} %fusion.18, f32[128,256]{1,0:T(8,128)S(1)} %fusion.21, f32[]{:T(128)} %bitcast.16, f32[]{:T(128)} %bitcast.15, f32[]{:T(128)} %bitcast.14, f32[128,128]{1,0:T(8,128)S(1)} %get-tuple-element.18, ...), kind=kOutput, calls=%fused_computation.9 | convolution fusion | flops 50593792 | bytes 851984 | tf_op jit(solution)/shard_map/dot_general | solution.py:22
  127.0 0.3 constant_dynamic-update-slice_fusion.7
  127.2 0.8 constant_dynamic-update-slice_fusion.6
  128.0 0.9 constant_dynamic-update-slice_fusion.5
  129.0 0.9 constant_dynamic-update-slice_fusion.4
  129.9 0.1 reduce-precision_convert_fusion
  130.0 1.0 pad_maximum_fusion.weights
  131.0 91.4 %all-gather.7.cloned.1.call-done.refs_0_.refs_1_.refs_2_.refs_3_ = f32[45056,128]{1,0:T(8,128)} async-done(((f32[5632,128]{1,0:T(8,128)}), f32[45056,128]{1,0:T(8,128)}) %all-gather.7.cloned.1.call-update) | async-done | bytes 23068688 | tf_op jit(solution)/shard_map/all_gather | solution.py:189
  222.4 26.6 %terms.2.refs_4_ = f32[12288,256]{1,0:T(8,128)} custom-call(s32[1]{0:T(128)} %bitcast.flag.leading, f32[1]{0:T(128)} %bitcast.17.total_weight, f32[12288,256]{1,0:T(8,128)} %rhs.4, f32[128,256]{1,0:T(8,128)} %get-tuple-element.22.top, bf16[1536,256]{1,0:T(8,128)(2,1)} %pad_maximum_fusion.weights, ...), custom_call_target="tpu_custom_call" | custom-call | flops 1 | bytes 1 | tf_op jit(solution)/shard_map/terms/pallas_call | solution.py:157
  249.0 3.1 %all-gather.5.cloned.1.call-done.refs_0_.refs_1_.refs_2_.refs_3_ = f32[4096,128]{1,0:T(8,128)} async-done(((f32[512,128]{1,0:T(8,128)}), f32[4096,128]{1,0:T(8,128)}) %all-gather.5.cloned.1.call-update) | async-done | bytes 2097168 | tf_op jit(solution)/shard_map/all_gather | solution.py:189
  252.1 3.9 %terms.3 = f32[12288,256]{1,0:T(8,128)} custom-call(s32[1]{0:T(128)} %bitcast.flag.leading, f32[1]{0:T(128)} %bitcast.17.total_weight, f32[12288,256]{1,0:T(8,128)} %rhs.4, f32[128,256]{1,0:T(8,128)} %get-tuple-element.22.top, bf16[1536,256]{1,0:T(8,128)(2,1)} %pad_maximum_fusion.weights, ...), custom_call_target="tpu_custom_call", output_to_operand_aliasing={{}: (9, {})} | custom-call | flops 1 | bytes 1 | tf_op jit(solution)/shard_map/terms/pallas_call | solution.py:157
  (17 shorter events, 0.2 us)
Async XLA Ops:
  7.2 6.6 %slice-start = ((f32[1,12288,128]{2,1,0:T(8,128)}), f32[1,128,128]{2,1,0:T(8,128)S(1)}, s32[]{:S(2)}) async-start(f32[1,12288,128]{2,1,0:T(8,128)} %param.4), calls=%async_computation.2 | async-start | bytes 131072 | tf_op jit(solution)/shard_map/slice | solution.py:191
  7.2 215.2 %all-gather.7.cloned.1.call-start = ((), (), s32[]{:S(2)}) async-start(), calls=%async_computation.1 | async-start | bytes 25952256 | tf_op jit(solution)/shard_map/all_gather | solution.py:189
  13.1 239.0 %all-gather.5.cloned.1.call-start = ((), (), s32[]{:S(2)}) async-start(), calls=%async_computation | async-start | bytes 2359296 | tf_op jit(solution)/shard_map/all_gather | solution.py:189
  13.9 7.9 %collective-permute-start = (f32[136,128]{0,1:T(8,128)S(1)}, f32[136,128]{0,1:T(8,128)S(1)}, u32[]{:S(2)}, u32[]{:S(2)}) collective-permute-start(f32[136,128]{0,1:T(8,128)S(1)} %concatenate.17), channel_id=1, source_target_pairs={{0,8},{8,16},{16,24},{1,9},{9,17},{17,25},{2,10},{10,18},{18,26},{... | collective-permute-start | bytes 208904 | tf_op jit(solution)/shard_map/ppermute | solution.py:41
  18.8 6.9 %collective-permute-start.2 = (f32[136,128]{0,1:T(8,128)S(1)}, f32[136,128]{0,1:T(8,128)S(1)}, u32[]{:S(2)}, u32[]{:S(2)}) collective-permute-start(f32[136,128]{0,1:T(8,128)S(1)} %concatenate.17), channel_id=1, source_target_pairs={{8,0},{16,8},{24,16},{9,1},{17,9},{25,17},{10,2},{18,10},{26,18},{... | collective-permute-start | bytes 208904 | tf_op jit(solution)/shard_map/ppermute | solution.py:41
  21.8 5.2 %collective-permute-start.1 = (f32[136,128]{0,1:T(8,128)S(1)}, f32[136,128]{0,1:T(8,128)S(1)}, u32[]{:S(2)}, u32[]{:S(2)}) collective-permute-start(f32[136,128]{0,1:T(8,128)S(1)} %collective-permute-done), channel_id=1, source_target_pairs={{8,16},{16,24},{9,17},{17,25},{10,18},{18,26},{11,19},{19,27},{12,... | collective-permute-start | bytes 208904 | tf_op jit(solution)/shard_map/ppermute | solution.py:41
  25.7 10.6 %collective-permute-start.3 = (f32[136,128]{0,1:T(8,128)S(1)}, f32[136,128]{0,1:T(8,128)S(1)}, u32[]{:S(2)}, u32[]{:S(2)}) collective-permute-start(f32[136,128]{0,1:T(8,128)S(1)} %collective-permute-done.2), channel_id=1, source_target_pairs={{8,0},{16,8},{9,1},{17,9},{10,2},{18,10},{11,3},{19,11},{12,4},{20... | collective-permute-start | bytes 208904 | tf_op jit(solution)/shard_map/ppermute | solution.py:41
  36.3 16.6 %collective-permute-start.4 = (f32[136,128]{0,1:T(8,128)S(1)}, f32[136,128]{0,1:T(8,128)S(1)}, u32[]{:S(2)}, u32[]{:S(2)}) collective-permute-start(f32[136,128]{0,1:T(8,128)S(1)} %broadcast_select_fusion), channel_id=1, source_target_pairs={{16,24},{8,0},{17,25},{9,1},{18,26},{10,2},{19,27},{11,3},{20,28},... | collective-permute-start | bytes 208904 | tf_op jit(solution)/shard_map/ppermute | solution.py:40
  53.0 10.4 %collective-permute-start.5 = (f32[128,128]{0,1:T(8,128)S(1)}, f32[128,128]{0,1:T(8,128)S(1)}, u32[]{:S(2)}, u32[]{:S(2)}) collective-permute-start(f32[128,128]{0,1:T(8,128)S(1)} %slice.99), channel_id=1, source_target_pairs={{0,6},{1,7},{8,14},{9,15},{16,22},{17,23},{24,30},{25,31}} | collective-permute-start | bytes 196616 | tf_op jit(solution)/shard_map/ppermute | solution.py:220
  57.3 6.1 %collective-permute-start.6 = (f32[128,128]{0,1:T(8,128)S(1)}, f32[128,128]{0,1:T(8,128)S(1)}, u32[]{:S(2)}, u32[]{:S(2)}) collective-permute-start(f32[128,128]{0,1:T(8,128)S(1)} %slice.100), channel_id=1, source_target_pairs={{0,4},{1,5},{8,12},{9,13},{16,20},{17,21},{24,28},{25,29}} | collective-permute-start | bytes 196616 | tf_op jit(solution)/shard_map/ppermute | solution.py:220
  58.6 4.8 %collective-permute-start.7 = (f32[128,128]{0,1:T(8,128)S(1)}, f32[128,128]{0,1:T(8,128)S(1)}, u32[]{:S(2)}, u32[]{:S(2)}) collective-permute-start(f32[128,128]{0,1:T(8,128)S(1)} %slice.101), channel_id=1, source_target_pairs={{0,2},{1,3},{8,10},{9,11},{16,18},{17,19},{24,26},{25,27}} | collective-permute-start | bytes 196616 | tf_op jit(solution)/shard_map/ppermute | solution.py:220
Sparse Core Ops, SparseCore 0:
  13.2 209.1 all-gather.6
  224.0 28.0 all-gather.4

commit v4 on v3

--- a/solution.py
+++ b/solution.py
@@ -25,8 +25,8 @@
 def chunk_sizes(part, width):
     unit = part // 12
     if part % 12 == 0 and unit % width == 0:
-        return [11 * unit, unit]
-    return [part - width, width]
+        return [8 * unit, unit, 3 * unit]
+    return [part - 2 * width, width, width]
 
 
 def block_rows(*extents):
@@ -170,6 +170,47 @@
     )(leading, *operands)
 
 
+def forwarded_call(common, own, column, bufs, weights, start, size, part, combined):
+    _, total_weight, rhs, top = common
+    width, sides = column.shape[1], rhs.shape[1]
+    block = block_rows(size, start, part)
+    at = lambda j, s: (s[0] * (part // block) + start // block + j, 0)
+    in_specs = [
+        pl.BlockSpec(memory_space=pltpu.SMEM),
+        pl.BlockSpec((block, sides), at),
+        pl.BlockSpec(top.shape, lambda j, s: (0, 0)),
+        pl.BlockSpec(weights.shape, lambda j, s: (0, 0)),
+        pl.BlockSpec((block, width), at),
+    ]
+    in_specs += [pl.BlockSpec((block, width), lambda j, s: (j, 0))] * len(bufs)
+    operands = [total_weight, rhs, top, weights, column, *bufs]
+    aliases = {}
+    if combined is not None:
+        in_specs.append(ANY)
+        operands.append(combined)
+        aliases = {len(operands): 0}
+    return pl.pallas_call(
+        functools.partial(terms_kernel, 1 + len(bufs), False),
+        grid_spec=pltpu.PrefetchScalarGridSpec(
+            num_scalar_prefetch=1,
+            grid=(size // block,),
+            in_specs=in_specs,
+            out_specs=pl.BlockSpec((block, sides), at),
+        ),
+        out_shape=jax.ShapeDtypeStruct(rhs.shape, F32),
+        input_output_aliases=aliases,
+        compiler_params=pltpu.CompilerParams(vmem_limit_bytes=VMEM_LIMIT),
+        cost_estimate=COST,
+        name="forwarded_terms",
+    )(own, *operands)
+
+
+def split_weights(x):
+    high = lax.reduce_precision(x, 8, 7)
+    high, low = high.astype(BF16), (x - high).astype(BF16)
+    return jnp.concatenate([high, high, low], axis=0)
+
+
 def body(panel_column, trailing, right_side, term_weights):
     column = panel_column[0]
     rows, width = column.shape
@@ -185,13 +226,18 @@
     slots = slot_terms(t, n_term)
 
     mine = [lax.dynamic_slice_in_dim(column, c * part + o, s, 0) for o, s in zip(starts, sizes)]
-    _, mine = gate(jnp.zeros((8, LANES), F32), [], mine)
-    gathered = [lax.all_gather(m, ("term", "col"), axis=0, tiled=True) for m in mine]
+    token = jnp.zeros((8, LANES), F32)
+    _, bulk = gate(token, [], mine[:2])
+    gathered = [lax.all_gather(m, ("term", "col"), axis=0, tiled=True) for m in bulk]
 
     sent = jnp.concatenate([column[:width], jnp.full((PAD, width), term_weights[0], F32)], axis=0)
     arrived = [(sent,)]
     for h in range(1, n_term):
         arrived.append(merge_hop(h, send_hop(h, arrived[-1], t, n_term), t, n_term))
+    _, (held,) = gate(token, [arrived[-1][0]], mine[2:])
+    forwarded = [(held,)]
+    for h in range(1, n_term - 1):
+        forwarded.append(merge_hop(h, send_hop(h, forwarded[-1], t, n_term), t, n_term))
 
     tops = right_side[:width]
     n_side = sides // LANES
@@ -229,22 +275,43 @@
     picked_t = dot(window_rows, inverse_t).T
     factor, updated = factor_call(leading, column, trailing[0], inverse_t, picked_t, lower)
 
+    _, last = gate(token, [factor], list(forwarded[-1]))
+    forwarded[-1] = tuple(last)
+    h = n_term - 1
+    forwarded.append(merge_hop(h, send_hop(h, forwarded[-1], t, n_term), t, n_term))
+    forwarded = [forwarded[h][place] for h, place, _, _ in slots]
+
     solved = [weights[s] * dot(inverses[s], right_top) for s in range(n_term)]
     top = sum(solved)
     tall = jnp.concatenate([dot(inverses[s].T, solved[s]) for s in range(n_term)], axis=0)
-    tall = lax.dynamic_slice_in_dim(
-        jnp.concatenate([tall, tall], axis=0), (n_term - t) * width, n_term * width, 0
+    by_term = split_weights(
+        lax.dynamic_slice_in_dim(
+            jnp.concatenate([tall, tall], axis=0), (n_term - t) * width, n_term * width, 0
+        )
     )
-    high = lax.reduce_precision(tall, 8, 7)
-    high, low = high.astype(BF16), (tall - high).astype(BF16)
-    stacked = jnp.concatenate([high, high, low], axis=0)
+    by_hop = [tall[:width]]
+    for _, _, source, valid in slots:
+        picked = lax.dynamic_slice_in_dim(tall, source * width, width, 0)
+        by_hop.append(jnp.where(valid, picked, 0.0))
+    by_hop = split_weights(jnp.concatenate(by_hop, axis=0))
 
     common = (leading, total_weight, right_side, top)
-    combined = None
-    for i, (start, size) in enumerate(zip(starts, sizes)):
-        combined = terms_call(
-            common, gathered[i], stacked, start, size, n_col, part, combined, [] if i else [factor]
+    def of_gather(i, combined, after):
+        return terms_call(
+            common, gathered[i], by_term, starts[i], sizes[i], n_col, part, combined, after
         )
+
+    combined = of_gather(0, None, [factor])
+    _, (passed,) = gate(token, [combined], forwarded[-1:])
+    forwarded[-1] = passed
+    for k in range(n_col):
+        ring = [(i, (i + k) % n_col) for i in range(n_col)]
+        bufs = [lax.ppermute(f, "col", ring) for f in forwarded] if k else forwarded
+        own = lax.rem(c - k + n_col, n_col).astype(jnp.int32)[None]
+        combined = forwarded_call(
+            common, own, column, bufs, by_hop, starts[2], sizes[2], part, combined
+        )
+    combined = of_gather(1, combined, [])
     return (factor[None], updated[None], combined)
 
 

time: 264 us -> 248 us (0.939)
  waiting for transfers between devices: 111 us -> 69.3 us
  local copies, waits for them, and re-layouts: 9.93 us -> 19 us
  starting transfers between devices: 16.4 us -> 24.8 us
  Pallas kernels: 55.4 us -> 60.3 us
  other arithmetic: 24.7 us -> 28.7 us
    all_gather x2, waiting for transfers between devices: 94.5 us -> 11.8 us  [body(): lax.all_gather(m, ('term', 'col'), axis=0, tiled=True)]
    ppermute x2 -> x4, waiting for transfers between devices: 12.5 us -> 57.4 us  [send_hop(): lax.ppermute(mine[-1], 'term', to_left)]
    pallas_call x0 -> x2, Pallas kernels: none -> 11.7 us  [forwarded_call(): pl.pallas_call(functools.partial(terms_kernel, 1 + len(bufs), False), gri...]
    pallas_call x2, Pallas kernels: 30.4 us -> 23.6 us  [terms_call(): pl.pallas_call(functools.partial(terms_kernel, n_terms, start == 0), grid...]
    ppermute x2 -> x4, starting transfers between devices: 5.59 us -> 10.1 us  [send_hop(): lax.ppermute(mine[0], 'term', to_right)]
    ppermute x1 -> x2, waiting for transfers between devices: 4.39 us -> 0.01 us  [send_hop(): return (lax.ppermute(mine[0], 'term', to_right + to_left),)]
    unnamed x4 -> x15, local copies, waits for them, and re-layouts: 0.12 us -> 4.13 us
    ppermute x2 -> x4, starting transfers between devices: 2.57 us -> 5.34 us  [send_hop(): lax.ppermute(mine[-1], 'term', to_left)]
  transfers between devices with their start and end apart: 10 -> 19, of which waited for: 5 -> 4; matrix products, arithmetic and copies ran while one was open for 14% -> 20% of each run, Pallas kernels for 20% -> 23%
where the time goes in v4:
time: 248 us; the launch traced here: 247 us
  waiting for transfers between devices  69.3 us (28%)
  Pallas kernels  60.3 us (24%)
  other arithmetic  28.7 us (12%)
  starting transfers between devices  24.8 us (10%)
  blocking collectives  19.6 us (8%)
  local copies, waits for them, and re-layouts  19 us (8%)
  between operations  17.1 us (7%)
  matrix products  7.96 us (3%)
    ppermute x4, waiting for transfers between devices, send_hop(): lax.ppermute(mine[-1], 'term', to_left)  57.4 us
    pallas_call x1, Pallas kernels, factor_call(): pl.pallas_call(functools.partial(factor_kernel, width), grid_spec=pltpu.P...  25 us
    pallas_call x2, Pallas kernels, terms_call(): pl.pallas_call(functools.partial(terms_kernel, n_terms, start == 0), grid...  23.6 us
    another operation x3, other arithmetic, body(): lower = jnp.linalg.cholesky(corner)  12.4 us
    all_gather x2, waiting for transfers between devices, body(): lax.all_gather(m, ('term', 'col'), axis=0, tiled=True)  11.8 us
    pallas_call x2, Pallas kernels, forwarded_call(): pl.pallas_call(functools.partial(terms_kernel, 1 + len(bufs), False), gri...  11.7 us
    all_gather x1, blocking collectives, body(): packed = lax.all_gather(jnp.concatenate(packed, axis=0), 'row', axis=0)  11.5 us
    another operation x2, other arithmetic, body(): lax.linalg.triangular_solve(lower, jnp.eye(width, dtype=F32), left_side=T...  11.1 us
  transfers between devices with their start and end apart: 19, of which 4 were waited for; matrix products, arithmetic and copies ran while one was open for 20% of the time, Pallas kernels for 23%

profile of v4, /device:TPU:0, one launch (start us, length us, event | category | flops | bytes accessed | tf_op | source)
XLA Modules:
  0.0 246.7 jit_solution(11034785430493924298)
XLA Ops:
  7.2 1.7 dynamic-slice_bitcast_fusion.2.refs_2_
  8.9 3.0 %dynamic-slice_bitcast_fusion.refs_1_ = f32[4096,128]{1,0:T(8,128)} fusion(f32[1,12288,128]{2,1,0:T(8,128)} %param.4, s32[]{:T(128)S(6)} %select_n.164), kind=kLoop, calls=%fused_computation | loop fusion | bytes 4194308 | tf_op jit(solution)/shard_map/dynamic_slice | solution.py:228
  11.9 0.6 broadcast_in_dim.54.clone.refs_0_
  13.3 0.8 slice_bitcast_fusion.2
  14.1 4.9 %collective-permute-start = (f32[136,128]{1,0:T(8,128)S(1)}, f32[136,128]{1,0:T(8,128)S(1)}, u32[]{:S(2)}, u32[]{:S(2)}) collective-permute-start(f32[136,128]{1,0:T(8,128)S(1)} %concatenate.25), channel_id=1, source_target_pairs={{0,8},{8,16},{16,24},{1,9},{9,17},{17,25},{2,10},{10,18},{18,26},{... | collective-permute-start | bytes 208904 | tf_op jit(solution)/shard_map/ppermute | solution.py:41
  19.1 1.3 collective-permute-start.2
  20.4 0.9 fusion.39
  21.3 2.2 dynamic-slice_bitcast_fusion.1.refs_2_
  23.4 0.8 slice_bitcast_fusion.4
  24.2 0.7 collective-permute-start.1
  24.9 0.4 collective-permute-done.2
  25.3 1.3 collective-permute-start.3
  26.6 10.7 %collective-permute-done.3 = f32[136,128]{1,0:T(8,128)S(1)} collective-permute-done((f32[136,128]{1,0:T(8,128)S(1)}, f32[136,128]{1,0:T(8,128)S(1)}, u32[]{:S(2)}, u32[]{:S(2)}) %collective-permute-start.3) | collective-permute-done | bytes 69664 | tf_op jit(solution)/shard_map/ppermute | solution.py:41
  37.3 1.3 collective-permute-start.4
  38.6 11.5 %all-gather.1 = f32[1280,128]{1,0:T(8,128)S(1)} all-gather(f32[320,128]{1,0:T(8,128)S(1)} %pad_maximum_fusion.2), channel_id=3, replica_groups=mesh['term'=4,'row'=4,'col'=2] {'row'}, dimensions={0}, use_global_device_ids=true | all-gather | bytes 819200 | tf_op jit(solution)/shard_map/all_gather | solution.py:247
  50.2 3.4 %collective-permute-start.5 = (f32[128,128]{1,0:T(8,128)S(1)}, f32[128,128]{1,0:T(8,128)S(1)}, u32[]{:S(2)}, u32[]{:S(2)}) collective-permute-start(f32[128,128]{1,0:T(8,128)S(1)} %slice.100), channel_id=1, source_target_pairs={{0,6},{1,7},{8,14},{9,15},{16,22},{17,23},{24,30},{25,31}} | collective-permute-start | bytes 196616 | tf_op jit(solution)/shard_map/ppermute | solution.py:266
  53.6 1.3 collective-permute-start.6
  54.9 1.3 collective-permute-start.7
  56.3 0.6 broadcast_in_dim.54.clone.1.refs_0_
  56.9 0.6 slice.105
  57.4 0.5 slice.106
  58.0 0.6 slice.107
  58.5 3.8 %collective-permute-start.8 = (f32[1536,128]{1,0:T(8,128)}, f32[1536,128]{1,0:T(8,128)S(1)}, u32[]{:S(2)}, u32[]{:S(2)}) collective-permute-start(f32[1536,128]{1,0:T(8,128)} %get-tuple-element.13), channel_id=1, source_target_pairs={{0,8},{8,16},{16,24},{1,9},{9,17},{17,25},{2,10},{10,18},{18,26},{... | collective-permute-start | bytes 2359304 | tf_op jit(solution)/shard_map/ppermute | solution.py:41
  62.3 1.3 collective-permute-start.10
  65.5 0.9 select_select_fusion.1
  66.5 11.7 %cholesky.17 = f32[128,128]{1,0:T(8,128)S(1)} custom-call(f32[128,128]{1,0:T(8,128)S(1)} %fusion.15), custom_call_target="Cholesky" | custom-call | tf_op jit(solution)/shard_map/jit(cholesky)/cholesky | solution.py:268
  78.3 0.6 compare_reduce_fusion
  78.9 1.3 select_bitcast_fusion
  80.2 9.8 %custom-call.6 = f32[1,128,128]{1,2,0:T(8,128)S(1)} custom-call(f32[1,128,128]{2,1,0:T(8,128)S(1)} %get-tuple-element.17), custom_call_target="InvertDiagBlocksLowerTriangular" | custom-call | tf_op jit(solution)/shard_map/triangular_solve | solution.py:269
  90.2 8.1 %all-gather = f32[512,128]{0,1:T(8,128)S(1)} all-gather(f32[128,128]{0,1:T(8,128)S(1)} %fusion.13), channel_id=2, replica_groups=mesh['term'=4,'row'=4,'col'=2] {'row'}, dimensions={0}, use_global_device_ids=true | all-gather | bytes 327680 | tf_op jit(solution)/shard_map/all_gather | solution.py:272
  98.4 0.3 fusion.21
  98.7 0.3 fusion.24
  99.0 0.6 slice_bitcast_fusion.3.inverse_t
  99.6 0.9 fusion.19.picked_t
  100.5 25.0 %factor_update.1 = (f32[12288,128]{1,0:T(8,128)}, f32[12288,128]{1,0:T(8,128)}) custom-call(s32[1]{0:T(128)} %bitcast.flag.leading, f32[12288,128]{1,0:T(8,128)} %bitcast.45, f32[12288,128]{1,0:T(8,128)} %bitcast.49, f32[128,128]{1,0:T(8,128)} %slice_bitcast_fusion.3.inverse_t, f32[128,128]{1,0:T(8,128)} %fusion.19.picked_t, f32[128,128]{1,0:T(8,128)} %get-tuple-element.18.lower), custom_call_target="tpu_custom_call" | custom-call | flops 1 | bytes 1 | tf_op jit(solution)/shard_map/factor_update/pallas_call | solution.py:97
  125.5 0.3 fusion.27
  125.8 2.9 %add_add_fusion = (f32[128,256]{1,0:T(8,128)}, f32[128,256]{1,0:T(8,128)S(1)}) fusion(f32[128,256]{1,0:T(8,128)S(1)} %fusion.21, f32[128,256]{1,0:T(8,128)S(1)} %fusion.24, f32[128,256]{1,0:T(8,128)S(1)} %fusion.27, f32[]{:T(128)} %bitcast.16, f32[]{:T(128)} %bitcast.15, f32[]{:T(128)} %bitcast.14, f32[128,128]{1,0:T(8,128)S(1)} %get-tuple-element.26, ...), kind=kOutput, calls=%fused_computation.27 | convolution fusion | flops 50593792 | bytes 851984 | tf_op jit(solution)/shard_map/dot_general | solution.py:22
  128.7 0.3 constant_dynamic-update-slice_fusion.8
  129.0 0.7 collective-permute-start.12
  129.7 1.5 collective-permute-start.13
  131.2 0.9 select_dynamic-update-slice_fusion.2
  132.1 0.9 select_dynamic-update-slice_fusion.1
  133.1 0.9 select_dynamic-update-slice_fusion
  134.1 1.0 copy-done.4
  135.1 46.3 %collective-permute-done.13 = f32[1536,128]{1,0:T(8,128)S(1)} collective-permute-done((f32[1536,128]{1,0:T(8,128)S(1)}, f32[1536,128]{1,0:T(8,128)S(1)}, u32[]{:S(2)}, u32[]{:S(2)}) %collective-permute-start.13) | collective-permute-done | bytes 786464 | tf_op jit(solution)/shard_map/ppermute | solution.py:41
  181.4 1.0 broadcast_select_fusion.refs_2_
  182.4 0.6 broadcast_in_dim.54.clone.2.refs_0_
  183.0 1.3 collective-permute-start.15
  184.2 0.7 constant_dynamic-update-slice_fusion.3
  184.9 0.7 constant_dynamic-update-slice_fusion.2
  185.6 0.7 constant_dynamic-update-slice_fusion.1
  186.2 0.7 constant_dynamic-update-slice_fusion
  186.9 1.1 reduce-precision_convert_fusion.1
  188.0 1.0 pad_maximum_fusion.1.weights
  189.0 0.5 collective-permute-start.9
  189.6 11.8 %all-gather.7.cloned.1.call-done.refs_0_.refs_1_.refs_2_.refs_3_ = f32[32768,128]{1,0:T(8,128)} async-done(((f32[4096,128]{1,0:T(8,128)}), f32[32768,128]{1,0:T(8,128)}) %all-gather.7.cloned.1.call-update) | async-done | bytes 16777232 | tf_op jit(solution)/shard_map/all_gather | solution.py:231
  201.4 19.7 %terms.2.refs_1_.refs_5_ = f32[12288,256]{1,0:T(8,128)} custom-call(s32[1]{0:T(128)} %bitcast.flag.leading, f32[1]{0:T(128)} %bitcast.17.total_weight, f32[12288,256]{1,0:T(8,128)} %rhs.9, f32[128,256]{1,0:T(8,128)} %get-tuple-element.38.top, bf16[1536,256]{1,0:T(8,128)(2,1)} %pad_maximum_fusion.1.weights, ...), custom_call_target="tpu_custom_call" | custom-call | flops 1 | bytes 1 | tf_op jit(solution)/shard_map/terms/pallas_call | solution.py:157
  221.1 0.6 broadcast_in_dim.54.refs_0_
  221.7 0.3 copy-done
  222.3 1.0 pad_maximum_fusion.weights
  223.3 5.9 %forwarded_terms.2.refs_5_ = f32[12288,256]{1,0:T(8,128)} custom-call(s32[1]{0:T(128)} %bitcast.24.leading, f32[1]{0:T(128)} %bitcast.17.total_weight, f32[12288,256]{1,0:T(8,128)} %rhs.9, f32[128,256]{1,0:T(8,128)} %get-tuple-element.38.top, bf16[1920,256]{1,0:T(8,128)(2,1)} %pad_maximum_fusion.weights, ...), custom_call_target="tpu_custom_call", output_to_operand_aliasing={{}: (10, {})} | custom-call | flops 1 | bytes 1 | tf_op jit(solution)/shard_map/forwarded_terms/pallas_call | solution.py:192
  229.3 0.9 copy-done.3
  230.1 5.9 %forwarded_terms.3.refs_4_ = f32[12288,256]{1,0:T(8,128)} custom-call(s32[1]{0:T(128)} %bitcast.22.leading, f32[1]{0:T(128)} %bitcast.17.total_weight, f32[12288,256]{1,0:T(8,128)} %rhs.9, f32[128,256]{1,0:T(8,128)} %get-tuple-element.38.top, bf16[1920,256]{1,0:T(8,128)(2,1)} %pad_maximum_fusion.weights, ...), custom_call_target="tpu_custom_call", output_to_operand_aliasing={{}: (10, {})} | custom-call | flops 1 | bytes 1 | tf_op jit(solution)/shard_map/forwarded_terms/pallas_call | solution.py:192
  236.0 3.9 %terms.3 = f32[12288,256]{1,0:T(8,128)} custom-call(s32[1]{0:T(128)} %bitcast.flag.leading, f32[1]{0:T(128)} %bitcast.17.total_weight, f32[12288,256]{1,0:T(8,128)} %rhs.9, f32[128,256]{1,0:T(8,128)} %get-tuple-element.38.top, bf16[1536,256]{1,0:T(8,128)(2,1)} %pad_maximum_fusion.1.weights, ...), custom_call_target="tpu_custom_call", output_to_operand_aliasing={{}: (9, {})} | custom-call | flops 1 | bytes 1 | tf_op jit(solution)/shard_map/terms/pallas_call | solution.py:157
  (50 shorter events, 1.1 us)
Async XLA Ops:
  7.2 194.3 %all-gather.7.cloned.1.call-start = ((), (), s32[]{:S(2)}) async-start(), calls=%async_computation.1 | async-start | bytes 18874368 | tf_op jit(solution)/shard_map/all_gather | solution.py:231
  12.6 223.4 %all-gather.5.cloned.1.call-start = ((), (), s32[]{:S(2)}) async-start(), calls=%async_computation | async-start | bytes 2359296 | tf_op jit(solution)/shard_map/all_gather | solution.py:231
  14.1 10.1 %collective-permute-start = (f32[136,128]{1,0:T(8,128)S(1)}, f32[136,128]{1,0:T(8,128)S(1)}, u32[]{:S(2)}, u32[]{:S(2)}) collective-permute-start(f32[136,128]{1,0:T(8,128)S(1)} %concatenate.25), channel_id=1, source_target_pairs={{0,8},{8,16},{16,24},{1,9},{9,17},{17,25},{2,10},{10,18},{18,26},{... | collective-permute-start | bytes 208904 | tf_op jit(solution)/shard_map/ppermute | solution.py:41
  19.1 6.2 %collective-permute-start.2 = (f32[136,128]{1,0:T(8,128)S(1)}, f32[136,128]{1,0:T(8,128)S(1)}, u32[]{:S(2)}, u32[]{:S(2)}) collective-permute-start(f32[136,128]{1,0:T(8,128)S(1)} %concatenate.25), channel_id=1, source_target_pairs={{8,0},{16,8},{24,16},{9,1},{17,9},{25,17},{10,2},{18,10},{26,18},{... | collective-permute-start | bytes 208904 | tf_op jit(solution)/shard_map/ppermute | solution.py:41
  24.2 2.3 collective-permute-start.1
  25.3 12.0 %collective-permute-start.3 = (f32[136,128]{1,0:T(8,128)S(1)}, f32[136,128]{1,0:T(8,128)S(1)}, u32[]{:S(2)}, u32[]{:S(2)}) collective-permute-start(f32[136,128]{1,0:T(8,128)S(1)} %collective-permute-done.2), channel_id=1, source_target_pairs={{8,0},{16,8},{9,1},{17,9},{10,2},{18,10},{11,3},{19,11},{12,4},{20... | collective-permute-start | bytes 208904 | tf_op jit(solution)/shard_map/ppermute | solution.py:41
  37.3 12.8 %collective-permute-start.4 = (f32[136,128]{1,0:T(8,128)S(1)}, f32[136,128]{1,0:T(8,128)S(1)}, u32[]{:S(2)}, u32[]{:S(2)}) collective-permute-start(f32[136,128]{1,0:T(8,128)S(1)} %broadcast_select_fusion.1), channel_id=1, source_target_pairs={{16,24},{8,0},{17,25},{9,1},{18,26},{10,2},{19,27},{11,3},{20,28},... | collective-permute-start | bytes 208904 | tf_op jit(solution)/shard_map/ppermute | solution.py:40
  50.1 6.7 %copy-start.5 = (f32[136,128]{1,0:T(8,128)}, f32[136,128]{1,0:T(8,128)S(1)}, u32[]{:S(2)}) copy-start(f32[136,128]{1,0:T(8,128)S(1)} %collective-permute-done.4.refs_1_) | copy-start | bytes 208900
  50.2 15.3 %collective-permute-start.5 = (f32[128,128]{1,0:T(8,128)S(1)}, f32[128,128]{1,0:T(8,128)S(1)}, u32[]{:S(2)}, u32[]{:S(2)}) collective-permute-start(f32[128,128]{1,0:T(8,128)S(1)} %slice.100), channel_id=1, source_target_pairs={{0,6},{1,7},{8,14},{9,15},{16,22},{17,23},{24,30},{25,31}} | collective-permute-start | bytes 196616 | tf_op jit(solution)/shard_map/ppermute | solution.py:266
  53.6 11.9 %collective-permute-start.6 = (f32[128,128]{1,0:T(8,128)S(1)}, f32[128,128]{1,0:T(8,128)S(1)}, u32[]{:S(2)}, u32[]{:S(2)}) collective-permute-start(f32[128,128]{1,0:T(8,128)S(1)} %slice.101), channel_id=1, source_target_pairs={{0,4},{1,5},{8,12},{9,13},{16,20},{17,21},{24,28},{25,29}} | collective-permute-start | bytes 196616 | tf_op jit(solution)/shard_map/ppermute | solution.py:266
  54.9 10.6 %collective-permute-start.7 = (f32[128,128]{1,0:T(8,128)S(1)}, f32[128,128]{1,0:T(8,128)S(1)}, u32[]{:S(2)}, u32[]{:S(2)}) collective-permute-start(f32[128,128]{1,0:T(8,128)S(1)} %slice.102), channel_id=1, source_target_pairs={{0,2},{1,3},{8,10},{9,11},{16,18},{17,19},{24,26},{25,27}} | collective-permute-start | bytes 196616 | tf_op jit(solution)/shard_map/ppermute | solution.py:266
  58.5 70.5 %collective-permute-start.8 = (f32[1536,128]{1,0:T(8,128)}, f32[1536,128]{1,0:T(8,128)S(1)}, u32[]{:S(2)}, u32[]{:S(2)}) collective-permute-start(f32[1536,128]{1,0:T(8,128)} %get-tuple-element.13), channel_id=1, source_target_pairs={{0,8},{8,16},{16,24},{1,9},{9,17},{17,25},{2,10},{10,18},{18,26},{... | collective-permute-start | bytes 2359304 | tf_op jit(solution)/shard_map/ppermute | solution.py:41
  62.3 67.5 %collective-permute-start.10 = (f32[1536,128]{1,0:T(8,128)}, f32[1536,128]{1,0:T(8,128)S(1)}, u32[]{:S(2)}, u32[]{:S(2)}) collective-permute-start(f32[1536,128]{1,0:T(8,128)} %get-tuple-element.13), channel_id=1, source_target_pairs={{8,0},{16,8},{24,16},{9,1},{17,9},{25,17},{10,2},{18,10},{26,18},{... | collective-permute-start | bytes 2359304 | tf_op jit(solution)/shard_map/ppermute | solution.py:41
  129.0 60.0 %copy-start.1 = (f32[1536,128]{1,0:T(8,128)}, f32[1536,128]{1,0:T(8,128)S(1)}, u32[]{:S(2)}) copy-start(f32[1536,128]{1,0:T(8,128)S(1)} %collective-permute-done.8.refs_1_) | copy-start | bytes 2359300
  129.0 5.1 %collective-permute-start.12 = (f32[1536,128]{1,0:T(8,128)S(1)}, f32[1536,128]{1,0:T(8,128)S(1)}, u32[]{:S(2)}, u32[]{:S(2)}) collective-permute-start(f32[1536,128]{1,0:T(8,128)S(1)} %collective-permute-done.8.refs_1_), channel_id=1, source_target_pairs={{8,16},{16,24},{9,17},{17,25},{10,18},{18,26},{11,19},{19,27},{12,... | collective-permute-start | bytes 2359304 | tf_op jit(solution)/shard_map/ppermute | solution.py:41
  129.7 59.3 %copy-start.2 = (f32[1536,128]{1,0:T(8,128)}, f32[1536,128]{1,0:T(8,128)S(1)}, u32[]{:S(2)}) copy-start(f32[1536,128]{1,0:T(8,128)S(1)} %collective-permute-done.10.refs_2_) | copy-start | bytes 2359300
  129.7 51.6 %collective-permute-start.13 = (f32[1536,128]{1,0:T(8,128)S(1)}, f32[1536,128]{1,0:T(8,128)S(1)}, u32[]{:S(2)}, u32[]{:S(2)}) collective-permute-start(f32[1536,128]{1,0:T(8,128)S(1)} %collective-permute-done.10.refs_2_), channel_id=1, source_target_pairs={{8,0},{16,8},{9,1},{17,9},{10,2},{18,10},{11,3},{19,11},{12,4},{20... | collective-permute-start | bytes 2359304 | tf_op jit(solution)/shard_map/ppermute | solution.py:41
  134.1 1.0 copy-start.4
  183.0 38.2 %collective-permute-start.15 = (f32[1536,128]{1,0:T(8,128)}, f32[1536,128]{1,0:T(8,128)S(1)}, u32[]{:S(2)}, u32[]{:S(2)}) collective-permute-start(f32[1536,128]{1,0:T(8,128)} %get-tuple-element.14.refs_3_), channel_id=1, source_target_pairs={{16,24},{8,0},{17,25},{9,1},{18,26},{10,2},{19,27},{11,3},{20,28},... | collective-permute-start | bytes 2359304 | tf_op jit(solution)/shard_map/ppermute | solution.py:40
  189.0 40.2 %collective-permute-start.11 = (f32[1536,128]{1,0:T(8,128)S(1)}, f32[1536,128]{1,0:T(8,128)}, u32[]{:S(2)}, u32[]{:S(2)}) collective-permute-start(f32[1536,128]{1,0:T(8,128)S(1)} %collective-permute-done.10.refs_2_), channel_id=1, source_target_pairs={{0,1},{1,0},{2,3},{3,2},{4,5},{5,4},{6,7},{7,6},{8,9},{9,8},{10,11... | collective-permute-start | bytes 2359304 | tf_op jit(solution)/shard_map/ppermute | solution.py:309
  189.0 40.2 %collective-permute-start.9 = (f32[1536,128]{1,0:T(8,128)S(1)}, f32[1536,128]{1,0:T(8,128)}, u32[]{:S(2)}, u32[]{:S(2)}) collective-permute-start(f32[1536,128]{1,0:T(8,128)S(1)} %collective-permute-done.8.refs_1_), channel_id=1, source_target_pairs={{0,1},{1,0},{2,3},{3,2},{4,5},{5,4},{6,7},{7,6},{8,9},{9,8},{10,11... | collective-permute-start | bytes 2359304 | tf_op jit(solution)/shard_map/ppermute | solution.py:309
  189.5 39.7 %collective-permute-start.14 = (f32[1536,128]{1,0:T(8,128)}, f32[1536,128]{1,0:T(8,128)}, u32[]{:S(2)}, u32[]{:S(2)}) collective-permute-start(f32[1536,128]{1,0:T(8,128)} %get-tuple-element.14.refs_3_), channel_id=1, source_target_pairs={{0,1},{1,0},{2,3},{3,2},{4,5},{5,4},{6,7},{7,6},{8,9},{9,8},{10,11... | collective-permute-start | bytes 2359304 | tf_op jit(solution)/shard_map/ppermute | solution.py:309
  221.1 0.9 copy-start
  222.0 7.2 %collective-permute-start.16 = (f32[1536,128]{1,0:T(8,128)}, f32[1536,128]{1,0:T(8,128)S(1)}, u32[]{:S(2)}, u32[]{:S(2)}) collective-permute-start(f32[1536,128]{1,0:T(8,128)} %get-tuple-element.16.refs_4_), channel_id=1, source_target_pairs={{0,1},{1,0},{2,3},{3,2},{4,5},{5,4},{6,7},{7,6},{8,9},{9,8},{10,11... | collective-permute-start | bytes 2359304 | tf_op jit(solution)/shard_map/ppermute | solution.py:309
  229.3 0.9 copy-start.3
Sparse Core Ops, SparseCore 0:
  12.7 188.7 all-gather.6
  203.0 31.7 all-gather.4

commit v5 on v4

--- a/solution.py
+++ b/solution.py
@@ -29,8 +29,8 @@
     return [part - 2 * width, width, width]
 
 
-def block_rows(*extents):
-    return math.gcd(512, *extents)
+def block_rows(*extents, most=512):
+    return math.gcd(most, *extents)
 
 
 def send_hop(h, mine, t, n):
@@ -134,7 +134,7 @@
     leading, total_weight, rhs, top = common
     width, sides = gathered.shape[1], rhs.shape[1]
     n_terms = gathered.shape[0] // (n_col * size)
-    block = block_rows(size, start, part)
+    block = block_rows(size, start, part, most=1024 if size > 1024 else 512)
     steps = size // block
     at = lambda k, j, s: (k * (part // block) + start // block + j, 0)
     in_specs = [
@@ -227,14 +227,15 @@
 
     mine = [lax.dynamic_slice_in_dim(column, c * part + o, s, 0) for o, s in zip(starts, sizes)]
     token = jnp.zeros((8, LANES), F32)
-    _, bulk = gate(token, [], mine[:2])
-    gathered = [lax.all_gather(m, ("term", "col"), axis=0, tiled=True) for m in bulk]
+    _, (bulk,) = gate(token, [], mine[:1])
+    gathered = [lax.all_gather(bulk, ("term", "col"), axis=0, tiled=True)]
 
     sent = jnp.concatenate([column[:width], jnp.full((PAD, width), term_weights[0], F32)], axis=0)
     arrived = [(sent,)]
     for h in range(1, n_term):
         arrived.append(merge_hop(h, send_hop(h, arrived[-1], t, n_term), t, n_term))
-    _, (held,) = gate(token, [arrived[-1][0]], mine[2:])
+    _, (small, held) = gate(token, [arrived[-1][0]], mine[1:])
+    gathered.append(lax.all_gather(small, ("term", "col"), axis=0, tiled=True))
     forwarded = [(held,)]
     for h in range(1, n_term - 1):
         forwarded.append(merge_hop(h, send_hop(h, forwarded[-1], t, n_term), t, n_term))

time: 248 us -> 246 us (level)
  waiting for transfers between devices: 69.3 us -> 73.9 us
  Pallas kernels: 60.3 us -> 57 us
  starting transfers between devices: 24.8 us -> 22.2 us
    ppermute x2, waiting for transfers between devices: 0.01 us -> 17.5 us  [send_hop(): return (lax.ppermute(mine[0], 'term', to_right + to_left),)]
    all_gather x2, waiting for transfers between devices: 11.8 us -> 4.47 us  [the longest x1 4.47 us: body(): gathered = [lax.all_gather(bulk, ('term', 'col'), axis=0, tiled=True)]]
    ppermute x4, waiting for transfers between devices: 57.4 us -> 51.9 us  [send_hop(): lax.ppermute(mine[-1], 'term', to_left)]
    pallas_call x2, Pallas kernels: 23.6 us -> 20.2 us  [terms_call(): pl.pallas_call(functools.partial(terms_kernel, n_terms, start == 0), grid...]
  transfers between devices with their start and end apart: 19 -> 19, of which waited for: 4 -> 6; matrix products, arithmetic and copies ran while one was open for 20% -> 20% of each run, Pallas kernels for 23% -> 22%
where the time goes in v5:
time: 246 us; the launch traced here: 245 us
  waiting for transfers between devices  73.9 us (30%)
  Pallas kernels  57 us (23%)
  other arithmetic  28.7 us (12%)
  starting transfers between devices  22.2 us (9%)
  local copies, waits for them, and re-layouts  19.1 us (8%)
  blocking collectives  18.7 us (8%)
  between operations  17.1 us (7%)
  matrix products  7.96 us (3%)
    ppermute x4, waiting for transfers between devices, send_hop(): lax.ppermute(mine[-1], 'term', to_left)  51.9 us
    pallas_call x1, Pallas kernels, factor_call(): pl.pallas_call(functools.partial(factor_kernel, width), grid_spec=pltpu.P...  25 us
    pallas_call x2, Pallas kernels, terms_call(): pl.pallas_call(functools.partial(terms_kernel, n_terms, start == 0), grid...  20.2 us
    ppermute x2, waiting for transfers between devices, send_hop(): return (lax.ppermute(mine[0], 'term', to_right + to_left),)  17.5 us
    another operation x3, other arithmetic, body(): lower = jnp.linalg.cholesky(corner)  12.4 us
    pallas_call x2, Pallas kernels, forwarded_call(): pl.pallas_call(functools.partial(terms_kernel, 1 + len(bufs), False), gri...  11.8 us
    another operation x2, other arithmetic, body(): lax.linalg.triangular_solve(lower, jnp.eye(width, dtype=F32), left_side=T...  11.1 us
    all_gather x1, blocking collectives, body(): packed = lax.all_gather(jnp.concatenate(packed, axis=0), 'row', axis=0)  10.6 us
  transfers between devices with their start and end apart: 19, of which 6 were waited for; matrix products, arithmetic and copies ran while one was open for 20% of the time, Pallas kernels for 22%

profile of v5, /device:TPU:0, one launch (start us, length us, event | category | flops | bytes accessed | tf_op | source)
XLA Modules:
  0.0 244.6 jit_solution(13064231326607457838)
XLA Ops:
  7.2 3.0 %dynamic-slice_bitcast_fusion.refs_1_ = f32[4096,128]{1,0:T(8,128)} fusion(f32[1,12288,128]{2,1,0:T(8,128)} %param.4, s32[]{:T(128)S(6)} %select_n.177), kind=kLoop, calls=%fused_computation | loop fusion | bytes 4194308 | tf_op jit(solution)/shard_map/dynamic_slice | solution.py:228
  10.3 0.6 broadcast_in_dim.54.clone.2.refs_0_
  11.6 0.8 slice_bitcast_fusion.2
  12.4 4.9 %collective-permute-start = (f32[136,128]{1,0:T(8,128)S(1)}, f32[136,128]{1,0:T(8,128)S(1)}, u32[]{:S(2)}, u32[]{:S(2)}) collective-permute-start(f32[136,128]{1,0:T(8,128)S(1)} %concatenate.25), channel_id=1, source_target_pairs={{0,8},{8,16},{16,24},{1,9},{9,17},{17,25},{2,10},{10,18},{18,26},{... | collective-permute-start | bytes 208904 | tf_op jit(solution)/shard_map/ppermute | solution.py:41
  17.4 1.3 collective-permute-start.2
  18.7 0.8 slice_bitcast_fusion.4
  19.4 0.9 fusion.39
  20.4 2.2 dynamic-slice_bitcast_fusion.1.refs_3_
  22.6 0.7 collective-permute-start.1
  23.2 0.3 collective-permute-done.2
  23.6 1.3 collective-permute-start.3
  24.9 10.6 %all-gather.1 = f32[1280,128]{1,0:T(8,128)S(1)} all-gather(f32[320,128]{1,0:T(8,128)S(1)} %pad_maximum_fusion.2), channel_id=3, replica_groups=mesh['term'=4,'row'=4,'col'=2] {'row'}, dimensions={0}, use_global_device_ids=true | all-gather | bytes 819200 | tf_op jit(solution)/shard_map/all_gather | solution.py:248
  35.7 1.3 collective-permute-start.4
  37.1 14.8 %collective-permute-done.4.refs_1_ = f32[136,128]{1,0:T(8,128)S(1)} collective-permute-done((f32[136,128]{1,0:T(8,128)S(1)}, f32[136,128]{1,0:T(8,128)S(1)}, u32[]{:S(2)}, u32[]{:S(2)}) %collective-permute-start.4) | collective-permute-done | bytes 69664 | tf_op jit(solution)/shard_map/ppermute | solution.py:40
  52.0 3.4 %collective-permute-start.5 = (f32[128,128]{1,0:T(8,128)S(1)}, f32[128,128]{1,0:T(8,128)S(1)}, u32[]{:S(2)}, u32[]{:S(2)}) collective-permute-start(f32[128,128]{1,0:T(8,128)S(1)} %slice.100), channel_id=1, source_target_pairs={{0,6},{1,7},{8,14},{9,15},{16,22},{17,23},{24,30},{25,31}} | collective-permute-start | bytes 196616 | tf_op jit(solution)/shard_map/ppermute | solution.py:267
  55.4 1.3 collective-permute-start.6
  56.7 1.3 collective-permute-start.7
  58.0 1.8 dynamic-slice_bitcast_fusion.2.refs_2_
  59.7 0.6 broadcast_in_dim.54.clone.refs_0_
  60.3 0.6 slice.105
  60.9 0.5 slice.106
  61.4 0.6 slice.107
  62.0 1.3 collective-permute-start.8
  63.3 1.3 collective-permute-start.10
  66.6 0.9 select_select_fusion.1
  67.6 11.7 %cholesky.17 = f32[128,128]{1,0:T(8,128)S(1)} custom-call(f32[128,128]{1,0:T(8,128)S(1)} %fusion.15), custom_call_target="Cholesky" | custom-call | tf_op jit(solution)/shard_map/jit(cholesky)/cholesky | solution.py:269
  79.3 0.6 compare_reduce_fusion
  80.0 1.3 select_bitcast_fusion
  81.2 9.8 %custom-call.6 = f32[1,128,128]{1,2,0:T(8,128)S(1)} custom-call(f32[1,128,128]{2,1,0:T(8,128)S(1)} %get-tuple-element.17), custom_call_target="InvertDiagBlocksLowerTriangular" | custom-call | tf_op jit(solution)/shard_map/triangular_solve | solution.py:270
  91.3 8.1 %all-gather = f32[512,128]{0,1:T(8,128)S(1)} all-gather(f32[128,128]{0,1:T(8,128)S(1)} %fusion.13), channel_id=2, replica_groups=mesh['term'=4,'row'=4,'col'=2] {'row'}, dimensions={0}, use_global_device_ids=true | all-gather | bytes 327680 | tf_op jit(solution)/shard_map/all_gather | solution.py:273
  99.4 0.3 fusion.21
  99.7 0.3 fusion.24
  100.0 0.6 slice_bitcast_fusion.3.inverse_t
  100.7 0.9 fusion.19.picked_t
  101.6 25.0 %factor_update.1 = (f32[12288,128]{1,0:T(8,128)}, f32[12288,128]{1,0:T(8,128)}) custom-call(s32[1]{0:T(128)} %bitcast.flag.leading, f32[12288,128]{1,0:T(8,128)} %bitcast.45, f32[12288,128]{1,0:T(8,128)} %bitcast.49, f32[128,128]{1,0:T(8,128)} %slice_bitcast_fusion.3.inverse_t, f32[128,128]{1,0:T(8,128)} %fusion.19.picked_t, f32[128,128]{1,0:T(8,128)} %get-tuple-element.18.lower), custom_call_target="tpu_custom_call" | custom-call | flops 1 | bytes 1 | tf_op jit(solution)/shard_map/factor_update/pallas_call | solution.py:97
  126.6 0.3 fusion.27
  126.9 2.9 %add_add_fusion = (f32[128,256]{1,0:T(8,128)}, f32[128,256]{1,0:T(8,128)S(1)}) fusion(f32[128,256]{1,0:T(8,128)S(1)} %fusion.21, f32[128,256]{1,0:T(8,128)S(1)} %fusion.24, f32[128,256]{1,0:T(8,128)S(1)} %fusion.27, f32[]{:T(128)} %bitcast.16, f32[]{:T(128)} %bitcast.15, f32[]{:T(128)} %bitcast.14, f32[128,128]{1,0:T(8,128)S(1)} %get-tuple-element.26, ...), kind=kOutput, calls=%fused_computation.27 | convolution fusion | flops 50593792 | bytes 851984 | tf_op jit(solution)/shard_map/dot_general | solution.py:22
  129.8 0.3 constant_dynamic-update-slice_fusion.8
  130.1 0.7 collective-permute-start.12
  130.8 1.5 collective-permute-start.13
  132.3 0.9 select_dynamic-update-slice_fusion.2
  133.2 0.9 select_dynamic-update-slice_fusion.1
  134.1 0.9 select_dynamic-update-slice_fusion
  135.2 1.0 copy-done.4
  136.2 51.3 %collective-permute-done.13 = f32[1536,128]{1,0:T(8,128)S(1)} collective-permute-done((f32[1536,128]{1,0:T(8,128)S(1)}, f32[1536,128]{1,0:T(8,128)S(1)}, u32[]{:S(2)}, u32[]{:S(2)}) %collective-permute-start.13) | collective-permute-done | bytes 786464 | tf_op jit(solution)/shard_map/ppermute | solution.py:41
  187.5 1.0 broadcast_select_fusion.refs_2_
  188.4 0.6 broadcast_in_dim.54.clone.1.refs_0_
  189.0 1.3 collective-permute-start.15
  190.3 0.7 constant_dynamic-update-slice_fusion.3
  191.0 0.7 constant_dynamic-update-slice_fusion.2
  191.7 0.7 constant_dynamic-update-slice_fusion.1
  192.3 0.7 constant_dynamic-update-slice_fusion
  193.0 1.1 reduce-precision_convert_fusion.1
  194.1 1.0 pad_maximum_fusion.1.weights
  195.1 0.5 collective-permute-start.9
  195.7 4.5 %all-gather.7.cloned.1.call-done.refs_0_.refs_1_.refs_2_.refs_3_ = f32[32768,128]{1,0:T(8,128)} async-done(((f32[4096,128]{1,0:T(8,128)}), f32[32768,128]{1,0:T(8,128)}) %all-gather.7.cloned.1.call-update) | async-done | bytes 16777232 | tf_op jit(solution)/shard_map/all_gather | solution.py:231
  200.2 16.3 %terms.2.refs_1_.refs_5_ = f32[12288,256]{1,0:T(8,128)} custom-call(s32[1]{0:T(128)} %bitcast.flag.leading, f32[1]{0:T(128)} %bitcast.17.total_weight, f32[12288,256]{1,0:T(8,128)} %rhs.9, f32[128,256]{1,0:T(8,128)} %get-tuple-element.38.top, bf16[1536,256]{1,0:T(8,128)(2,1)} %pad_maximum_fusion.1.weights, ...), custom_call_target="tpu_custom_call" | custom-call | flops 1 | bytes 1 | tf_op jit(solution)/shard_map/terms/pallas_call | solution.py:157
  216.5 2.7 %collective-permute-done.15.refs_2_ = f32[1536,128]{1,0:T(8,128)S(1)} collective-permute-done((f32[1536,128]{1,0:T(8,128)}, f32[1536,128]{1,0:T(8,128)S(1)}, u32[]{:S(2)}, u32[]{:S(2)}) %collective-permute-start.15) | collective-permute-done | bytes 786464 | tf_op jit(solution)/shard_map/ppermute | solution.py:40
  219.2 0.6 broadcast_in_dim.54.refs_0_
  220.2 1.0 pad_maximum_fusion.weights
  221.2 5.9 %forwarded_terms.2.refs_5_ = f32[12288,256]{1,0:T(8,128)} custom-call(s32[1]{0:T(128)} %bitcast.24.leading, f32[1]{0:T(128)} %bitcast.17.total_weight, f32[12288,256]{1,0:T(8,128)} %rhs.9, f32[128,256]{1,0:T(8,128)} %get-tuple-element.38.top, bf16[1920,256]{1,0:T(8,128)(2,1)} %pad_maximum_fusion.weights, ...), custom_call_target="tpu_custom_call", output_to_operand_aliasing={{}: (10, {})} | custom-call | flops 1 | bytes 1 | tf_op jit(solution)/shard_map/forwarded_terms/pallas_call | solution.py:192
  227.2 0.9 copy-done.3
  228.0 5.9 %forwarded_terms.3.refs_4_ = f32[12288,256]{1,0:T(8,128)} custom-call(s32[1]{0:T(128)} %bitcast.22.leading, f32[1]{0:T(128)} %bitcast.17.total_weight, f32[12288,256]{1,0:T(8,128)} %rhs.9, f32[128,256]{1,0:T(8,128)} %get-tuple-element.38.top, bf16[1920,256]{1,0:T(8,128)(2,1)} %pad_maximum_fusion.weights, ...), custom_call_target="tpu_custom_call", output_to_operand_aliasing={{}: (10, {})} | custom-call | flops 1 | bytes 1 | tf_op jit(solution)/shard_map/forwarded_terms/pallas_call | solution.py:192
  233.9 3.9 %terms.3 = f32[12288,256]{1,0:T(8,128)} custom-call(s32[1]{0:T(128)} %bitcast.flag.leading, f32[1]{0:T(128)} %bitcast.17.total_weight, f32[12288,256]{1,0:T(8,128)} %rhs.9, f32[128,256]{1,0:T(8,128)} %get-tuple-element.38.top, bf16[1536,256]{1,0:T(8,128)(2,1)} %pad_maximum_fusion.1.weights, ...), custom_call_target="tpu_custom_call", output_to_operand_aliasing={{}: (9, {})} | custom-call | flops 1 | bytes 1 | tf_op jit(solution)/shard_map/terms/pallas_call | solution.py:157
  (50 shorter events, 1.4 us)
Async XLA Ops:
  7.2 193.0 %all-gather.7.cloned.1.call-start = ((), (), s32[]{:S(2)}) async-start(), calls=%async_computation.1 | async-start | bytes 18874368 | tf_op jit(solution)/shard_map/all_gather | solution.py:231
  10.9 223.0 %all-gather.5.cloned.1.call-start = ((), (), s32[]{:S(2)}) async-start(), calls=%async_computation | async-start | bytes 2359296 | tf_op jit(solution)/shard_map/all_gather | solution.py:238
  12.4 10.1 %collective-permute-start = (f32[136,128]{1,0:T(8,128)S(1)}, f32[136,128]{1,0:T(8,128)S(1)}, u32[]{:S(2)}, u32[]{:S(2)}) collective-permute-start(f32[136,128]{1,0:T(8,128)S(1)} %concatenate.25), channel_id=1, source_target_pairs={{0,8},{8,16},{16,24},{1,9},{9,17},{17,25},{2,10},{10,18},{18,26},{... | collective-permute-start | bytes 208904 | tf_op jit(solution)/shard_map/ppermute | solution.py:41
  17.4 6.2 %collective-permute-start.2 = (f32[136,128]{1,0:T(8,128)S(1)}, f32[136,128]{1,0:T(8,128)S(1)}, u32[]{:S(2)}, u32[]{:S(2)}) collective-permute-start(f32[136,128]{1,0:T(8,128)S(1)} %concatenate.25), channel_id=1, source_target_pairs={{8,0},{16,8},{24,16},{9,1},{17,9},{25,17},{10,2},{18,10},{26,18},{... | collective-permute-start | bytes 208904 | tf_op jit(solution)/shard_map/ppermute | solution.py:41
  22.6 12.9 %collective-permute-start.1 = (f32[136,128]{1,0:T(8,128)S(1)}, f32[136,128]{1,0:T(8,128)S(1)}, u32[]{:S(2)}, u32[]{:S(2)}) collective-permute-start(f32[136,128]{1,0:T(8,128)S(1)} %collective-permute-done), channel_id=1, source_target_pairs={{8,16},{16,24},{9,17},{17,25},{10,18},{18,26},{11,19},{19,27},{12,... | collective-permute-start | bytes 208904 | tf_op jit(solution)/shard_map/ppermute | solution.py:41
  23.6 12.1 %collective-permute-start.3 = (f32[136,128]{1,0:T(8,128)S(1)}, f32[136,128]{1,0:T(8,128)S(1)}, u32[]{:S(2)}, u32[]{:S(2)}) collective-permute-start(f32[136,128]{1,0:T(8,128)S(1)} %collective-permute-done.2), channel_id=1, source_target_pairs={{8,0},{16,8},{9,1},{17,9},{10,2},{18,10},{11,3},{19,11},{12,4},{20... | collective-permute-start | bytes 208904 | tf_op jit(solution)/shard_map/ppermute | solution.py:41
  35.7 16.2 %collective-permute-start.4 = (f32[136,128]{1,0:T(8,128)S(1)}, f32[136,128]{1,0:T(8,128)S(1)}, u32[]{:S(2)}, u32[]{:S(2)}) collective-permute-start(f32[136,128]{1,0:T(8,128)S(1)} %broadcast_select_fusion.1), channel_id=1, source_target_pairs={{16,24},{8,0},{17,25},{9,1},{18,26},{10,2},{19,27},{11,3},{20,28},... | collective-permute-start | bytes 208904 | tf_op jit(solution)/shard_map/ppermute | solution.py:40
  51.9 8.4 %copy-start.5 = (f32[136,128]{1,0:T(8,128)}, f32[136,128]{1,0:T(8,128)S(1)}, u32[]{:S(2)}) copy-start(f32[136,128]{1,0:T(8,128)S(1)} %collective-permute-done.4.refs_1_) | copy-start | bytes 208900
  52.0 14.6 %collective-permute-start.5 = (f32[128,128]{1,0:T(8,128)S(1)}, f32[128,128]{1,0:T(8,128)S(1)}, u32[]{:S(2)}, u32[]{:S(2)}) collective-permute-start(f32[128,128]{1,0:T(8,128)S(1)} %slice.100), channel_id=1, source_target_pairs={{0,6},{1,7},{8,14},{9,15},{16,22},{17,23},{24,30},{25,31}} | collective-permute-start | bytes 196616 | tf_op jit(solution)/shard_map/ppermute | solution.py:267
  55.4 11.2 %collective-permute-start.6 = (f32[128,128]{1,0:T(8,128)S(1)}, f32[128,128]{1,0:T(8,128)S(1)}, u32[]{:S(2)}, u32[]{:S(2)}) collective-permute-start(f32[128,128]{1,0:T(8,128)S(1)} %slice.101), channel_id=1, source_target_pairs={{0,4},{1,5},{8,12},{9,13},{16,20},{17,21},{24,28},{25,29}} | collective-permute-start | bytes 196616 | tf_op jit(solution)/shard_map/ppermute | solution.py:267
  56.7 9.9 %collective-permute-start.7 = (f32[128,128]{1,0:T(8,128)S(1)}, f32[128,128]{1,0:T(8,128)S(1)}, u32[]{:S(2)}, u32[]{:S(2)}) collective-permute-start(f32[128,128]{1,0:T(8,128)S(1)} %slice.102), channel_id=1, source_target_pairs={{0,2},{1,3},{8,10},{9,11},{16,18},{17,19},{24,26},{25,27}} | collective-permute-start | bytes 196616 | tf_op jit(solution)/shard_map/ppermute | solution.py:267
  62.0 68.1 %collective-permute-start.8 = (f32[1536,128]{1,0:T(8,128)}, f32[1536,128]{1,0:T(8,128)S(1)}, u32[]{:S(2)}, u32[]{:S(2)}) collective-permute-start(f32[1536,128]{1,0:T(8,128)} %get-tuple-element.13), channel_id=1, source_target_pairs={{0,8},{8,16},{16,24},{1,9},{9,17},{17,25},{2,10},{10,18},{18,26},{... | collective-permute-start | bytes 2359304 | tf_op jit(solution)/shard_map/ppermute | solution.py:41
  63.3 67.5 %collective-permute-start.10 = (f32[1536,128]{1,0:T(8,128)}, f32[1536,128]{1,0:T(8,128)S(1)}, u32[]{:S(2)}, u32[]{:S(2)}) collective-permute-start(f32[1536,128]{1,0:T(8,128)} %get-tuple-element.13), channel_id=1, source_target_pairs={{8,0},{16,8},{24,16},{9,1},{17,9},{25,17},{10,2},{18,10},{26,18},{... | collective-permute-start | bytes 2359304 | tf_op jit(solution)/shard_map/ppermute | solution.py:41
  130.0 65.1 %copy-start.1 = (f32[1536,128]{1,0:T(8,128)}, f32[1536,128]{1,0:T(8,128)S(1)}, u32[]{:S(2)}) copy-start(f32[1536,128]{1,0:T(8,128)S(1)} %collective-permute-done.8.refs_1_) | copy-start | bytes 2359300
  130.1 5.1 %collective-permute-start.12 = (f32[1536,128]{1,0:T(8,128)S(1)}, f32[1536,128]{1,0:T(8,128)S(1)}, u32[]{:S(2)}, u32[]{:S(2)}) collective-permute-start(f32[1536,128]{1,0:T(8,128)S(1)} %collective-permute-done.8.refs_1_), channel_id=1, source_target_pairs={{8,16},{16,24},{9,17},{17,25},{10,18},{18,26},{11,19},{19,27},{12,... | collective-permute-start | bytes 2359304 | tf_op jit(solution)/shard_map/ppermute | solution.py:41
  130.8 64.3 %copy-start.2 = (f32[1536,128]{1,0:T(8,128)}, f32[1536,128]{1,0:T(8,128)S(1)}, u32[]{:S(2)}) copy-start(f32[1536,128]{1,0:T(8,128)S(1)} %collective-permute-done.10.refs_2_) | copy-start | bytes 2359300
  130.8 56.7 %collective-permute-start.13 = (f32[1536,128]{1,0:T(8,128)S(1)}, f32[1536,128]{1,0:T(8,128)S(1)}, u32[]{:S(2)}, u32[]{:S(2)}) collective-permute-start(f32[1536,128]{1,0:T(8,128)S(1)} %collective-permute-done.10.refs_2_), channel_id=1, source_target_pairs={{8,0},{16,8},{9,1},{17,9},{10,2},{18,10},{11,3},{19,11},{12,4},{20... | collective-permute-start | bytes 2359304 | tf_op jit(solution)/shard_map/ppermute | solution.py:41
  135.1 1.0 copy-start.4
  189.0 30.2 %collective-permute-start.15 = (f32[1536,128]{1,0:T(8,128)}, f32[1536,128]{1,0:T(8,128)S(1)}, u32[]{:S(2)}, u32[]{:S(2)}) collective-permute-start(f32[1536,128]{1,0:T(8,128)} %get-tuple-element.14.refs_3_), channel_id=1, source_target_pairs={{16,24},{8,0},{17,25},{9,1},{18,26},{10,2},{19,27},{11,3},{20,28},... | collective-permute-start | bytes 2359304 | tf_op jit(solution)/shard_map/ppermute | solution.py:40
  195.1 32.0 %collective-permute-start.11 = (f32[1536,128]{1,0:T(8,128)S(1)}, f32[1536,128]{1,0:T(8,128)}, u32[]{:S(2)}, u32[]{:S(2)}) collective-permute-start(f32[1536,128]{1,0:T(8,128)S(1)} %collective-permute-done.10.refs_2_), channel_id=1, source_target_pairs={{0,1},{1,0},{2,3},{3,2},{4,5},{5,4},{6,7},{7,6},{8,9},{9,8},{10,11... | collective-permute-start | bytes 2359304 | tf_op jit(solution)/shard_map/ppermute | solution.py:310
  195.1 32.0 %collective-permute-start.9 = (f32[1536,128]{1,0:T(8,128)S(1)}, f32[1536,128]{1,0:T(8,128)}, u32[]{:S(2)}, u32[]{:S(2)}) collective-permute-start(f32[1536,128]{1,0:T(8,128)S(1)} %collective-permute-done.8.refs_1_), channel_id=1, source_target_pairs={{0,1},{1,0},{2,3},{3,2},{4,5},{5,4},{6,7},{7,6},{8,9},{9,8},{10,11... | collective-permute-start | bytes 2359304 | tf_op jit(solution)/shard_map/ppermute | solution.py:310
  195.6 31.5 %collective-permute-start.14 = (f32[1536,128]{1,0:T(8,128)}, f32[1536,128]{1,0:T(8,128)}, u32[]{:S(2)}, u32[]{:S(2)}) collective-permute-start(f32[1536,128]{1,0:T(8,128)} %get-tuple-element.14.refs_3_), channel_id=1, source_target_pairs={{0,1},{1,0},{2,3},{3,2},{4,5},{5,4},{6,7},{7,6},{8,9},{9,8},{10,11... | collective-permute-start | bytes 2359304 | tf_op jit(solution)/shard_map/ppermute | solution.py:310
  219.2 0.9 copy-start
  220.1 7.0 %collective-permute-start.16 = (f32[1536,128]{1,0:T(8,128)}, f32[1536,128]{1,0:T(8,128)S(1)}, u32[]{:S(2)}, u32[]{:S(2)}) collective-permute-start(f32[1536,128]{1,0:T(8,128)} %get-tuple-element.16.refs_4_), channel_id=1, source_target_pairs={{0,1},{1,0},{2,3},{3,2},{4,5},{5,4},{6,7},{7,6},{8,9},{9,8},{10,11... | collective-permute-start | bytes 2359304 | tf_op jit(solution)/shard_map/ppermute | solution.py:310
  227.1 0.9 copy-start.3
Sparse Core Ops, SparseCore 0:
  11.0 189.1 all-gather.6
  201.8 31.3 all-gather.4

commit v6 on v5

--- a/solution.py
+++ b/solution.py
@@ -78,14 +78,13 @@
 
 
 def factor_kernel(width, flag, panel, trailing, inverse_t, picked_t, lower, factor, updated):
-    solved = dot(panel[...], inverse_t[...])
-    factor[...] = solved
+    both = dot(panel[...], jnp.concatenate([inverse_t[...], picked_t[...]], axis=1))
+    factor[...] = both[:, :width]
+    updated[...] = trailing[...] - both[:, width:]
 
     @pl.when((pl.program_id(0) == 0) & (flag[0] == 1))
     def _():
         factor[:width] = lower[...]
-
-    updated[...] = trailing[...] - dot(factor[...], picked_t[...])
 
 
 def factor_call(leading, panel, trailing, inverse_t, picked_t, lower):
@@ -273,7 +272,7 @@
     inverses = lax.all_gather(inverse, "row", axis=0)[:n_term]
 
     inverse_t = inverses[0].T
-    picked_t = dot(window_rows, inverse_t).T
+    picked_t = dot(inverse_t, dot(window_rows, inverse_t).T)
     factor, updated = factor_call(leading, column, trailing[0], inverse_t, picked_t, lower)
 
     _, last = gate(token, [factor], list(forwarded[-1]))

time: 246 us -> 245 us (level)
  Pallas kernels: 57 us -> 49.4 us
  waiting for transfers between devices: 73.9 us -> 80.7 us
    all_gather x1, waiting for transfers between devices: 4.47 us -> 14.6 us  [body(): gathered = [lax.all_gather(bulk, ('term', 'col'), axis=0, tiled=True)]]
    pallas_call x1, Pallas kernels: 25 us -> 17.4 us  [factor_call(): pl.pallas_call(functools.partial(factor_kernel, width), grid_spec=pltpu.P...]
    ppermute x4, waiting for transfers between devices: 51.9 us -> 48.7 us  [send_hop(): lax.ppermute(mine[-1], 'term', to_left)]
    dot_general x9 -> x10, matrix products: 7.71 us -> 7.9 us  [dot(): return jnp.dot(left, right, precision=HIGH, preferred_element_type=F32)]
  transfers between devices with their start and end apart: 19 -> 19, of which waited for: 6 -> 6; matrix products, arithmetic and copies ran while one was open for 20% -> 21% of each run, Pallas kernels for 22% -> 19%
where the time goes in v6:
time: 245 us; the launch traced here: 244 us
  waiting for transfers between devices  80.7 us (33%)
  Pallas kernels  49.4 us (20%)
  other arithmetic  28.7 us (12%)
  starting transfers between devices  22.2 us (9%)
  local copies, waits for them, and re-layouts  19.1 us (8%)
  blocking collectives  18.7 us (8%)
  between operations  17.1 us (7%)
  matrix products  8.15 us (3%)
    ppermute x4, waiting for transfers between devices, send_hop(): lax.ppermute(mine[-1], 'term', to_left)  48.7 us
    pallas_call x2, Pallas kernels, terms_call(): pl.pallas_call(functools.partial(terms_kernel, n_terms, start == 0), grid...  20.2 us
    pallas_call x1, Pallas kernels, factor_call(): pl.pallas_call(functools.partial(factor_kernel, width), grid_spec=pltpu.P...  17.4 us
    ppermute x2, waiting for transfers between devices, send_hop(): return (lax.ppermute(mine[0], 'term', to_right + to_left),)  17.3 us
    all_gather x1, waiting for transfers between devices, body(): gathered = [lax.all_gather(bulk, ('term', 'col'), axis=0, tiled=True)]  14.6 us
    another operation x3, other arithmetic, body(): lower = jnp.linalg.cholesky(corner)  12.4 us
    pallas_call x2, Pallas kernels, forwarded_call(): pl.pallas_call(functools.partial(terms_kernel, 1 + len(bufs), False), gri...  11.7 us
    another operation x2, other arithmetic, body(): lax.linalg.triangular_solve(lower, jnp.eye(width, dtype=F32), left_side=T...  11.1 us
  transfers between devices with their start and end apart: 19, of which 6 were waited for; matrix products, arithmetic and copies ran while one was open for 21% of the time, Pallas kernels for 19%

profile of v6, /device:TPU:0, one launch (start us, length us, event | category | flops | bytes accessed | tf_op | source)
XLA Modules:
  0.0 244.0 jit_solution(1874571561694879582)
XLA Ops:
  7.2 3.0 %dynamic-slice_bitcast_fusion.refs_1_ = f32[4096,128]{1,0:T(8,128)} fusion(f32[1,12288,128]{2,1,0:T(8,128)} %param.4, s32[]{:T(128)S(6)} %select_n.177), kind=kLoop, calls=%fused_computation | loop fusion | bytes 4194308 | tf_op jit(solution)/shard_map/dynamic_slice | solution.py:227
  10.3 0.6 broadcast_in_dim.54.clone.2.refs_0_
  11.6 0.8 slice_bitcast_fusion.2
  12.4 4.9 %collective-permute-start = (f32[136,128]{1,0:T(8,128)S(1)}, f32[136,128]{1,0:T(8,128)S(1)}, u32[]{:S(2)}, u32[]{:S(2)}) collective-permute-start(f32[136,128]{1,0:T(8,128)S(1)} %concatenate.25), channel_id=1, source_target_pairs={{0,8},{8,16},{16,24},{1,9},{9,17},{17,25},{2,10},{10,18},{18,26},{... | collective-permute-start | bytes 208904 | tf_op jit(solution)/shard_map/ppermute | solution.py:41
  17.4 1.3 collective-permute-start.2
  18.7 0.8 slice_bitcast_fusion.4
  19.4 0.9 fusion.41
  20.4 2.2 dynamic-slice_bitcast_fusion.1.refs_3_
  22.6 0.7 collective-permute-start.1
  23.2 0.3 collective-permute-done.2
  23.6 1.3 collective-permute-start.3
  24.9 10.6 %all-gather.1 = f32[1280,128]{1,0:T(8,128)S(1)} all-gather(f32[320,128]{1,0:T(8,128)S(1)} %pad_maximum_fusion.2), channel_id=3, replica_groups=mesh['term'=4,'row'=4,'col'=2] {'row'}, dimensions={0}, use_global_device_ids=true | all-gather | bytes 819200 | tf_op jit(solution)/shard_map/all_gather | solution.py:247
  35.7 1.3 collective-permute-start.4
  37.1 14.8 %collective-permute-done.4.refs_1_ = f32[136,128]{1,0:T(8,128)S(1)} collective-permute-done((f32[136,128]{1,0:T(8,128)S(1)}, f32[136,128]{1,0:T(8,128)S(1)}, u32[]{:S(2)}, u32[]{:S(2)}) %collective-permute-start.4) | collective-permute-done | bytes 69664 | tf_op jit(solution)/shard_map/ppermute | solution.py:40
  52.0 3.4 %collective-permute-start.5 = (f32[128,128]{1,0:T(8,128)S(1)}, f32[128,128]{1,0:T(8,128)S(1)}, u32[]{:S(2)}, u32[]{:S(2)}) collective-permute-start(f32[128,128]{1,0:T(8,128)S(1)} %slice.100), channel_id=1, source_target_pairs={{0,6},{1,7},{8,14},{9,15},{16,22},{17,23},{24,30},{25,31}} | collective-permute-start | bytes 196616 | tf_op jit(solution)/shard_map/ppermute | solution.py:266
  55.4 1.3 collective-permute-start.6
  56.7 1.3 collective-permute-start.7
  58.0 1.8 dynamic-slice_bitcast_fusion.2.refs_2_
  59.7 0.6 broadcast_in_dim.54.clone.refs_0_
  60.3 0.6 slice.105
  60.9 0.5 slice.106
  61.4 0.6 slice.107
  62.0 1.3 collective-permute-start.8
  63.3 1.3 collective-permute-start.10
  66.6 0.9 select_select_fusion.1
  67.6 11.7 %cholesky.17 = f32[128,128]{1,0:T(8,128)S(1)} custom-call(f32[128,128]{1,0:T(8,128)S(1)} %fusion.15), custom_call_target="Cholesky" | custom-call | tf_op jit(solution)/shard_map/jit(cholesky)/cholesky | solution.py:268
  79.3 0.6 compare_reduce_fusion
  80.0 1.3 select_bitcast_fusion
  81.2 9.8 %custom-call.6 = f32[1,128,128]{1,2,0:T(8,128)S(1)} custom-call(f32[1,128,128]{2,1,0:T(8,128)S(1)} %get-tuple-element.17), custom_call_target="InvertDiagBlocksLowerTriangular" | custom-call | tf_op jit(solution)/shard_map/triangular_solve | solution.py:269
  91.3 8.1 %all-gather = f32[512,128]{0,1:T(8,128)S(1)} all-gather(f32[128,128]{0,1:T(8,128)S(1)} %fusion.13), channel_id=2, replica_groups=mesh['term'=4,'row'=4,'col'=2] {'row'}, dimensions={0}, use_global_device_ids=true | all-gather | bytes 327680 | tf_op jit(solution)/shard_map/all_gather | solution.py:272
  99.4 0.3 fusion.21
  99.7 0.3 fusion.24
  100.3 0.9 fusion.31.picked_t
  101.2 0.6 slice_bitcast_fusion.3.inverse_t
  101.8 17.4 %factor_update.1 = (f32[12288,128]{1,0:T(8,128)}, f32[12288,128]{1,0:T(8,128)}) custom-call(s32[1]{0:T(128)} %bitcast.flag.leading, f32[12288,128]{1,0:T(8,128)} %bitcast.46, f32[12288,128]{1,0:T(8,128)} %bitcast.50, f32[128,128]{1,0:T(8,128)} %slice_bitcast_fusion.3.inverse_t, f32[128,128]{1,0:T(8,128)} %fusion.31.picked_t, f32[128,128]{1,0:T(8,128)} %get-tuple-element.18.lower), custom_call_target="tpu_custom_call" | custom-call | flops 1 | bytes 1 | tf_op jit(solution)/shard_map/factor_update/pallas_call | solution.py:96
  119.2 0.3 fusion.27
  119.5 2.9 %add_add_fusion = (f32[128,256]{1,0:T(8,128)}, f32[128,256]{1,0:T(8,128)S(1)}) fusion(f32[128,256]{1,0:T(8,128)S(1)} %fusion.21, f32[128,256]{1,0:T(8,128)S(1)} %fusion.24, f32[128,256]{1,0:T(8,128)S(1)} %fusion.27, f32[]{:T(128)} %bitcast.16, f32[]{:T(128)} %bitcast.15, f32[]{:T(128)} %bitcast.14, f32[128,128]{1,0:T(8,128)S(1)} %get-tuple-element.26, ...), kind=kOutput, calls=%fused_computation.27 | convolution fusion | flops 50593792 | bytes 851984 | tf_op jit(solution)/shard_map/dot_general | solution.py:22
  122.4 0.3 constant_dynamic-update-slice_fusion.8
  122.7 0.7 collective-permute-start.12
  123.5 1.3 collective-permute-start.13
  124.8 0.9 select_dynamic-update-slice_fusion.2
  125.7 0.9 select_dynamic-update-slice_fusion.1
  126.6 0.9 select_dynamic-update-slice_fusion
  127.6 1.0 copy-done.4
  128.6 48.1 %collective-permute-done.13 = f32[1536,128]{1,0:T(8,128)S(1)} collective-permute-done((f32[1536,128]{1,0:T(8,128)S(1)}, f32[1536,128]{1,0:T(8,128)S(1)}, u32[]{:S(2)}, u32[]{:S(2)}) %collective-permute-start.13) | collective-permute-done | bytes 786464 | tf_op jit(solution)/shard_map/ppermute | solution.py:41
  176.7 1.0 broadcast_select_fusion.refs_2_
  177.7 0.6 broadcast_in_dim.54.clone.1.refs_0_
  178.3 1.5 collective-permute-start.15
  179.8 0.7 constant_dynamic-update-slice_fusion.3
  180.5 0.7 constant_dynamic-update-slice_fusion.2
  181.1 0.7 constant_dynamic-update-slice_fusion.1
  181.8 0.7 constant_dynamic-update-slice_fusion
  182.4 1.1 reduce-precision_convert_fusion.1
  183.6 1.0 pad_maximum_fusion.1.weights
  184.6 0.5 collective-permute-start.9
  185.1 14.6 %all-gather.7.cloned.1.call-done.refs_0_.refs_1_.refs_2_.refs_3_ = f32[32768,128]{1,0:T(8,128)} async-done(((f32[4096,128]{1,0:T(8,128)}), f32[32768,128]{1,0:T(8,128)}) %all-gather.7.cloned.1.call-update) | async-done | bytes 16777232 | tf_op jit(solution)/shard_map/all_gather | solution.py:230
  199.7 16.3 %terms.2.refs_1_.refs_5_ = f32[12288,256]{1,0:T(8,128)} custom-call(s32[1]{0:T(128)} %bitcast.flag.leading, f32[1]{0:T(128)} %bitcast.17.total_weight, f32[12288,256]{1,0:T(8,128)} %rhs.9, f32[128,256]{1,0:T(8,128)} %get-tuple-element.38.top, bf16[1536,256]{1,0:T(8,128)(2,1)} %pad_maximum_fusion.1.weights, ...), custom_call_target="tpu_custom_call" | custom-call | flops 1 | bytes 1 | tf_op jit(solution)/shard_map/terms/pallas_call | solution.py:156
  216.1 2.5 %collective-permute-done.15.refs_2_ = f32[1536,128]{1,0:T(8,128)S(1)} collective-permute-done((f32[1536,128]{1,0:T(8,128)}, f32[1536,128]{1,0:T(8,128)S(1)}, u32[]{:S(2)}, u32[]{:S(2)}) %collective-permute-start.15) | collective-permute-done | bytes 786464 | tf_op jit(solution)/shard_map/ppermute | solution.py:40
  218.6 0.6 broadcast_in_dim.54.refs_0_
  219.6 1.0 pad_maximum_fusion.weights
  220.6 5.9 %forwarded_terms.2.refs_5_ = f32[12288,256]{1,0:T(8,128)} custom-call(s32[1]{0:T(128)} %bitcast.24.leading, f32[1]{0:T(128)} %bitcast.17.total_weight, f32[12288,256]{1,0:T(8,128)} %rhs.9, f32[128,256]{1,0:T(8,128)} %get-tuple-element.38.top, bf16[1920,256]{1,0:T(8,128)(2,1)} %pad_maximum_fusion.weights, ...), custom_call_target="tpu_custom_call", output_to_operand_aliasing={{}: (10, {})} | custom-call | flops 1 | bytes 1 | tf_op jit(solution)/shard_map/forwarded_terms/pallas_call | solution.py:191
  226.5 0.9 copy-done.3
  227.4 5.9 %forwarded_terms.3.refs_4_ = f32[12288,256]{1,0:T(8,128)} custom-call(s32[1]{0:T(128)} %bitcast.22.leading, f32[1]{0:T(128)} %bitcast.17.total_weight, f32[12288,256]{1,0:T(8,128)} %rhs.9, f32[128,256]{1,0:T(8,128)} %get-tuple-element.38.top, bf16[1920,256]{1,0:T(8,128)(2,1)} %pad_maximum_fusion.weights, ...), custom_call_target="tpu_custom_call", output_to_operand_aliasing={{}: (10, {})} | custom-call | flops 1 | bytes 1 | tf_op jit(solution)/shard_map/forwarded_terms/pallas_call | solution.py:191
  233.3 3.9 %terms.3 = f32[12288,256]{1,0:T(8,128)} custom-call(s32[1]{0:T(128)} %bitcast.flag.leading, f32[1]{0:T(128)} %bitcast.17.total_weight, f32[12288,256]{1,0:T(8,128)} %rhs.9, f32[128,256]{1,0:T(8,128)} %get-tuple-element.38.top, bf16[1536,256]{1,0:T(8,128)(2,1)} %pad_maximum_fusion.1.weights, ...), custom_call_target="tpu_custom_call", output_to_operand_aliasing={{}: (9, {})} | custom-call | flops 1 | bytes 1 | tf_op jit(solution)/shard_map/terms/pallas_call | solution.py:156
  (51 shorter events, 1.6 us)
Async XLA Ops:
  7.2 192.5 %all-gather.7.cloned.1.call-start = ((), (), s32[]{:S(2)}) async-start(), calls=%async_computation.1 | async-start | bytes 18874368 | tf_op jit(solution)/shard_map/all_gather | solution.py:230
  10.9 222.4 %all-gather.5.cloned.1.call-start = ((), (), s32[]{:S(2)}) async-start(), calls=%async_computation | async-start | bytes 2359296 | tf_op jit(solution)/shard_map/all_gather | solution.py:237
  12.4 10.1 %collective-permute-start = (f32[136,128]{1,0:T(8,128)S(1)}, f32[136,128]{1,0:T(8,128)S(1)}, u32[]{:S(2)}, u32[]{:S(2)}) collective-permute-start(f32[136,128]{1,0:T(8,128)S(1)} %concatenate.25), channel_id=1, source_target_pairs={{0,8},{8,16},{16,24},{1,9},{9,17},{17,25},{2,10},{10,18},{18,26},{... | collective-permute-start | bytes 208904 | tf_op jit(solution)/shard_map/ppermute | solution.py:41
  17.4 6.2 %collective-permute-start.2 = (f32[136,128]{1,0:T(8,128)S(1)}, f32[136,128]{1,0:T(8,128)S(1)}, u32[]{:S(2)}, u32[]{:S(2)}) collective-permute-start(f32[136,128]{1,0:T(8,128)S(1)} %concatenate.25), channel_id=1, source_target_pairs={{8,0},{16,8},{24,16},{9,1},{17,9},{25,17},{10,2},{18,10},{26,18},{... | collective-permute-start | bytes 208904 | tf_op jit(solution)/shard_map/ppermute | solution.py:41
  22.6 12.9 %collective-permute-start.1 = (f32[136,128]{1,0:T(8,128)S(1)}, f32[136,128]{1,0:T(8,128)S(1)}, u32[]{:S(2)}, u32[]{:S(2)}) collective-permute-start(f32[136,128]{1,0:T(8,128)S(1)} %collective-permute-done), channel_id=1, source_target_pairs={{8,16},{16,24},{9,17},{17,25},{10,18},{18,26},{11,19},{19,27},{12,... | collective-permute-start | bytes 208904 | tf_op jit(solution)/shard_map/ppermute | solution.py:41
  23.6 12.1 %collective-permute-start.3 = (f32[136,128]{1,0:T(8,128)S(1)}, f32[136,128]{1,0:T(8,128)S(1)}, u32[]{:S(2)}, u32[]{:S(2)}) collective-permute-start(f32[136,128]{1,0:T(8,128)S(1)} %collective-permute-done.2), channel_id=1, source_target_pairs={{8,0},{16,8},{9,1},{17,9},{10,2},{18,10},{11,3},{19,11},{12,4},{20... | collective-permute-start | bytes 208904 | tf_op jit(solution)/shard_map/ppermute | solution.py:41
  35.7 16.2 %collective-permute-start.4 = (f32[136,128]{1,0:T(8,128)S(1)}, f32[136,128]{1,0:T(8,128)S(1)}, u32[]{:S(2)}, u32[]{:S(2)}) collective-permute-start(f32[136,128]{1,0:T(8,128)S(1)} %broadcast_select_fusion.1), channel_id=1, source_target_pairs={{16,24},{8,0},{17,25},{9,1},{18,26},{10,2},{19,27},{11,3},{20,28},... | collective-permute-start | bytes 208904 | tf_op jit(solution)/shard_map/ppermute | solution.py:40
  51.9 8.4 %copy-start.5 = (f32[136,128]{1,0:T(8,128)}, f32[136,128]{1,0:T(8,128)S(1)}, u32[]{:S(2)}) copy-start(f32[136,128]{1,0:T(8,128)S(1)} %collective-permute-done.4.refs_1_) | copy-start | bytes 208900
  52.0 14.6 %collective-permute-start.5 = (f32[128,128]{1,0:T(8,128)S(1)}, f32[128,128]{1,0:T(8,128)S(1)}, u32[]{:S(2)}, u32[]{:S(2)}) collective-permute-start(f32[128,128]{1,0:T(8,128)S(1)} %slice.100), channel_id=1, source_target_pairs={{0,6},{1,7},{8,14},{9,15},{16,22},{17,23},{24,30},{25,31}} | collective-permute-start | bytes 196616 | tf_op jit(solution)/shard_map/ppermute | solution.py:266
  55.4 11.2 %collective-permute-start.6 = (f32[128,128]{1,0:T(8,128)S(1)}, f32[128,128]{1,0:T(8,128)S(1)}, u32[]{:S(2)}, u32[]{:S(2)}) collective-permute-start(f32[128,128]{1,0:T(8,128)S(1)} %slice.101), channel_id=1, source_target_pairs={{0,4},{1,5},{8,12},{9,13},{16,20},{17,21},{24,28},{25,29}} | collective-permute-start | bytes 196616 | tf_op jit(solution)/shard_map/ppermute | solution.py:266
  56.7 9.9 %collective-permute-start.7 = (f32[128,128]{1,0:T(8,128)S(1)}, f32[128,128]{1,0:T(8,128)S(1)}, u32[]{:S(2)}, u32[]{:S(2)}) collective-permute-start(f32[128,128]{1,0:T(8,128)S(1)} %slice.102), channel_id=1, source_target_pairs={{0,2},{1,3},{8,10},{9,11},{16,18},{17,19},{24,26},{25,27}} | collective-permute-start | bytes 196616 | tf_op jit(solution)/shard_map/ppermute | solution.py:266
  62.0 60.7 %collective-permute-start.8 = (f32[1536,128]{1,0:T(8,128)}, f32[1536,128]{1,0:T(8,128)S(1)}, u32[]{:S(2)}, u32[]{:S(2)}) collective-permute-start(f32[1536,128]{1,0:T(8,128)} %get-tuple-element.13), channel_id=1, source_target_pairs={{0,8},{8,16},{16,24},{1,9},{9,17},{17,25},{2,10},{10,18},{18,26},{... | collective-permute-start | bytes 2359304 | tf_op jit(solution)/shard_map/ppermute | solution.py:41
  63.3 60.1 %collective-permute-start.10 = (f32[1536,128]{1,0:T(8,128)}, f32[1536,128]{1,0:T(8,128)S(1)}, u32[]{:S(2)}, u32[]{:S(2)}) collective-permute-start(f32[1536,128]{1,0:T(8,128)} %get-tuple-element.13), channel_id=1, source_target_pairs={{8,0},{16,8},{24,16},{9,1},{17,9},{25,17},{10,2},{18,10},{26,18},{... | collective-permute-start | bytes 2359304 | tf_op jit(solution)/shard_map/ppermute | solution.py:41
  122.7 61.8 %copy-start.1 = (f32[1536,128]{1,0:T(8,128)}, f32[1536,128]{1,0:T(8,128)S(1)}, u32[]{:S(2)}) copy-start(f32[1536,128]{1,0:T(8,128)S(1)} %collective-permute-done.8.refs_1_) | copy-start | bytes 2359300
  122.7 4.9 %collective-permute-start.12 = (f32[1536,128]{1,0:T(8,128)S(1)}, f32[1536,128]{1,0:T(8,128)S(1)}, u32[]{:S(2)}, u32[]{:S(2)}) collective-permute-start(f32[1536,128]{1,0:T(8,128)S(1)} %collective-permute-done.8.refs_1_), channel_id=1, source_target_pairs={{8,16},{16,24},{9,17},{17,25},{10,18},{18,26},{11,19},{19,27},{12,... | collective-permute-start | bytes 2359304 | tf_op jit(solution)/shard_map/ppermute | solution.py:41
  123.5 61.1 %copy-start.2 = (f32[1536,128]{1,0:T(8,128)}, f32[1536,128]{1,0:T(8,128)S(1)}, u32[]{:S(2)}) copy-start(f32[1536,128]{1,0:T(8,128)S(1)} %collective-permute-done.10.refs_2_) | copy-start | bytes 2359300
  123.5 53.3 %collective-permute-start.13 = (f32[1536,128]{1,0:T(8,128)S(1)}, f32[1536,128]{1,0:T(8,128)S(1)}, u32[]{:S(2)}, u32[]{:S(2)}) collective-permute-start(f32[1536,128]{1,0:T(8,128)S(1)} %collective-permute-done.10.refs_2_), channel_id=1, source_target_pairs={{8,0},{16,8},{9,1},{17,9},{10,2},{18,10},{11,3},{19,11},{12,4},{20... | collective-permute-start | bytes 2359304 | tf_op jit(solution)/shard_map/ppermute | solution.py:41
  127.6 1.0 copy-start.4
  178.3 40.3 %collective-permute-start.15 = (f32[1536,128]{1,0:T(8,128)}, f32[1536,128]{1,0:T(8,128)S(1)}, u32[]{:S(2)}, u32[]{:S(2)}) collective-permute-start(f32[1536,128]{1,0:T(8,128)} %get-tuple-element.14.refs_3_), channel_id=1, source_target_pairs={{16,24},{8,0},{17,25},{9,1},{18,26},{10,2},{19,27},{11,3},{20,28},... | collective-permute-start | bytes 2359304 | tf_op jit(solution)/shard_map/ppermute | solution.py:40
  184.5 41.9 %collective-permute-start.11 = (f32[1536,128]{1,0:T(8,128)S(1)}, f32[1536,128]{1,0:T(8,128)}, u32[]{:S(2)}, u32[]{:S(2)}) collective-permute-start(f32[1536,128]{1,0:T(8,128)S(1)} %collective-permute-done.10.refs_2_), channel_id=1, source_target_pairs={{0,1},{1,0},{2,3},{3,2},{4,5},{5,4},{6,7},{7,6},{8,9},{9,8},{10,11... | collective-permute-start | bytes 2359304 | tf_op jit(solution)/shard_map/ppermute | solution.py:309
  184.6 41.9 %collective-permute-start.9 = (f32[1536,128]{1,0:T(8,128)S(1)}, f32[1536,128]{1,0:T(8,128)}, u32[]{:S(2)}, u32[]{:S(2)}) collective-permute-start(f32[1536,128]{1,0:T(8,128)S(1)} %collective-permute-done.8.refs_1_), channel_id=1, source_target_pairs={{0,1},{1,0},{2,3},{3,2},{4,5},{5,4},{6,7},{7,6},{8,9},{9,8},{10,11... | collective-permute-start | bytes 2359304 | tf_op jit(solution)/shard_map/ppermute | solution.py:309
  185.1 41.4 %collective-permute-start.14 = (f32[1536,128]{1,0:T(8,128)}, f32[1536,128]{1,0:T(8,128)}, u32[]{:S(2)}, u32[]{:S(2)}) collective-permute-start(f32[1536,128]{1,0:T(8,128)} %get-tuple-element.14.refs_3_), channel_id=1, source_target_pairs={{0,1},{1,0},{2,3},{3,2},{4,5},{5,4},{6,7},{7,6},{8,9},{9,8},{10,11... | collective-permute-start | bytes 2359304 | tf_op jit(solution)/shard_map/ppermute | solution.py:309
  218.6 0.9 copy-start
  219.5 7.0 %collective-permute-start.16 = (f32[1536,128]{1,0:T(8,128)}, f32[1536,128]{1,0:T(8,128)S(1)}, u32[]{:S(2)}, u32[]{:S(2)}) collective-permute-start(f32[1536,128]{1,0:T(8,128)} %get-tuple-element.16.refs_4_), channel_id=1, source_target_pairs={{0,1},{1,0},{2,3},{3,2},{4,5},{5,4},{6,7},{7,6},{8,9},{9,8},{10,11... | collective-permute-start | bytes 2359304 | tf_op jit(solution)/shard_map/ppermute | solution.py:309
  226.5 0.9 copy-start.3
Sparse Core Ops, SparseCore 0:
  11.0 188.6 all-gather.6
  201.3 31.7 all-gather.4
